TPU v7x, 32 devices: a whole 2x2x4 slice. The times are simulated.
32 devices in a mesh: fsdp: 8 (over z, x), dp: 4 (over y, core).
Axes of the slice: x: 2, y: 2, z: 4, core: 2. Of those that a mesh axis runs over, the one named last changes fastest.
Arguments:
- tokens: bfloat16 [192, 197, 768], P(('fsdp', 'dp')), may hold values from -6 to 6
- w_qkv: bfloat16 [768, 2304], P(('fsdp', 'dp')), may hold values from -0.21875 to 0.21875
- w_out: bfloat16 [768, 768], P(('fsdp', 'dp')), may hold values from -1.25 to 1.25
- w_up: bfloat16 [768, 3072], P(('fsdp', 'dp')), may hold values from -0.21875 to 0.21875
- w_down: bfloat16 [3072, 768], P(('fsdp', 'dp')), may hold values from -0.109375 to 0.109375
- norm1_scale: bfloat16 [768], P(('fsdp', 'dp')), may hold values from 0.25 to 1.75
- norm1_offset: bfloat16 [768], P(('fsdp', 'dp')), may hold values from -4 to 4
- qv_bias: bfloat16 [1536], P(('fsdp', 'dp')), may hold values from -6 to 6
- out_bias: bfloat16 [768], P(('fsdp', 'dp')), may hold values from -4 to 4
- norm2_scale: bfloat16 [768], P(('fsdp', 'dp')), may hold values from 0.25 to 1.75
- norm2_offset: bfloat16 [768], P(('fsdp', 'dp')), may hold values from -4 to 4
- up_bias: bfloat16 [3072], P(('fsdp', 'dp')), may hold values from -6 to 6
- down_bias: bfloat16 [768], P(('fsdp', 'dp')), may hold values from -4 to 4
- cotangent: bfloat16 [192, 197, 768], P(('fsdp', 'dp')), may hold values from -6 to 6
- counts: int32 [32], P(('fsdp', 'dp')), may hold values from 1 to 6, 128 in all
Outputs:
- out_tokens: bfloat16 [192, 197, 768], P(('fsdp', 'dp'))
- grad_tokens: float32 [192, 197, 768], P(('fsdp', 'dp'))
- grad_w_qkv: float32 [768, 2304], P(('fsdp', 'dp'))
- grad_w_out: float32 [768, 768], P(('fsdp', 'dp'))
- grad_w_up: float32 [768, 3072], P(('fsdp', 'dp'))
- grad_w_down: float32 [3072, 768], P(('fsdp', 'dp'))
- grad_norm1_scale: float32 [768], P(('fsdp', 'dp'))
- grad_norm1_offset: float32 [768], P(('fsdp', 'dp'))
- grad_qv_bias: float32 [1536], P(('fsdp', 'dp'))
- grad_out_bias: float32 [768], P(('fsdp', 'dp'))
- grad_norm2_scale: float32 [768], P(('fsdp', 'dp'))
- grad_norm2_offset: float32 [768], P(('fsdp', 'dp'))
- grad_up_bias: float32 [3072], P(('fsdp', 'dp'))
- grad_down_bias: float32 [768], P(('fsdp', 'dp'))
Inputs may be any that keep to these rules, and one draw needn't show every extreme that they name: counts[i] is the number of images of the i-th device along fsdp+dp, which fill the first of its 6 slots; the entries sum to 128.
All inputs are finite; a program needn't handle non-finite values.
Results may differ from a plain program's by a relative error of at most 0.011.
Values may be sent and summed in bfloat16 or wider, within the bound.
No kernel may reach another device: no remote copies, remote signals or barrier semaphores. Data moves between devices by JAX's collectives and lax.ppermute only.
A program may use at most 192 MiB of HBM per device.

v0:
```python
import jax
import jax.numpy as jnp
from jax import lax
from jax.sharding import PartitionSpec as P

HEADS = 12


EPSILON = 1e-06


def norm_scaled(values, scale_vec):
    center = values - jnp.mean(values, axis=-1, keepdims=True)
    spread = jnp.mean(center * center, axis=-1, keepdims=True)
    return center * lax.rsqrt(spread + EPSILON) * scale_vec


def exact_gelu(values):
    return jax.nn.gelu(values, approximate=False)


def column_total(values):
    return jnp.sum(values.astype(jnp.float32), axis=0)


def per_device(
    tokens,
    w_qkv,
    w_out,
    w_up,
    w_down,
    norm1_scale,
    norm1_offset,
    qv_bias,
    out_bias,
    norm2_scale,
    norm2_offset,
    up_bias,
    down_bias,
    cotangent,
    counts,
):
    gathered = (
        lax.all_gather(w_qkv, ("fsdp", "dp"), axis=0, tiled=True),
        lax.all_gather(w_out, ("fsdp", "dp"), axis=0, tiled=True),
        lax.all_gather(w_up, ("fsdp", "dp"), axis=0, tiled=True),
        lax.all_gather(w_down, ("fsdp", "dp"), axis=0, tiled=True),
        lax.all_gather(norm1_scale, ("fsdp", "dp"), axis=0, tiled=True),
        lax.all_gather(norm1_offset, ("fsdp", "dp"), axis=0, tiled=True),
        lax.all_gather(qv_bias, ("fsdp", "dp"), axis=0, tiled=True),
        lax.all_gather(out_bias, ("fsdp", "dp"), axis=0, tiled=True),
        lax.all_gather(norm2_scale, ("fsdp", "dp"), axis=0, tiled=True),
        lax.all_gather(norm2_offset, ("fsdp", "dp"), axis=0, tiled=True),
        lax.all_gather(up_bias, ("fsdp", "dp"), axis=0, tiled=True),
        lax.all_gather(down_bias, ("fsdp", "dp"), axis=0, tiled=True),
    )
    full_qkv = gathered[0]
    full_out = gathered[1]
    full_up = gathered[2]
    full_down = gathered[3]
    scale_one = gathered[4].astype(jnp.float32)
    offset_one = gathered[5].astype(jnp.float32)
    qv_full = gathered[6].astype(jnp.float32)
    out_shift = gathered[7].astype(jnp.float32)
    scale_two = gathered[8].astype(jnp.float32)
    offset_two = gathered[9].astype(jnp.float32)
    up_shift = gathered[10].astype(jnp.float32)
    down_shift = gathered[11].astype(jnp.float32)
    per_holder, seq_len, model_width = tokens.shape
    row_count = per_holder * seq_len
    head_size = model_width // HEADS
    split_shape = (per_holder, seq_len, HEADS, head_size)
    scale_factor = head_size ** (-0.5)
    live_slots = (jnp.arange(per_holder) < counts[0]).astype(jnp.float32)
    live_rows = jnp.repeat(live_slots, seq_len, total_repeat_length=row_count)[:, None]
    inputs = tokens.reshape(row_count, model_width).astype(jnp.float32)
    normed = (norm_scaled(inputs, scale_one) + offset_one).astype(jnp.bfloat16)
    bias_full = jnp.concatenate(
        [qv_full[:model_width], jnp.zeros((model_width,), jnp.float32), qv_full[model_width:]]
    )
    projected = (jnp.dot(normed, full_qkv, preferred_element_type=jnp.float32) + bias_full).astype(
        jnp.bfloat16
    )
    queries = projected[:, :model_width].reshape(split_shape)
    key_rows = projected[:, model_width : 2 * model_width].reshape(split_shape)
    value_rows = projected[:, 2 * model_width :].reshape(split_shape)
    raw_scores = (
        jnp.einsum("bqhd,bkhd->bhqk", queries, key_rows, preferred_element_type=jnp.float32)
        * scale_factor
    )
    top_score = jnp.max(raw_scores, axis=-1, keepdims=True)
    expo_scores = jnp.exp(raw_scores - top_score)
    total_score = jnp.sum(expo_scores, axis=-1, keepdims=True)
    log_total = top_score + jnp.log(total_score)
    probs_low = (expo_scores / total_score).astype(jnp.bfloat16)
    head_out = jnp.einsum(
        "bhqk,bkhd->bqhd", probs_low, value_rows, preferred_element_type=jnp.float32
    )
    head_out = head_out.reshape(row_count, model_width).astype(jnp.bfloat16)
    middle = inputs + jnp.dot(head_out, full_out, preferred_element_type=jnp.float32) + out_shift
    normed_two = (norm_scaled(middle, scale_two) + offset_two).astype(jnp.bfloat16)
    hidden = jnp.dot(normed_two, full_up, preferred_element_type=jnp.float32) + up_shift
    active = exact_gelu(hidden).astype(jnp.bfloat16)
    result = (
        middle + jnp.dot(active, full_down, preferred_element_type=jnp.float32) + down_shift
    ) * live_rows
    out_tokens = result.astype(jnp.bfloat16).reshape(tokens.shape)
    late_params = (
        lax.all_gather(w_qkv, ("fsdp", "dp"), axis=0, tiled=True),
        lax.all_gather(w_out, ("fsdp", "dp"), axis=0, tiled=True),
        lax.all_gather(w_up, ("fsdp", "dp"), axis=0, tiled=True),
        lax.all_gather(w_down, ("fsdp", "dp"), axis=0, tiled=True),
        lax.all_gather(norm1_scale, ("fsdp", "dp"), axis=0, tiled=True),
        lax.all_gather(norm2_scale, ("fsdp", "dp"), axis=0, tiled=True),
    )
    late_qkv = late_params[0]
    late_out = late_params[1]
    late_up = late_params[2]
    late_down = late_params[3]
    late_scale_one = late_params[4].astype(jnp.float32)
    late_scale_two = late_params[5].astype(jnp.float32)
    seed_rows = cotangent.reshape(row_count, model_width).astype(jnp.float32) * live_rows
    seed_low = seed_rows.astype(jnp.bfloat16)
    grad_down = jnp.einsum("rf,rd->fd", active, seed_low, preferred_element_type=jnp.float32)
    grad_down_bias = column_total(seed_low)
    back_active = jnp.einsum("rd,fd->rf", seed_low, late_down, preferred_element_type=jnp.float32)
    gelu_pull = jax.vjp(exact_gelu, hidden)[1]
    back_hidden = gelu_pull(back_active)[0].astype(jnp.bfloat16)
    grad_up = jnp.einsum("rd,rf->df", normed_two, back_hidden, preferred_element_type=jnp.float32)
    grad_up_bias = column_total(back_hidden)
    back_normed_two = jnp.einsum(
        "rf,df->rd", back_hidden, late_up, preferred_element_type=jnp.float32
    )
    norm_two_pull = jax.vjp(norm_scaled, middle, late_scale_two)[1]
    middle_part, grad_scale_two = norm_two_pull(back_normed_two)
    grad_offset_two = jnp.sum(back_normed_two, axis=0)
    back_middle = seed_rows + middle_part
    back_branch = back_middle.astype(jnp.bfloat16)
    grad_out = jnp.einsum("rd,re->de", head_out, back_branch, preferred_element_type=jnp.float32)
    grad_out_bias = column_total(back_branch)
    back_head = jnp.einsum("re,de->rd", back_branch, late_out, preferred_element_type=jnp.float32)
    back_head = back_head.astype(jnp.bfloat16).reshape(split_shape)
    again_scores = (
        jnp.einsum("bqhd,bkhd->bhqk", queries, key_rows, preferred_element_type=jnp.float32)
        * scale_factor
    )
    probs_full = jnp.exp(again_scores - log_total)
    probs_again = probs_full.astype(jnp.bfloat16)
    back_probs = jnp.einsum(
        "bqhd,bkhd->bhqk", back_head, value_rows, preferred_element_type=jnp.float32
    )
    back_values = jnp.einsum(
        "bhqk,bqhd->bkhd", probs_again, back_head, preferred_element_type=jnp.float32
    )
    row_dot = jnp.sum(probs_full * back_probs, axis=-1, keepdims=True)
    back_scaled = (probs_full * (back_probs - row_dot) * scale_factor).astype(jnp.bfloat16)
    back_queries = jnp.einsum(
        "bhqk,bkhd->bqhd", back_scaled, key_rows, preferred_element_type=jnp.float32
    )
    back_keys = jnp.einsum(
        "bhqk,bqhd->bkhd", back_scaled, queries, preferred_element_type=jnp.float32
    )
    back_projected = jnp.concatenate(
        [
            back_queries.reshape(row_count, model_width),
            back_keys.reshape(row_count, model_width),
            back_values.reshape(row_count, model_width),
        ],
        axis=1,
    ).astype(jnp.bfloat16)
    grad_qkv = jnp.einsum("rd,re->de", normed, back_projected, preferred_element_type=jnp.float32)
    column_sums = column_total(back_projected)
    grad_qv = jnp.concatenate([column_sums[:model_width], column_sums[2 * model_width :]])
    back_normed = jnp.einsum(
        "re,de->rd", back_projected, late_qkv, preferred_element_type=jnp.float32
    )
    norm_one_pull = jax.vjp(norm_scaled, inputs, late_scale_one)[1]
    input_part, grad_scale_one = norm_one_pull(back_normed)
    grad_offset_one = jnp.sum(back_normed, axis=0)
    grad_inputs = (back_middle + input_part).reshape(tokens.shape)
    shares = (
        lax.psum_scatter(grad_qkv, ("fsdp", "dp"), scatter_dimension=0, tiled=True),
        lax.psum_scatter(grad_out, ("fsdp", "dp"), scatter_dimension=0, tiled=True),
        lax.psum_scatter(grad_up, ("fsdp", "dp"), scatter_dimension=0, tiled=True),
        lax.psum_scatter(grad_down, ("fsdp", "dp"), scatter_dimension=0, tiled=True),
        lax.psum_scatter(grad_scale_one, ("fsdp", "dp"), scatter_dimension=0, tiled=True),
        lax.psum_scatter(grad_offset_one, ("fsdp", "dp"), scatter_dimension=0, tiled=True),
        lax.psum_scatter(grad_qv, ("fsdp", "dp"), scatter_dimension=0, tiled=True),
        lax.psum_scatter(grad_out_bias, ("fsdp", "dp"), scatter_dimension=0, tiled=True),
        lax.psum_scatter(grad_scale_two, ("fsdp", "dp"), scatter_dimension=0, tiled=True),
        lax.psum_scatter(grad_offset_two, ("fsdp", "dp"), scatter_dimension=0, tiled=True),
        lax.psum_scatter(grad_up_bias, ("fsdp", "dp"), scatter_dimension=0, tiled=True),
        lax.psum_scatter(grad_down_bias, ("fsdp", "dp"), scatter_dimension=0, tiled=True),
    )
    return (
        out_tokens,
        grad_inputs,
        shares[0],
        shares[1],
        shares[2],
        shares[3],
        shares[4],
        shares[5],
        shares[6],
        shares[7],
        shares[8],
        shares[9],
        shares[10],
        shares[11],
    )


def solution(mesh):
    return jax.shard_map(
        per_device,
        mesh=mesh,
        in_specs=(
            P(("fsdp", "dp"), None, None),
            P(("fsdp", "dp"), None),
            P(("fsdp", "dp"), None),
            P(("fsdp", "dp"), None),
            P(("fsdp", "dp"), None),
            P(("fsdp", "dp")),
            P(("fsdp", "dp")),
            P(("fsdp", "dp")),
            P(("fsdp", "dp")),
            P(("fsdp", "dp")),
            P(("fsdp", "dp")),
            P(("fsdp", "dp")),
            P(("fsdp", "dp")),
            P(("fsdp", "dp"), None, None),
            P(("fsdp", "dp")),
        ),
        out_specs=(
            P(("fsdp", "dp"), None, None),
            P(("fsdp", "dp"), None, None),
            P(("fsdp", "dp"), None),
            P(("fsdp", "dp"), None),
            P(("fsdp", "dp"), None),
            P(("fsdp", "dp"), None),
            P(("fsdp", "dp")),
            P(("fsdp", "dp")),
            P(("fsdp", "dp")),
            P(("fsdp", "dp")),
            P(("fsdp", "dp")),
            P(("fsdp", "dp")),
            P(("fsdp", "dp")),
            P(("fsdp", "dp")),
        ),
        check_vma=False,
    )
```

profile of v0, /device:TPU:0, one launch (start us, length us, event | category | flops | bytes accessed | tf_op | source)
XLA Modules:
  0.0 826.2 jit_solution(1980006920451821563)
XLA Ops:
  19.8 43.3 %all-reduce.17 = (bf16[1536]{0:T(1024)(128)(2,1)S(1)}, bf16[768]{0:T(1024)(128)(2,1)S(1)}, bf16[768]{0:T(1024)(128)(2,1)S(1)}, bf16[768]{0:T(1024)(128)(2,1)S(1)...) all-reduce(bf16[1536]{0:T(1024)(128)(2,1)S(1)} %dynamic-update-slic, ...), channel_id=1, replica_groups=mesh['fsdp'=8,'dp'=4] {'fsdp','dp'}, use_global_device_ids=true, to_apply=%add.2 | all-reduce | flops 9216 | bytes 36864
  74.2 7.8 fusion.11
  84.3 6.5 reshape.261
  90.8 6.7 copy.65
  97.5 6.5 reshape.260
  104.0 6.7 copy.64
  110.7 4.9 reshape.259
  115.7 5.9 copy.66
  121.6 10.6 %multiply_reduce_fusion.1 = (f32[6,12,197]{2,1,0:T(8,128)S(1)}, f32[6,12,197,197]{2,3,1,0:T(8,128)}) fusion(bf16[6,197,12,64]{1,3,2,0:T(8,128)(2,1)} %copy.64, bf16[6,197,12,64]{1,3,2,0:T(8,128)(2,1)} %copy.65), kind=kOutput, calls=%fused_computation.28 | convolution fusion | flops 363238048 | bytes 14864832 | tf_op jit(solution)/shard_map/bqhd,bkhd->bhqk/dot_general | solution.py:88
  132.3 8.8 %fusion.10 = f32[6,12,197]{2,1,0:T(8,128)S(1)} fusion(f32[6,12,197,197]{2,3,1,0:T(8,128)} %get-tuple-element.70, f32[6,12,197]{2,1,0:T(8,128)S(1)} %get-tuple-element.69), kind=kLoop, calls=%fused_computation.27 | loop fusion | flops 8368560 | bytes 11290464 | tf_op jit(solution)/shard_map/reduce_sum | solution.py:93
  141.7 8.6 %convert_bitcast_fusion.3 = bf16[6,197,12,64]{1,3,2,0:T(8,128)(2,1)S(1)} fusion(bf16[6,197,12,64]{1,3,2,0:T(8,128)(2,1)S(1)} %copy.66, f32[6,12,197,197]{2,3,1,0:T(8,128)} %get-tuple-element.70, f32[6,12,197]{2,1,0:T(8,128)S(1)} %fusion.10, f32[6,12,197]{2,1,0:T(8,128)S(1)} %get-tuple-element.69), kind=kOutput, calls=%fused_computation.67 | convolution fusion | flops 369748512 | bytes 14921568 | tf_op jit(solution)/shard_map/bhqk,bkhd->bqhd/dot_general | solution.py:96
  156.1 5.0 fusion.61
  164.1 31.4 %all-gather.9.cloned.1.call-done = bf16[768,3072]{1,0:T(8,128)(2,1)} async-done(((bf16[24,3072]{1,0:T(8,128)(2,1)}), bf16[768,3072]{1,0:T(8,128)(2,1)}) %all-gather.9.cloned.1.call-update) | async-done | bytes 4718608 | tf_op jit(solution)/shard_map/all_gather | solution.py:46
  195.5 42.6 %multiply_convert_fusion.1 = (bf16[1182,3072]{1,0:T(8,128)(2,1)}, f32[1182,3072]{1,0:T(8,128)}, f32[1182,3072]{1,0:T(8,128)}) fusion(f32[3072]{0:T(1024)S(1)} %convert_element_type.126, bf16[768,3072]{1,0:T(8,128)(2,1)} %all-gather.9.cloned.1.call-done, f32[1182,768]{1,0:T(8,128)} %copy-done.3, f32[768]{0:T(1024)S(1)} %convert_element_type.124, ...), kind=kOutput, calls=%fused_computation.11 | convolution fusion | flops 5821567488 | bytes 44688624 | tf_op jit(solution)/shard_map/dot_general | solution.py:102
  238.1 22.5 %all-gather.11.cloned.1.call-done = bf16[3072,768]{1,0:T(8,128)(2,1)} async-done(((bf16[96,768]{1,0:T(8,128)(2,1)}), bf16[3072,768]{1,0:T(8,128)(2,1)}) %all-gather.11.cloned.1.call-update) | async-done | bytes 4718608 | tf_op jit(solution)/shard_map/all_gather | solution.py:47
  260.7 20.9 %convert_reduce_fusion = (f32[3072]{0:T(1024)S(1)}, bf16[1182,3072]{1,0:T(8,128)(2,1)}) fusion(f32[1182,3072]{1,0:T(8,128)} %get-tuple-element.55, f32[1182,3072]{1,0:T(8,128)} %get-tuple-element.73, bf16[3072,768]{1,0:T(8,128)(2,1)} %all-gather.11.cloned.1.call-done, f32[1182,768]{1,0:T(8,128)} %reshape.229, f32[1182]{0:T(1024)S(1)} %copy-done.18), kind=kOutput, calls=%fused_computation.9 | convolution fusion | flops 5637285888 | bytes 44677752 | tf_op jit(solution)/shard_map/rd,fd->rf/dot_general | solution.py:126
  281.5 12.5 %multiply_reduce_fusion.3 = (f32[768]{0:T(1024)S(1)}, f32[1182]{0:T(1024)S(1)}, f32[768]{0:T(1024)S(1)}, f32[1182,768]{1,0:T(8,128)S(1)}) fusion(f32[1182,768]{1,0:T(8,128)} %copy-done.3, f32[1182]{0:T(1024)S(1)} %fusion.39, f32[1182]{0:T(1024)S(1)} %broadcast_multiply_fusion, f32[768]{0:T(1024)S(1)} %convert_element_type.123, ...), kind=kOutput, calls=%fused_computation.51 | convolution fusion | flops 5584634880 | bytes 19266408 | tf_op jit(solution)/shard_map/rf,df->rd/dot_general | solution.py:131
  305.4 5.0 reshape.262
  310.4 6.0 copy.70
  316.4 8.3 %convert_bitcast_fusion = bf16[6,197,12,64]{1,3,2,0:T(8,128)(2,1)S(1)} fusion(bf16[6,197,12,64]{1,3,2,0:T(8,128)(2,1)S(1)} %copy.70, f32[6,12,197,197]{2,3,1,0:T(8,128)} %get-tuple-element.70, f32[6,12,197]{2,1,0:T(8,128)S(1)} %copy-done.15), kind=kOutput, calls=%fused_computation.64 | convolution fusion | flops 366954272 | bytes 14864832 | tf_op jit(solution)/shard_map/bhqk,bqhd->bkhd/dot_general | solution.py:152
  324.8 7.3 fusion.62
  337.4 25.9 %convert_bitcast_fusion.1 = bf16[6,197,12,64]{1,3,2,0:T(8,128)(2,1)} fusion(bf16[6,197,12,64]{1,3,2,0:T(8,128)(2,1)} %copy.64, f32[6,12,197,197]{2,3,1,0:T(8,128)} %fusion.62, f32[6,12,197,197]{2,3,1,0:T(8,128)} %get-tuple-element.70, f32[6,12,197]{2,1,0:T(8,128)S(1)} %copy-done.15), kind=kOutput, calls=%fused_computation.65 | convolution fusion | flops 383734144 | bytes 26041824 | tf_op jit(solution)/shard_map/bhqk,bqhd->bkhd/dot_general | solution.py:160
  370.4 25.9 %convert_bitcast_fusion.2 = bf16[6,197,12,64]{1,3,2,0:T(8,128)(2,1)} fusion(bf16[6,197,12,64]{1,3,2,0:T(8,128)(2,1)} %copy.65, f32[6,12,197,197]{2,3,1,0:T(8,128)} %fusion.62, f32[6,12,197,197]{2,3,1,0:T(8,128)} %get-tuple-element.70, f32[6,12,197]{2,1,0:T(8,128)S(1)} %copy-done.15), kind=kOutput, calls=%fused_computation.66 | convolution fusion | flops 383734144 | bytes 26041824 | tf_op jit(solution)/shard_map/bhqk,bkhd->bqhd/dot_general | solution.py:157
  408.7 7.7 fusion.52
  416.6 12.3 %fusion.51 = f32[3072,768]{1,0:T(8,128)} fusion(bf16[1182,3072]{1,0:T(8,128)(2,1)} %get-tuple-element.54, f32[1182,768]{1,0:T(8,128)} %reshape.229, f32[1182]{0:T(1024)S(1)} %copy-done.18), kind=kOutput, calls=%fused_computation.95 | convolution fusion | flops 5579191296 | bytes 20335224 | tf_op jit(solution)/shard_map/rf,rd->fd/dot_general | solution.py:124
  429.0 12.8 %fusion.53 = f32[768,3072]{1,0:T(8,128)} fusion(bf16[1182,3072]{1,0:T(8,128)(2,1)} %get-tuple-element.77, f32[1182,768]{1,0:T(8,128)} %copy-done.3, f32[768]{0:T(1024)S(1)} %convert_element_type.124, f32[768]{0:T(1024)S(1)} %convert_element_type.123, f32[1182]{0:T(1024)S(1)} %fusion.39, f32[1182]{0:T(1024)S(1)} %broadcast_multiply_fusion), kind=kOutput, calls=%fused_computation.97 | convolution fusion | flops 5581914624 | bytes 20346096 | tf_op jit(solution)/shard_map/rd,rf->df/dot_general | solution.py:129
  443.8 10.6 %fusion.32 = bf16[1182,768]{1,0:T(8,128)(2,1)S(1)} fusion(f32[1182,768]{1,0:T(8,128)} %copy-done.3, bf16[1182,3072]{1,0:T(8,128)(2,1)} %get-tuple-element.54, bf16[3072,768]{1,0:T(8,128)(2,1)} %all-gather.11.cloned.1.call-done, f32[1182]{0:T(1024)S(1)} %copy-done.18, f32[768]{0:T(1024)S(1)} %convert_element_type.128), kind=kOutput, calls=%fused_computation.63 | convolution fusion | flops 5581006848 | bytes 17435256 | tf_op jit(solution)/shard_map/dot_general | solution.py:105
  460.0 11.5 %multiply_reduce_fusion.4 = (f32[768]{0:T(1024)S(1)}, f32[1182]{0:T(1024)S(1)}, f32[768]{0:T(1024)S(1)}, f32[1182,768]{1,0:T(8,128)}) fusion(f32[1182,768]{1,0:T(8,128)S(1)} %copy-done.6, f32[1182]{0:T(1024)S(1)} %copy-done.24, f32[1182]{0:T(1024)S(1)} %copy-done.22, f32[768]{0:T(1024)S(1)} %copy-done.26, bf16[1182,2304]{0,1:T(8,128)(2,1)} %copy-done.10, ...), kind=kOutput, calls=%fused_computation.53 | convolution fusion | flops 4190291200 | bytes 16271208 | tf_op jit(solution)/shard_map/re,de->rd/dot_general | solution.py:174
  471.4 42.3 %all-reduce.16 = (f32[768]{0:T(1024)S(1)}, f32[768]{0:T(1024)S(1)}, f32[1536]{0:T(1024)S(1)}, f32[768]{0:T(1024)S(1)}, f32[768]{0:T(1024)S(1)}, /*index=5*/f32[7...) all-reduce(f32[768]{0:T(1024)S(1)} %get-tuple-element.28, ...), channel_id=6, replica_groups=mesh['fsdp'=8,'dp'=4] {'fsdp','dp'}, use_global_device_ids=true, to_apply=%region_16.17.clone | all-reduce | flops 9216 | bytes 73728
  529.2 6.6 reduce-scatter.5.cloned.1.call-done
  535.7 141.3 %reduce-scatter.11.cloned.1.call-done = f32[96,768]{1,0:T(8,128)} async-done(((f32[3072,768]{1,0:T(8,128)}), f32[96,768]{1,0:T(8,128)}) %reduce-scatter.11.cloned.1.call-update) | async-done | bytes 294928 | tf_op jit(solution)/shard_map/reduce_scatter | solution.py:185
  677.0 142.1 %reduce-scatter.9.cloned.1.call-done = f32[24,3072]{1,0:T(8,128)} async-done(((f32[768,3072]{1,0:T(8,128)}), f32[24,3072]{1,0:T(8,128)}) %reduce-scatter.9.cloned.1.call-update) | async-done | bytes 294928 | tf_op jit(solution)/shard_map/reduce_scatter | solution.py:184
  (186 shorter events, 93.5 us)
Async XLA Ops:
  7.2 67.0 %all-gather.5.cloned.1.call-start = ((), (), s32[]{:S(2)}) async-start(), calls=%async_computation.4 | async-start | bytes 3649536 | tf_op jit(solution)/shard_map/all_gather | solution.py:44
  7.9 148.2 %all-gather.7.cloned.1.call-start = ((), (), s32[]{:S(2)}) async-start(), calls=%async_computation.5 | async-start | bytes 1216512 | tf_op jit(solution)/shard_map/all_gather | solution.py:45
  8.7 186.8 %all-gather.9.cloned.1.call-start = ((), (), s32[]{:S(2)}) async-start(), calls=%async_computation.6 | async-start | bytes 4866048 | tf_op jit(solution)/shard_map/all_gather | solution.py:46
  9.4 8.4 %copy-start.36 = (bf16[24]{0:T(256)(128)(2,1)S(1)}, bf16[24]{0:T(256)(128)(2,1)}, u32[]{:S(2)}) copy-start(bf16[24]{0:T(256)(128)(2,1)} %param.26) | copy-start | bytes 148
  9.4 8.7 %copy-start.37 = (bf16[24]{0:T(256)(128)(2,1)S(1)}, bf16[24]{0:T(256)(128)(2,1)}, u32[]{:S(2)}) copy-start(bf16[24]{0:T(256)(128)(2,1)} %param.27) | copy-start | bytes 148
  9.4 8.9 %copy-start.38 = (bf16[24]{0:T(256)(128)(2,1)S(1)}, bf16[24]{0:T(256)(128)(2,1)}, u32[]{:S(2)}) copy-start(bf16[24]{0:T(256)(128)(2,1)} %param.25) | copy-start | bytes 148
  9.4 9.1 %copy-start.39 = (bf16[24]{0:T(256)(128)(2,1)S(1)}, bf16[24]{0:T(256)(128)(2,1)}, u32[]{:S(2)}) copy-start(bf16[24]{0:T(256)(128)(2,1)} %param.22) | copy-start | bytes 148
  9.5 9.3 %copy-start.40 = (bf16[24]{0:T(256)(128)(2,1)S(1)}, bf16[24]{0:T(256)(128)(2,1)}, u32[]{:S(2)}) copy-start(bf16[24]{0:T(256)(128)(2,1)} %param.23) | copy-start | bytes 148
  9.5 9.6 %copy-start.41 = (bf16[24]{0:T(256)(128)(2,1)S(1)}, bf16[24]{0:T(256)(128)(2,1)}, u32[]{:S(2)}) copy-start(bf16[24]{0:T(256)(128)(2,1)} %param.29) | copy-start | bytes 148
  9.5 9.8 %copy-start.42 = (bf16[48]{0:T(256)(128)(2,1)S(1)}, bf16[48]{0:T(256)(128)(2,1)}, u32[]{:S(2)}) copy-start(bf16[48]{0:T(256)(128)(2,1)} %param.24) | copy-start | bytes 292
  9.5 10.0 %copy-start.43 = (bf16[96]{0:T(256)(128)(2,1)S(1)}, bf16[96]{0:T(256)(128)(2,1)}, u32[]{:S(2)}) copy-start(bf16[96]{0:T(256)(128)(2,1)} %param.28) | copy-start | bytes 580
  9.5 251.2 %all-gather.11.cloned.1.call-start = ((), (), s32[]{:S(2)}) async-start(), calls=%async_computation.7 | async-start | bytes 4866048 | tf_op jit(solution)/shard_map/all_gather | solution.py:47
  10.1 519.1 %reduce-scatter.7.cloned.1.call-start = ((), (), s32[]{:S(2)}) async-start(), calls=%async_computation.9 | async-start | bytes 2433024 | tf_op jit(solution)/shard_map/reduce_scatter | solution.py:183
  12.0 62.2 %copy-start.21 = (f32[1182]{0:T(1024)}, f32[1182]{0:T(1024)S(1)}, u32[]{:S(2)}) copy-start(f32[1182]{0:T(1024)S(1)} %div.51) | copy-start | bytes 14188
  14.2 52.8 %copy-start.30 = (pred[1182]{0:T(1024)(128)(4,1)S(1)}, pred[1182]{0:T(1024)(128)(4,1)}, u32[]{:S(2)}) copy-start(pred[1182]{0:T(1024)(128)(4,1)} %constant.201) | copy-start | bytes 3550
  14.3 52.8 %copy-start.31 = (pred[1182]{0:T(1024)(128)(4,1)S(1)}, pred[1182]{0:T(1024)(128)(4,1)}, u32[]{:S(2)}) copy-start(pred[1182]{0:T(1024)(128)(4,1)} %constant.200) | copy-start | bytes 3550
  14.3 52.8 %copy-start.32 = (pred[1182]{0:T(1024)(128)(4,1)S(1)}, pred[1182]{0:T(1024)(128)(4,1)}, u32[]{:S(2)}) copy-start(pred[1182]{0:T(1024)(128)(4,1)} %constant.199) | copy-start | bytes 3550
  14.3 52.8 %copy-start.33 = (pred[1182]{0:T(1024)(128)(4,1)S(1)}, pred[1182]{0:T(1024)(128)(4,1)}, u32[]{:S(2)}) copy-start(pred[1182]{0:T(1024)(128)(4,1)} %constant.198) | copy-start | bytes 3550
  14.3 52.8 %copy-start.34 = (pred[1182]{0:T(1024)(128)(4,1)S(1)}, pred[1182]{0:T(1024)(128)(4,1)}, u32[]{:S(2)}) copy-start(pred[1182]{0:T(1024)(128)(4,1)} %constant.197) | copy-start | bytes 3550
  63.1 11.1 %copy-start.25 = (f32[768]{0:T(1024)}, f32[768]{0:T(1024)S(1)}, u32[]{:S(2)}) copy-start(f32[768]{0:T(1024)S(1)} %convert_element_type.113) | copy-start | bytes 9220
  63.1 18.9 %copy-start.27 = (f32[768]{0:T(1024)}, f32[768]{0:T(1024)S(1)}, u32[]{:S(2)}) copy-start(f32[768]{0:T(1024)S(1)} %convert_element_type.114) | copy-start | bytes 9220
  63.2 11.0 %copy-start.19 = (f32[1182]{0:T(1024)}, f32[1182]{0:T(1024)S(1)}, u32[]{:S(2)}) copy-start(f32[1182]{0:T(1024)S(1)} %add.135) | copy-start | bytes 14188
  63.2 11.0 %copy-start.23 = (f32[1182]{0:T(1024)}, f32[1182]{0:T(1024)S(1)}, u32[]{:S(2)}) copy-start(f32[1182]{0:T(1024)S(1)} %rsqrt.22) | copy-start | bytes 14188
  121.6 20.1 %copy-start = (bf16[6,197,12,64]{1,3,2,0:T(8,128)(2,1)}, bf16[6,197,12,64]{1,3,2,0:T(8,128)(2,1)S(1)}, u32[]{:S(2)}) copy-start(bf16[6,197,12,64]{1,3,2,0:T(8,128)(2,1)S(1)} %copy.66) | copy-start | bytes 5446660
  164.1 96.5 %copy-start.18 = (f32[1182]{0:T(1024)S(1)}, f32[1182]{0:T(1024)}, u32[]{:S(2)}) copy-start(f32[1182]{0:T(1024)} %select_select_fusion) | copy-start | bytes 14188
  281.5 12.5 %copy-start.17 = (f32[1182]{0:T(1024)S(1)}, f32[1182]{0:T(1024)}, u32[]{:S(2)}) copy-start(f32[1182]{0:T(1024)} %copy-done.16) | copy-start | bytes 14188
  281.5 12.5 %copy-start.4 = (f32[1182,768]{1,0:T(8,128)S(1)}, f32[1182,768]{1,0:T(8,128)}, u32[]{:S(2)}) copy-start(f32[1182,768]{1,0:T(8,128)} %copy-done.3) | copy-start | bytes 10893316
  301.7 234.0 %reduce-scatter.5.cloned.1.call-start = ((), (), s32[]{:S(2)}) async-start(), calls=%async_computation.8 | async-start | bytes 7299072 | tf_op jit(solution)/shard_map/reduce_scatter | solution.py:182
  316.4 8.3 %copy-start.1 = (bf16[6,197,12,64]{1,3,2,0:T(8,128)(2,1)S(1)}, bf16[6,197,12,64]{1,3,2,0:T(8,128)(2,1)}, u32[]{:S(2)}) copy-start(bf16[6,197,12,64]{1,3,2,0:T(8,128)(2,1)} %copy-done) | copy-start | bytes 5446660
  416.5 260.5 %reduce-scatter.11.cloned.1.call-start = ((), (), s32[]{:S(2)}) async-start(), calls=%async_computation.11 | async-start | bytes 9732096 | tf_op jit(solution)/shard_map/reduce_scatter | solution.py:185
  428.9 390.2 %reduce-scatter.9.cloned.1.call-start = ((), (), s32[]{:S(2)}) async-start(), calls=%async_computation.10 | async-start | bytes 9732096 | tf_op jit(solution)/shard_map/reduce_scatter | solution.py:184
  460.0 57.3 %copy-start.20 = (f32[1182]{0:T(1024)S(1)}, f32[1182]{0:T(1024)}, u32[]{:S(2)}) copy-start(f32[1182]{0:T(1024)} %copy-done.19) | copy-start | bytes 14188
  (20 other events, 59.2 us)
Sparse Core Ops, SparseCore 0:
  10.9 63.2 all-gather.4
  77.1 52.8 all-gather.6
  132.9 62.5 all-gather.8
  198.2 62.3 all-gather.10
  301.8 97.8 reduce-scatter.6
  416.6 119.0 reduce-scatter.4
  542.2 134.7 reduce-scatter.10
  684.5 134.5 reduce-scatter.8
where the time goes:
time: 831 us; the launch traced here: 826 us
  waiting for transfers between devices  349 us (42%)
  matrix products  237 us (29%)
  local copies, waits for them, and re-layouts  107 us (13%)
  blocking collectives  85.6 us (10%)
  other arithmetic  31.7 us (4%)
  between operations  15.7 us (2%)
    reduce_scatter x1, waiting for transfers between devices, per_device(): lax.psum_scatter(grad_up, ('fsdp', 'dp'), scatter_dimension=0, tiled=True)  142 us
    reduce_scatter x1, waiting for transfers between devices, per_device(): lax.psum_scatter(grad_down, ('fsdp', 'dp'), scatter_dimension=0, tiled=True)  141 us
    unnamed x2, blocking collectives  85.6 us
    dot_general x1, matrix products, per_device(): jnp.dot(normed_two, full_up, preferred_element_type=jnp.float32) + up_shift  42.6 us
    all_gather x1, waiting for transfers between devices, per_device(): lax.all_gather(w_up, ('fsdp', 'dp'), axis=0, tiled=True)  31.4 us
    dot_general x1, matrix products, per_device(): jnp.einsum('bhqk,bqhd->bkhd', back_scaled, queries, preferred_element_typ...  25.9 us
    dot_general x1, matrix products, per_device(): jnp.einsum('bhqk,bkhd->bqhd', back_scaled, key_rows, preferred_element_ty...  25.9 us
    all_gather x1, waiting for transfers between devices, per_device(): lax.all_gather(w_down, ('fsdp', 'dp'), axis=0, tiled=True)  22.5 us
  transfers between devices with their start and end apart: 8, of which 6 were waited for; matrix products, arithmetic and copies ran while one was open for 40% of the time, Pallas kernels for 0%

commit v1 on v0

v1 whole, which is shorter than its diff:
```python
import functools
import math

import jax
import jax.numpy as jnp
from jax import lax
from jax.experimental import pallas as pl
from jax.experimental.pallas import tpu as pltpu
from jax.sharding import PartitionSpec as P

HEADS = 12
EPSILON = 1e-06
AXES = ("fsdp", "dp")
LOW = jnp.bfloat16
WIDE = jnp.float32
NN = (((1,), (0,)), ((), ()))
NT = (((1,), (1,)), ((), ()))
TN = (((0,), (0,)), ((), ()))


def dot(a, b, dims=NN):
    return lax.dot_general(a, b, dims, preferred_element_type=WIDE)


def attend(seq_len, factor, proj_ref, out_ref):
    rows, model_width = out_ref.shape[1:]
    lane = lax.broadcasted_iota(jnp.int32, (1, 128), 1)
    key_at = lax.broadcasted_iota(jnp.int32, (1, rows), 1)
    ones = jnp.ones((rows, 128), jnp.bfloat16)
    zero = jnp.zeros((), jnp.bfloat16)
    for pair in range(model_width // 128):
        at = pair * 128
        queries = proj_ref[0, :, at : at + 128]
        keys = proj_ref[0, :, model_width + at : model_width + at + 128]
        values = proj_ref[0, :, 2 * model_width + at : 2 * model_width + at + 128]
        wide = jnp.concatenate([values, ones], axis=1)
        halves = []
        for half in range(2):
            mine = (lane < 64) if half == 0 else (lane >= 64)
            scores = dot(jnp.where(mine, queries, zero), keys, NT)
            scores = jnp.where(key_at < seq_len, scores, -jnp.inf)
            top = jnp.max(scores, axis=1, keepdims=True)
            expo = jnp.exp((scores - top) * factor).astype(jnp.bfloat16)
            both = dot(expo, wide, NN)
            halves.append(both[:, :128] / both[:, 128:])
        out_ref[0, :, at : at + 128] = jnp.where(lane < 64, halves[0], halves[1]).astype(jnp.bfloat16)


def attend_back(seq_len, factor, proj_ref, back_ref, out_ref):
    rows, model_width = back_ref.shape[1:]
    lane = lax.broadcasted_iota(jnp.int32, (1, 128), 1)
    key_at = lax.broadcasted_iota(jnp.int32, (rows, 1), 0)
    zero = jnp.zeros((), jnp.bfloat16)
    for pair in range(model_width // 128):
        at = pair * 128
        queries = proj_ref[0, :, at : at + 128]
        keys = proj_ref[0, :, model_width + at : model_width + at + 128]
        values = proj_ref[0, :, 2 * model_width + at : 2 * model_width + at + 128]
        back = back_ref[0, :, at : at + 128]
        parts = []
        for half in range(2):
            mine = (lane < 64) if half == 0 else (lane >= 64)
            queries_one = jnp.where(mine, queries, zero)
            back_one = jnp.where(mine, back, zero)
            scores = dot(keys, queries_one, NT)
            scores = jnp.where(key_at < seq_len, scores, -jnp.inf)
            top = jnp.max(scores, axis=0, keepdims=True)
            expo = jnp.exp((scores - top) * factor)
            probs = expo * (1.0 / jnp.sum(expo, axis=0, keepdims=True))
            back_probs = dot(values, back_one, NT)
            weighted = probs * back_probs
            row_dot = jnp.sum(weighted, axis=0, keepdims=True)
            scaled = ((weighted - probs * row_dot) * factor).astype(jnp.bfloat16)
            parts.append(
                (
                    dot(scaled, keys, TN),
                    dot(scaled, queries_one, NN),
                    dot(probs.astype(jnp.bfloat16), back_one, NN),
                )
            )
        first, second = parts
        out_ref[0, :, at : at + 128] = jnp.where(lane < 64, first[0], second[0]).astype(jnp.bfloat16)
        out_ref[0, :, model_width + at : model_width + at + 128] = (first[1] + second[1]).astype(jnp.bfloat16)
        out_ref[0, :, 2 * model_width + at : 2 * model_width + at + 128] = (first[2] + second[2]).astype(jnp.bfloat16)


def whole(shape):
    return pl.BlockSpec((1,) + shape, lambda i: (i, 0, 0))


def attention(projected, seq_len, factor):
    images, rows, wide = projected.shape
    return pl.pallas_call(
        functools.partial(attend, seq_len, factor),
        grid=(images,),
        in_specs=[whole((rows, wide))],
        out_specs=whole((rows, wide // 3)),
        out_shape=jax.ShapeDtypeStruct((images, rows, wide // 3), jnp.bfloat16),
        compiler_params=pltpu.CompilerParams(vmem_limit_bytes=40 << 20),
    )(projected)


def attention_back(projected, back_head, seq_len, factor):
    images, rows, wide = projected.shape
    return pl.pallas_call(
        functools.partial(attend_back, seq_len, factor),
        grid=(images,),
        in_specs=[whole((rows, wide)), whole((rows, wide // 3))],
        out_specs=whole((rows, wide)),
        out_shape=jax.ShapeDtypeStruct((images, rows, wide), jnp.bfloat16),
        compiler_params=pltpu.CompilerParams(vmem_limit_bytes=40 << 20),
    )(projected, back_head)


TERMS = (0.254829592, -0.284496736, 1.421413741, -1.453152027, 1.061405429)


def gelu_and_slope(hidden):
    size = jnp.abs(hidden) * math.sqrt(0.5)
    t = 1.0 / (1.0 + 0.3275911 * size)
    bell = jnp.exp(-size * size)
    series = TERMS[4] * t + TERMS[3]
    for term in TERMS[2::-1]:
        series = series * t + term
    tail = 0.5 * series * t * bell
    below = jnp.where(hidden < 0, tail, 1.0 - tail)
    return hidden * below, below + hidden * bell * (1.0 / math.sqrt(2.0 * math.pi))


def expand(step, rows_ref, weight_ref, shift_ref, active_ref, slope_ref):
    for start in range(0, rows_ref.shape[0], step):
        at = pl.ds(start, step)
        hidden = dot(rows_ref[at, :], weight_ref[...]) + shift_ref[...]
        active, slope = gelu_and_slope(hidden)
        active_ref[at, :] = active.astype(LOW)
        slope_ref[at, :] = slope.astype(LOW)


def expanded(rows, weight, shift, step, width=512):
    count, depth = rows.shape
    full = weight.shape[1]
    out = jax.ShapeDtypeStruct((count, full), LOW)
    spec = pl.BlockSpec((count, width), lambda j: (0, j))
    return pl.pallas_call(
        functools.partial(expand, step),
        grid=(full // width,),
        in_specs=[
            pl.BlockSpec((count, depth), lambda j: (0, 0)),
            pl.BlockSpec((depth, width), lambda j: (0, j)),
            pl.BlockSpec((1, width), lambda j: (0, j)),
        ],
        out_specs=[spec, spec],
        out_shape=[out, out],
        compiler_params=pltpu.CompilerParams(vmem_limit_bytes=40 << 20),
        cost_estimate=pl.CostEstimate(
            flops=2 * count * depth * full, bytes_accessed=6 * count * full, transcendentals=2 * count * full
        ),
    )(rows, weight, shift)


def centred(values):
    center = values - jnp.mean(values, axis=-1, keepdims=True)
    rate = lax.rsqrt(jnp.mean(center * center, axis=-1, keepdims=True) + EPSILON)
    return center * rate, rate


def norm_back(values, scale, grad):
    unit, rate = centred(values)
    scaled = grad * scale
    inner = jnp.mean(scaled * unit, axis=-1, keepdims=True)
    back = rate * (scaled - jnp.mean(scaled, axis=-1, keepdims=True) - unit * inner)
    return back, jnp.sum(grad * unit, axis=0), jnp.sum(grad, axis=0)


def column_total(values):
    return jnp.sum(values.astype(WIDE), axis=0)


def per_device(
    devices,
    tokens,
    w_qkv,
    w_out,
    w_up,
    w_down,
    norm1_scale,
    norm1_offset,
    qv_bias,
    out_bias,
    norm2_scale,
    norm2_offset,
    up_bias,
    down_bias,
    cotangent,
    counts,
):
    images, seq_len, width = tokens.shape
    share = width // devices
    rows = -(-seq_len // 16) * 16
    row_count = images * rows
    factor = (width // HEADS) ** -0.5
    small = (norm1_scale, norm1_offset, qv_bias, out_bias, norm2_scale, norm2_offset, up_bias, down_bias)
    small_sizes = [v.shape[0] for v in small]

    def columns(matrix):
        return [matrix[:, at : at + width] for at in range(0, matrix.shape[1], width)]

    def small_rows(parts):
        flat = jnp.concatenate(parts, axis=-1)
        return jnp.pad(flat, [(0, 0)] * (flat.ndim - 1) + [(0, 16 * width - flat.shape[-1])]).reshape(
            flat.shape[:-1] + (16, width)
        )

    def small_split(block):
        flat, at, parts = block.reshape(block.shape[0], -1), 0, []
        for size in small_sizes:
            parts.append(flat[:, at : at + size])
            at += size
        return parts

    pack = jnp.concatenate([*columns(w_qkv), w_out, *columns(w_up), w_down, small_rows(small)], axis=0)
    whole = lax.all_gather(pack, AXES, axis=0, tiled=False)
    at = 0

    def take(count, size=share):
        nonlocal at
        parts = []
        for _ in range(count):
            parts.append(whole[:, at : at + size].reshape(devices * size, width))
            at += size
        return parts[0] if count == 1 else jnp.concatenate(parts, axis=1)

    full_qkv = take(w_qkv.shape[1] // width)
    full_out = take(1)
    full_up = take(w_up.shape[1] // width)
    full_down = take(1, w_down.shape[0])
    vectors = [v.reshape(-1).astype(WIDE) for v in small_split(whole[:, at:])]
    scale_one, offset_one, qv_full, out_shift, scale_two, offset_two, up_shift, down_shift = vectors

    def padded(array):
        return jnp.pad(array, ((0, 0), (0, rows - seq_len), (0, 0))).reshape(row_count, width)

    live = (jnp.arange(images) < counts[0])[:, None, None]
    inputs = padded(tokens).astype(WIDE)
    seed_low = padded(jnp.where(live, cotangent, jnp.zeros((), LOW)))

    normed = (centred(inputs)[0] * scale_one + offset_one).astype(LOW)
    bias_full = jnp.concatenate([qv_full[:width], jnp.zeros((width,), WIDE), qv_full[width:]])
    projected = (dot(normed, full_qkv) + bias_full).astype(LOW).reshape(images, rows, 3 * width)
    head_out = attention(projected, seq_len, factor).reshape(row_count, width)
    middle = inputs + dot(head_out, full_out) + out_shift
    normed_two = (centred(middle)[0] * scale_two + offset_two).astype(LOW)
    active, slope = expanded(normed_two, full_up, up_shift[None], rows)
    result = (middle + dot(active, full_down) + down_shift).reshape(images, rows, width)[:, :seq_len]
    out_tokens = jnp.where(live, result, 0.0).astype(LOW)

    grad_down = dot(active, seed_low, TN).astype(LOW)
    back_hidden = (dot(seed_low, full_down, NT) * slope.astype(WIDE)).astype(LOW)
    grad_up = dot(normed_two, back_hidden, TN).astype(LOW)
    back_two = dot(back_hidden, full_up, NT)
    middle_part, grad_scale_two, grad_offset_two = norm_back(middle, scale_two, back_two)
    back_middle = seed_low.astype(WIDE) + middle_part
    back_branch = back_middle.astype(LOW)
    grad_out = dot(head_out, back_branch, TN).astype(LOW)
    blocks = lambda matrix: [m.reshape(devices, -1, width) for m in columns(matrix)]
    early = jnp.concatenate([*blocks(grad_out), *blocks(grad_up), *blocks(grad_down)], axis=1)
    early = lax.psum_scatter(early, AXES, scatter_dimension=0, tiled=True)[0]

    back_head = dot(back_branch, full_out, NT).astype(LOW).reshape(images, rows, width)
    back_projected = attention_back(projected, back_head, seq_len, factor).reshape(row_count, 3 * width)
    grad_qkv = dot(normed, back_projected, TN).astype(LOW)
    back_one = dot(back_projected, full_qkv, NT)
    input_part, grad_scale_one, grad_offset_one = norm_back(inputs, scale_one, back_one)
    grad_inputs = (back_middle + input_part).reshape(images, rows, width)[:, :seq_len]
    sums = column_total(back_projected)
    small_grads = (
        grad_scale_one,
        grad_offset_one,
        jnp.concatenate([sums[:width], sums[2 * width :]]),
        column_total(back_branch),
        grad_scale_two,
        grad_offset_two,
        column_total(back_hidden),
        column_total(seed_low),
    )
    small_block = small_rows([v.astype(LOW).reshape(devices, -1) for v in small_grads])
    late = jnp.concatenate([*blocks(grad_qkv), small_block], axis=1)
    late = lax.psum_scatter(late, AXES, scatter_dimension=0, tiled=True)[0]

    def join(block, count):
        return jnp.concatenate([block[i * share : (i + 1) * share] for i in range(count)], axis=1).astype(WIDE)

    ups = w_up.shape[1] // width
    small_out = [v[0].astype(WIDE) for v in small_split(late[None, 3 * share :])]
    return (
        out_tokens,
        grad_inputs,
        join(late, 3),
        join(early, 1),
        join(early[share:], ups),
        early[share * (1 + ups) :].astype(WIDE),
        *small_out,
    )


def solution(mesh):
    split = P(AXES)
    return jax.shard_map(
        functools.partial(per_device, mesh.shape["fsdp"] * mesh.shape["dp"]),
        mesh=mesh,
        in_specs=(split,) * 15,
        out_specs=(split,) * 14,
        check_vma=False,
    )
```

time: 831 us -> 562 us (0.68)
  matrix products: 237 us -> 92.1 us
  blocking collectives: 85.6 us -> 0 us
  Pallas kernels: 0 us -> 55.4 us
  local copies, waits for them, and re-layouts: 107 us -> 51.6 us
  waiting for transfers between devices: 349 us -> 310 us
    dot_general x18 -> x11, matrix products: 237 us -> 92.1 us  [dot(): return lax.dot_general(a, b, dims, preferred_element_type=WIDE)]
    unnamed x2 -> x0, blocking collectives: 85.6 us -> none
    reduce_scatter x4 -> x2, waiting for transfers between devices: 290 us -> 209 us  [the longest x1 144 us: per_device(): early = lax.psum_scatter(early, AXES, scatter_dimension=0, tiled=True)[0]]
    reshape x13 -> x4, local copies, waits for them, and re-layouts: 65.5 us -> 0.32 us  [the longest x3 0.27 us: per_device(): v.astype(LOW).reshape(devices, -1)]
    pallas_call x0 -> x3, Pallas kernels: none -> 55.4 us  [the longest x1 27.6 us: attention_back(): pl.pallas_call(functools.partial(attend_back, seq_len, factor), grid=(ima...]
    all_gather x4 -> x1, waiting for transfers between devices: 56.5 us -> 101 us  [per_device(): whole = lax.all_gather(pack, AXES, axis=0, tiled=False)]
    slice x3 -> x11, local copies, waits for them, and re-layouts: 2.23 us -> 19.8 us  [the longest x2 11.7 us: take(): parts.append(whole[:, at:at + size].reshape(devices * size, width))]
    reduce_sum x9 -> x6, other arithmetic: 24.2 us -> 10.5 us  [the longest x3 7.43 us: column_total(): return jnp.sum(values.astype(WIDE), axis=0)]
  transfers between devices with their start and end apart: 8 -> 3, of which waited for: 6 -> 3; matrix products, arithmetic and copies ran while one was open for 40% -> 9% of each run, Pallas kernels for 0% -> 0%
where the time goes in v1:
time: 562 us; the launch traced here: 558 us
  waiting for transfers between devices  310 us (55%)
  matrix products  92.1 us (16%)
  Pallas kernels  55.4 us (10%)
  local copies, waits for them, and re-layouts  51.6 us (9%)
  other arithmetic  32.8 us (6%)
  between operations  15.2 us (3%)
    reduce_scatter x1, waiting for transfers between devices, per_device(): early = lax.psum_scatter(early, AXES, scatter_dimension=0, tiled=True)[0]  144 us
    all_gather x1, waiting for transfers between devices, per_device(): whole = lax.all_gather(pack, AXES, axis=0, tiled=False)  101 us
    dot_general x11, matrix products, dot(): return lax.dot_general(a, b, dims, preferred_element_type=WIDE)  92.1 us
    reduce_scatter x1, waiting for transfers between devices, per_device(): late = lax.psum_scatter(late, AXES, scatter_dimension=0, tiled=True)[0]  65.1 us
    pallas_call x1, Pallas kernels, attention_back(): pl.pallas_call(functools.partial(attend_back, seq_len, factor), grid=(ima...  27.6 us
    unnamed x64, local copies, waits for them, and re-layouts  21.9 us
    pallas_call x1, Pallas kernels, expanded(): pl.pallas_call(functools.partial(expand, step), grid=(full // width,), in...  20 us
    slice x2, local copies, waits for them, and re-layouts, take(): parts.append(whole[:, at:at + size].reshape(devices * size, width))  11.7 us
  transfers between devices with their start and end apart: 3, of which 3 were waited for; matrix products, arithmetic and copies ran while one was open for 9% of the time, Pallas kernels for 0%

profile of v1, /device:TPU:0, one launch (start us, length us, event | category | flops | bytes accessed | tf_op | source)
XLA Modules:
  0.0 557.9 jit_solution(5965967137203063927)
XLA Ops:
  7.2 5.6 concatenate.39
  21.5 1.8 convert_reduce_fusion
  24.2 2.2 pad_convert_fusion
  26.4 2.5 fusion.3
  28.9 101.4 %all-gather.3.cloned.1.call-done = bf16[9728,768]{1,0:T(8,128)(2,1)} async-done(((bf16[304,768]{1,0:T(8,128)(2,1)}), bf16[9728,768]{1,0:T(8,128)(2,1)}) %all-gather.3.cloned.1.call-update) | async-done | bytes 14942224 | tf_op jit(solution)/shard_map/all_gather | solution.py:222
  131.9 4.9 slice.303
  136.8 6.8 %fusion.30 = (bf16[32,24,768]{2,1,0:T(8,128)(2,1)S(1)}, bf16[32,24,768]{2,1,0:T(8,128)(2,1)}, bf16[32,24,768]{2,1,0:T(8,128)(2,1)}, bf16[32,24,768]{2,1,0:T(8,12...) fusion(bf16[32,304,768]{2,1,0:T(8,128)(2,1)} %bitcast.136), kind=kLoop, calls=%fused_computation.118 | loop fusion | bytes 18874368 | tf_op jit(solution)/shard_map/slice | solution.py:229
  144.4 7.5 %fusion = bf16[1248,2304]{1,0:T(8,128)(2,1)S(1)} fusion(f32[2304]{0:T(1024)S(1)} %pad_maximum_fusion.5, f32[1248,768]{1,0:T(8,128)} %fusion.3, f32[768]{0:T(1024)S(1)} %reshape.371, f32[768]{0:T(1024)S(1)} %reshape.370, bf16[768,768]{1,0:T(8,128)(2,1)S(1)} %bitcast.163, bf16[768,768]{1,0:T(8,128)(2,1)} %bitcast.165, bf16[768,768]{1,0:T(8,128)(2,1)} %bitcast.167), kind=kOutput, calls=%fused_computation.2 | convolution fusion | flops 4435845120 | bytes 13138944 | tf_op jit(solution)/shard_map/dot_general | solution.py:22
  151.9 7.8 %shard_map.254 = bf16[6,208,768]{2,1,0:T(8,128)(2,1)S(1)} custom-call(bf16[6,208,2304]{2,1,0:T(8,128)(2,1)S(1)} %bitcast.127), custom_call_target="tpu_custom_call" | custom-call | tf_op jit(solution)/shard_map/pallas_call | solution.py:93
  159.7 1.8 fusion.35
  165.4 20.0 %shard_map.255 = (bf16[1248,3072]{1,0:T(8,128)(2,1)S(1)}, bf16[1248,3072]{1,0:T(8,128)(2,1)}) custom-call(bf16[1248,768]{1,0:T(8,128)(2,1)S(1)} %add_convert_fusion.1.rows_ref, bf16[768,3072]{1,0:T(8,128)(2,1)S(1)} %pad_maximum_fusion.weight_ref, f32[1,3072]{1,0:T(1,128)S(1)} %reshape.375.shift_ref), custom_call_target="tpu_custom_call" | custom-call | flops 5888802816 | bytes 23003136 | tf_op jit(solution)/shard_map/pallas_call | solution.py:144
  185.4 12.5 %fusion.2 = bf16[1248,768]{1,0:T(8,128)(2,1)S(1)} fusion(f32[1248,768]{1,0:T(8,128)} %copy-done.5, bf16[1248,3072]{1,0:T(8,128)(2,1)S(1)} %get-tuple-element.16, bf16[3072,768]{1,0:T(8,128)(2,1)} %bitcast.152, f32[768]{0:T(1024)S(1)} %reshape.376), kind=kOutput, calls=%fused_computation.11 | convolution fusion | flops 5891678208 | bytes 18140160 | tf_op jit(solution)/shard_map/dot_general | solution.py:22
  198.0 2.1 broadcast_select_fusion
  200.6 12.6 %fusion.36 = (bf16[3072]{0:T(1024)(128)(2,1)S(1)}, bf16[1248,3072]{1,0:T(8,128)(2,1)}) fusion(bf16[1248,3072]{1,0:T(8,128)(2,1)} %get-tuple-element.17, bf16[1248,768]{1,0:T(8,128)(2,1)S(1)} %bitcast.138, bf16[3072,768]{1,0:T(8,128)(2,1)} %bitcast.153), kind=kOutput, calls=%fused_computation.124 | convolution fusion | flops 5904135168 | bytes 21977088 | tf_op jit(solution)/shard_map/dot_general | solution.py:22
  213.2 12.3 %multiply_reduce_fusion = (bf16[768]{0:T(1024)(128)(2,1)S(1)}, f32[1248]{0:T(1024)S(1)}, f32[1248]{0:T(1024)S(1)}, bf16[768]{0:T(1024)(128)(2,1)S(1)}, f32[1248,768]{1,0:T(8,128)}) fusion(f32[1248,768]{1,0:T(8,128)S(1)} %copy-done.6, f32[1248]{0:T(1024)S(1)} %add_rsqrt_fusion, f32[1248]{0:T(1024)S(1)} %broadcast_multiply_fusion.4, f32[768]{0:T(1024)S(1)} %reshape.373, ...), kind=kOutput, calls=%fused_computation.14 | convolution fusion | flops 5916299264 | bytes 20080128 | tf_op jit(solution)/shard_map/dot_general | solution.py:22
  225.5 3.4 convert_reduce_fusion.1
  229.0 1.7 convolution_convert_fusion.2
  230.8 27.6 %shard_map.256 = bf16[6,208,2304]{2,1,0:T(8,128)(2,1)S(1)} custom-call(bf16[6,208,2304]{2,1,0:T(8,128)(2,1)S(1)} %bitcast.128, bf16[6,208,768]{2,1,0:T(8,128)(2,1)S(1)} %bitcast.129), custom_call_target="tpu_custom_call" | custom-call | tf_op jit(solution)/shard_map/pallas_call | solution.py:105
  258.4 2.5 copy-done
  260.9 3.5 reduce.7
  264.4 10.2 %bitcast_convert_fusion = bf16[768,2304]{1,0:T(8,128)(2,1)} fusion(bf16[6,208,2304]{2,1,0:T(8,128)(2,1)} %copy-done, f32[768]{0:T(1024)S(1)} %reshape.371, f32[768]{0:T(1024)S(1)} %reshape.370, f32[6,208]{1,0:T(8,128)S(1)} %add_rsqrt_fusion.1, f32[6,208]{1,0:T(8,128)S(1)} %broadcast_multiply_fusion.5, bf16[6,197,768]{2,1,0:T(8,128)(2,1)} %param.15), kind=kOutput, calls=%fused_computation.3 | convolution fusion | flops 4424122368 | bytes 11121408 | tf_op jit(solution)/shard_map/dot_general | solution.py:22
  275.1 12.3 %fusion.29 = (bf16[768]{0:T(1024)(128)(2,1)S(1)}, bf16[768]{0:T(1024)(128)(2,1)S(1)}, f32[1248]{0:T(1024)S(1)}, f32[1248]{0:T(1024)S(1)}, f32[1248,768]{1,0:T(8,128)}) fusion(f32[1248]{0:T(1024)S(1)} %rsqrt.23, f32[1248]{0:T(1024)S(1)} %div.31, bf16[6,197,768]{2,1,0:T(8,128)(2,1)} %param.15, f32[1248,768]{1,0:T(8,128)} %fusion.3, f32[768]{0:T(1024)S(1)} %reshape.370, ...), kind=kOutput, calls=%fused_computation.117 | convolution fusion | flops 4436799488 | bytes 18799104 | tf_op jit(solution)/shard_map/dot_general | solution.py:22
  287.5 3.6 fusion.32
  291.7 3.5 pad_maximum_fusion.1
  295.5 4.4 convolution_convert_fusion.3
  301.1 9.9 %convolution_convert_fusion.1 = bf16[768,3072]{1,0:T(8,128)(2,1)S(1)} fusion(bf16[1248,768]{1,0:T(8,128)(2,1)S(1)} %add_convert_fusion.1.rows_ref, bf16[1248,3072]{1,0:T(8,128)(2,1)} %get-tuple-element.78), kind=kOutput, calls=%fused_computation.5 | convolution fusion | flops 5891162112 | bytes 14303232 | tf_op jit(solution)/shard_map/dot_general | solution.py:22
  317.0 6.9 %convolution_convert_fusion = bf16[3072,768]{1,0:T(8,128)(2,1)S(1)} fusion(bf16[1248,3072]{1,0:T(8,128)(2,1)S(1)} %bitcast.133, bf16[1248,768]{1,0:T(8,128)(2,1)S(1)} %bitcast.139), kind=kOutput, calls=%fused_computation.4 | convolution fusion | flops 5891162112 | bytes 14303232 | tf_op jit(solution)/shard_map/dot_general | solution.py:22
  323.9 2.5 constant_dynamic-update-slice_fusion.3
  328.0 4.1 multiply_add_fusion
  332.1 2.1 slice.306
  334.2 65.1 %reduce-scatter.3.cloned.1.call-done = bf16[1,88,768]{2,1,0:T(8,128)(2,1)} async-done(((bf16[32,88,768]{2,1,0:T(8,128)(2,1)}), bf16[1,88,768]{2,1,0:T(8,128)(2,1)}) %reduce-scatter.3.cloned.1.call-update) | async-done | bytes 135184 | tf_op jit(solution)/shard_map/reduce_scatter | solution.py:288
  403.4 144.0 %reduce-scatter.5.cloned.1.call-done = bf16[1,216,768]{2,1,0:T(8,128)(2,1)} async-done(((bf16[32,216,768]{2,1,0:T(8,128)(2,1)}), bf16[1,216,768]{2,1,0:T(8,128)(2,1)}) %reduce-scatter.5.cloned.1.call-update) | async-done | bytes 331792 | tf_op jit(solution)/shard_map/reduce_scatter | solution.py:267
  (126 shorter events, 33.7 us)
Async XLA Ops:
  7.2 16.2 %copy-start.3 = (bf16[6,197,768]{2,1,0:T(8,128)(2,1)S(1)}, bf16[6,197,768]{2,1,0:T(8,128)(2,1)}, u32[]{:S(2)}) copy-start(bf16[6,197,768]{2,1,0:T(8,128)(2,1)} %param.15) | copy-start | bytes 5446660
  7.2 123.0 %all-gather.3.cloned.1.call-start = ((), (), s32[]{:S(2)}) async-start(), calls=%async_computation.4 | async-start | bytes 15409152 | tf_op jit(solution)/shard_map/all_gather | solution.py:222
  20.0 0.8 copy-start.20
  20.8 378.5 %reduce-scatter.3.cloned.1.call-start = ((), (), s32[]{:S(2)}) async-start(), calls=%async_computation.2 | async-start | bytes 4460544 | tf_op jit(solution)/shard_map/reduce_scatter | solution.py:288
  143.6 8.3 %copy-start.16 = (bf16[32,24,768]{2,1,0:T(8,128)(2,1)}, bf16[32,24,768]{2,1,0:T(8,128)(2,1)S(1)}, u32[]{:S(2)}) copy-start(bf16[32,24,768]{2,1,0:T(8,128)(2,1)S(1)} %get-tuple-element.35) | copy-start | bytes 3538948
  151.9 7.8 %copy-start.14 = (f32[6,208,768]{2,1,0:T(8,128)S(1)}, f32[6,208,768]{2,1,0:T(8,128)}, u32[]{:S(2)}) copy-start(f32[6,208,768]{2,1,0:T(8,128)} %pad_convert_fusion) | copy-start | bytes 11501572
  151.9 7.8 %copy-start.18 = (bf16[32,24,768]{2,1,0:T(8,128)(2,1)S(1)}, bf16[32,24,768]{2,1,0:T(8,128)(2,1)}, u32[]{:S(2)}) copy-start(bf16[32,24,768]{2,1,0:T(8,128)(2,1)} %get-tuple-element.34) | copy-start | bytes 3538948
  159.6 2.4 copy-start.1
  161.5 1.8 copy-start.5
  162.0 2.0 copy-start.10
  162.1 2.4 copy-start.11
  162.1 2.7 copy-start.12
  185.4 12.5 %copy-start.2 = (bf16[1248,3072]{1,0:T(8,128)(2,1)}, bf16[1248,3072]{1,0:T(8,128)(2,1)S(1)}, u32[]{:S(2)}) copy-start(bf16[1248,3072]{1,0:T(8,128)(2,1)S(1)} %get-tuple-element.16) | copy-start | bytes 23003140
  185.4 12.5 %copy-start.15 = (bf16[6,197,768]{2,1,0:T(8,128)(2,1)S(1)}, bf16[6,197,768]{2,1,0:T(8,128)(2,1)}, u32[]{:S(2)}) copy-start(bf16[6,197,768]{2,1,0:T(8,128)(2,1)} %param.28) | copy-start | bytes 5446660
  200.6 24.9 %copy-start.8 = (bf16[6,208,768]{2,1,0:T(8,128)(2,1)}, bf16[6,208,768]{2,1,0:T(8,128)(2,1)S(1)}, u32[]{:S(2)}) copy-start(bf16[6,208,768]{2,1,0:T(8,128)(2,1)S(1)} %get-tuple-element.46) | copy-start | bytes 5750788
  200.6 12.6 %copy-start.6 = (f32[1248,768]{1,0:T(8,128)S(1)}, f32[1248,768]{1,0:T(8,128)}, u32[]{:S(2)}) copy-start(f32[1248,768]{1,0:T(8,128)} %copy-done.5) | copy-start | bytes 11501572
  200.6 12.6 %copy-start.13 = (bf16[32,24,768]{2,1,0:T(8,128)(2,1)S(1)}, bf16[32,24,768]{2,1,0:T(8,128)(2,1)}, u32[]{:S(2)}) copy-start(bf16[32,24,768]{2,1,0:T(8,128)(2,1)} %get-tuple-element.33) | copy-start | bytes 3538948
  225.5 3.4 copy-start.19
  228.9 1.9 copy-start.7
  258.4 2.5 copy-start
  264.4 10.7 %copy-start.17 = (bf16[32,24,768]{2,1,0:T(8,128)(2,1)S(1)}, bf16[32,24,768]{2,1,0:T(8,128)(2,1)}, u32[]{:S(2)}) copy-start(bf16[32,24,768]{2,1,0:T(8,128)(2,1)} %copy-done.16) | copy-start | bytes 3538948
  295.3 252.0 %reduce-scatter.5.cloned.1.call-start = ((), (), s32[]{:S(2)}) async-start(), calls=%async_computation.3 | async-start | bytes 10948608 | tf_op jit(solution)/shard_map/reduce_scatter | solution.py:267
  311.1 4.9 slice-start
  311.4 4.6 slice-start.1
  312.5 4.5 copy-start.9
  326.4 1.5 copy-start.4
Sparse Core Ops, SparseCore 0:
  20.9 109.3 all-gather.2
  295.4 103.8 reduce-scatter.2
  406.4 140.8 reduce-scatter.4

commit v2 on v1

--- a/solution.py
+++ b/solution.py
@@ -176,8 +176,80 @@
     return jnp.sum(values.astype(WIDE), axis=0)
 
 
+def places(sizes):
+    return [(name, 1 << k) for name in AXES for k in reversed(range(sizes[name].bit_length() - 1))]
+
+
+def flipped(block, name, bit, sizes):
+    return lax.ppermute(block, name, [(i, i ^ bit) for i in range(sizes[name])])
+
+
+def is_set(name, bit):
+    return (lax.axis_index(name) & bit) != 0
+
+
+def routes(sizes):
+    order = places(sizes)
+    far = [p for p in order if p[0] == "fsdp" and p[1] > 1]
+    near = [p for p in order if p[0] == "fsdp" and p[1] == 1]
+    other = [p for p in order if p[0] == "dp" and p[1] > 1]
+    core = [p for p in order if p[0] == "dp" and p[1] == 1]
+    return far, near + other, other + near, core
+
+
+def gather_by(block, steps, done, order, sizes):
+    for place in steps:
+        got = flipped(block, *place, sizes)
+        high = is_set(*place)
+        at = sum(order.index(p) < order.index(place) for p in done)
+        block = jnp.stack([jnp.where(high, got, block), jnp.where(high, block, got)], axis=at)
+        done = done + [place]
+    return block, done
+
+
+def scatter_by(block, steps, left, sizes, kind=LOW):
+    for place in steps:
+        at = left.index(place)
+        bit = is_set(*place).astype(jnp.int32)
+        got = flipped(lax.dynamic_index_in_dim(block, 1 - bit, at, keepdims=False), *place, sizes)
+        mine = lax.dynamic_index_in_dim(block, bit, at, keepdims=False)
+        block = (mine.astype(WIDE) + got.astype(WIDE)).astype(kind)
+        left = [p for p in left if p != place]
+    return block, left
+
+
+def gathered(block, sizes):
+    order = places(sizes)
+    far, one_way, other_way, core = routes(sizes)
+    block, done = gather_by(block, far, [], order, sizes)
+    half = block.shape[-1] // 2
+    parts = []
+    for part, way in ((block[..., :half], one_way), (block[..., half:], other_way)):
+        part, _ = gather_by(part, way + core, done, order, sizes)
+        parts.append(part.reshape((-1,) + part.shape[-2:]))
+    return parts
+
+
+def scattered(blocks, sizes):
+    order = places(sizes)
+    far, one_way, other_way, core = routes(sizes)
+    blocks = blocks.reshape((2,) * len(order) + blocks.shape[1:])
+    blocks, left = scatter_by(blocks, core, order, sizes)
+    half = blocks.shape[-1] // 2
+    one, rest = scatter_by(blocks[..., :half], one_way[::-1], left, sizes)
+    two, rest = scatter_by(blocks[..., half:], other_way[::-1], left, sizes)
+    blocks, rest = scatter_by(jnp.concatenate([one, two], axis=-1), far[:0:-1], rest, sizes)
+    return scatter_by(blocks, far[:1], rest, sizes, WIDE)[0]
+
+
+def scattered_small(blocks, sizes):
+    order = places(sizes)
+    blocks = blocks.reshape((2,) * len(order) + blocks.shape[1:])
+    return scatter_by(blocks, order[::-1], order, sizes, WIDE)[0]
+
+
 def per_device(
-    devices,
+    sizes,
     tokens,
     w_qkv,
     w_out,
@@ -194,6 +266,7 @@
     cotangent,
     counts,
 ):
+    devices = sizes["fsdp"] * sizes["dp"]
     images, seq_len, width = tokens.shape
     share = width // devices
     rows = -(-seq_len // 16) * 16
@@ -207,8 +280,8 @@
 
     def small_rows(parts):
         flat = jnp.concatenate(parts, axis=-1)
-        return jnp.pad(flat, [(0, 0)] * (flat.ndim - 1) + [(0, 16 * width - flat.shape[-1])]).reshape(
-            flat.shape[:-1] + (16, width)
+        return jnp.pad(flat, [(0, 0)] * (flat.ndim - 1) + [(0, 8 * width - flat.shape[-1])]).reshape(
+            flat.shape[:-1] + (8, width)
         )
 
     def small_split(block):
@@ -218,8 +291,15 @@
             at += size
         return parts
 
-    pack = jnp.concatenate([*columns(w_qkv), w_out, *columns(w_up), w_down, small_rows(small)], axis=0)
-    whole = lax.all_gather(pack, AXES, axis=0, tiled=False)
+    first = jnp.concatenate([*columns(w_qkv), small_rows(small)], axis=0)
+    first_left, first_right = gathered(first, sizes)
+    qkv_parts = []
+    for i in range(3):
+        for part in (first_left, first_right):
+            qkv_parts.append(part[:, i * share : (i + 1) * share].reshape(width, width // 2))
+    full_qkv = jnp.concatenate(qkv_parts, axis=1)
+    rest = jnp.concatenate([w_out, *columns(w_up), w_down], axis=0)
+    whole = lax.all_gather(rest, AXES, axis=0, tiled=False)
     at = 0
 
     def take(count, size=share):
@@ -230,11 +310,10 @@
             at += size
         return parts[0] if count == 1 else jnp.concatenate(parts, axis=1)
 
-    full_qkv = take(w_qkv.shape[1] // width)
     full_out = take(1)
     full_up = take(w_up.shape[1] // width)
     full_down = take(1, w_down.shape[0])
-    vectors = [v.reshape(-1).astype(WIDE) for v in small_split(whole[:, at:])]
+    vectors = [v.reshape(-1).astype(WIDE) for v in small_split(first_left[:, 3 * share :])]
     scale_one, offset_one, qv_full, out_shift, scale_two, offset_two, up_shift, down_shift = vectors
 
     def padded(array):
@@ -283,15 +362,15 @@
         column_total(back_hidden),
         column_total(seed_low),
     )
-    small_block = small_rows([v.astype(LOW).reshape(devices, -1) for v in small_grads])
-    late = jnp.concatenate([*blocks(grad_qkv), small_block], axis=1)
-    late = lax.psum_scatter(late, AXES, scatter_dimension=0, tiled=True)[0]
+    small_block = small_rows([v.reshape(devices, -1) for v in small_grads])[:, :1]
+    small_sum = scattered_small(small_block, sizes)
+    late = scattered(jnp.concatenate(blocks(grad_qkv), axis=1), sizes)
 
     def join(block, count):
         return jnp.concatenate([block[i * share : (i + 1) * share] for i in range(count)], axis=1).astype(WIDE)
 
     ups = w_up.shape[1] // width
-    small_out = [v[0].astype(WIDE) for v in small_split(late[None, 3 * share :])]
+    small_out = [v[0] for v in small_split(small_sum[None])]
     return (
         out_tokens,
         grad_inputs,
@@ -306,7 +385,7 @@
 def solution(mesh):
     split = P(AXES)
     return jax.shard_map(
-        functools.partial(per_device, mesh.shape["fsdp"] * mesh.shape["dp"]),
+        functools.partial(per_device, dict(mesh.shape)),
         mesh=mesh,
         in_specs=(split,) * 15,
         out_specs=(split,) * 14,

time: 562 us -> 381 us (0.68)
  waiting for transfers between devices: 310 us -> 116 us
  starting transfers between devices: 0.33 us -> 25.7 us
  matrix products: 92.1 us -> 81.4 us
    reduce_scatter x1, waiting for transfers between devices: 144 us -> 28.4 us  [per_device(): early = lax.psum_scatter(early, AXES, scatter_dimension=0, tiled=True)[0]]
    all_gather x1, waiting for transfers between devices: 101 us -> 8.83 us  [per_device(): whole = lax.all_gather(rest, AXES, axis=0, tiled=False)]
    ppermute x0 -> x20, waiting for transfers between devices: none -> 78.5 us  [flipped(): return lax.ppermute(block, name, [(i, i ^ bit) for i in range(sizes[name])])]
    reduce_scatter x1 -> x0, waiting for transfers between devices: 65.1 us -> none  [per_device(): late = lax.psum_scatter(late, AXES, scatter_dimension=0, tiled=True)[0]]
    ppermute x0 -> x20, starting transfers between devices: none -> 25.6 us  [flipped(): return lax.ppermute(block, name, [(i, i ^ bit) for i in range(sizes[name])])]
    dot_general x11, matrix products: 92.1 us -> 81.4 us  [dot(): return lax.dot_general(a, b, dims, preferred_element_type=WIDE)]
    unnamed x64 -> x74, local copies, waits for them, and re-layouts: 21.9 us -> 17.4 us
  transfers between devices with their start and end apart: 3 -> 22, of which waited for: 3 -> 16; matrix products, arithmetic and copies ran while one was open for 9% -> 17% of each run, Pallas kernels for 0% -> 10%
where the time goes in v2:
time: 381 us; the launch traced here: 375 us
  waiting for transfers between devices  116 us (30%)
  matrix products  81.4 us (21%)
  Pallas kernels  56 us (15%)
  local copies, waits for them, and re-layouts  48 us (13%)
  other arithmetic  31.8 us (8%)
  starting transfers between devices  25.7 us (7%)
  between operations  16.2 us (4%)
    dot_general x11, matrix products, dot(): return lax.dot_general(a, b, dims, preferred_element_type=WIDE)  81.4 us
    ppermute x20, waiting for transfers between devices, flipped(): return lax.ppermute(block, name, [(i, i ^ bit) for i in range(sizes[name])])  78.5 us
    reduce_scatter x1, waiting for transfers between devices, per_device(): early = lax.psum_scatter(early, AXES, scatter_dimension=0, tiled=True)[0]  28.4 us
    pallas_call x1, Pallas kernels, attention_back(): pl.pallas_call(functools.partial(attend_back, seq_len, factor), grid=(ima...  27.9 us
    ppermute x20, starting transfers between devices, flipped(): return lax.ppermute(block, name, [(i, i ^ bit) for i in range(sizes[name])])  25.6 us
    pallas_call x1, Pallas kernels, expanded(): pl.pallas_call(functools.partial(expand, step), grid=(full // width,), in...  20.4 us
    unnamed x74, local copies, waits for them, and re-layouts  17.4 us
    all_gather x1, waiting for transfers between devices, per_device(): whole = lax.all_gather(rest, AXES, axis=0, tiled=False)  8.83 us
  transfers between devices with their start and end apart: 22, of which 16 were waited for; matrix products, arithmetic and copies ran while one was open for 17% of the time, Pallas kernels for 10%

profile of v2, /device:TPU:0, one launch (start us, length us, event | category | flops | bytes accessed | tf_op | source)
XLA Modules:
  0.0 374.9 jit_solution(14239335740841485895)
XLA Ops:
  13.0 5.4 %concatenate.51 = bf16[288]{0:T(512)(128)(2,1)S(1)} concatenate(bf16[24]{0:T(256)(128)(2,1)} %param.20, bf16[24]{0:T(256)(128)(2,1)} %param.21, bf16[48]{0:T(256)(128)(2,1)} %param.22, bf16[24]{0:T(256)(128)(2,1)} %param.23, bf16[24]{0:T(256)(128)(2,1)} %param.24, bf16[24]{0:T(256)(128)(2,1)} %param.25, bf16[96]{0:T(256)(128)(2,1)} %param.26, bf16[24]{0:T(256)(128)(2,1)} %param.27), dimensions={0} | concatenate | bytes 1152 | tf_op jit(solution)/shard_map/concatenate | solution.py:282
  19.3 4.1 %collective-permute-start = (bf16[80,768]{1,0:T(8,128)(2,1)S(1)}, bf16[80,768]{1,0:T(8,128)(2,1)S(1)}, u32[]{:S(2)}, u32[]{:S(2)}) collective-permute-start(bf16[80,768]{1,0:T(8,128)(2,1)S(1)} %pad_maximum_fusion.11), channel_id=1, source_target_pairs={{0,16},{4,20},{8,24},{12,28},{16,0},{20,4},{24,8},{28,12},{1,17},{... | collective-permute-start | bytes 368648 | tf_op jit(solution)/shard_map/ppermute | solution.py:184
  23.4 8.6 %collective-permute-done = bf16[80,768]{1,0:T(8,128)(2,1)S(1)} collective-permute-done((bf16[80,768]{1,0:T(8,128)(2,1)S(1)}, bf16[80,768]{1,0:T(8,128)(2,1)S(1)}, u32[]{:S(2)}, u32[]{:S(2)}) %collective-permute-start) | collective-permute-done | bytes 122912 | tf_op jit(solution)/shard_map/ppermute | solution.py:184
  32.0 3.1 collective-permute-start.1
  37.0 5.7 %collective-permute-done.1 = bf16[2,80,768]{2,1,0:T(8,128)(2,1)S(1)} collective-permute-done((bf16[2,80,768]{2,1,0:T(8,128)(2,1)S(1)}, bf16[2,80,768]{2,1,0:T(8,128)(2,1)S(1)}, u32[]{:S(2)}, u32[]{:S(2)}) %collective-permute-start.1) | collective-permute-done | bytes 245792 | tf_op jit(solution)/shard_map/ppermute | solution.py:184
  47.1 8.7 %collective-permute-done.5 = bf16[2,2,80,384]{3,2,1,0:T(8,128)(2,1)S(1)} collective-permute-done((bf16[2,2,80,384]{3,2,1,0:T(8,128)(2,1)S(1)}, bf16[2,2,80,384]{3,2,1,0:T(8,128)(2,1)S(1)}, u32[]{:S(2)}, u32[]{:S(2)}) %collective-permute-start.5) | collective-permute-done | bytes 245792 | tf_op jit(solution)/shard_map/ppermute | solution.py:184
  62.5 9.1 %collective-permute-done.6 = bf16[2,2,2,80,384]{4,3,1,0,2:T(8,128)(2,1)S(1)} collective-permute-done((bf16[2,2,2,80,384]{4,3,1,0,2:T(8,128)(2,1)}, bf16[2,2,2,80,384]{4,3,1,0,2:T(8,128)(2,1)S(1)}, u32[]{:S(2)}, u32[]{:S(2)}) %collective-permute-start.6) | collective-permute-done | bytes 491552 | tf_op jit(solution)/shard_map/ppermute | solution.py:184
  88.3 5.1 %fusion = bf16[1248,2304]{1,0:T(8,128)(2,1)S(1)} fusion(bf16[768,2304]{1,0:T(8,128)(2,1)S(1)} %constant_dynamic-update-slice_fusion, f32[2304]{0:T(1024)S(1)} %pad_maximum_fusion.13, f32[1248,768]{1,0:T(8,128)S(1)} %copy-done.11, f32[768]{0:T(1024)S(1)} %reshape.388, f32[768]{0:T(1024)S(1)} %reshape.387), kind=kOutput, calls=%fused_computation.4 | convolution fusion | flops 4425228288 | bytes 13138944 | tf_op jit(solution)/shard_map/dot_general | solution.py:22
  93.4 7.8 %shard_map.254 = bf16[6,208,768]{2,1,0:T(8,128)(2,1)S(1)} custom-call(bf16[6,208,2304]{2,1,0:T(8,128)(2,1)S(1)} %bitcast.206), custom_call_target="tpu_custom_call" | custom-call | tf_op jit(solution)/shard_map/pallas_call | solution.py:93
  103.6 8.8 %all-gather.3.cloned.1.call-done = bf16[6912,768]{1,0:T(8,128)(2,1)} async-done(((bf16[216,768]{1,0:T(8,128)(2,1)}), bf16[6912,768]{1,0:T(8,128)(2,1)}) %all-gather.3.cloned.1.call-update) | async-done | bytes 10616848 | tf_op jit(solution)/shard_map/all_gather | solution.py:302
  112.4 4.9 %slice.321 = bf16[32,96,768]{2,1,0:T(8,128)(2,1)} slice(bf16[32,216,768]{2,1,0:T(8,128)(2,1)} %bitcast.214), slice={[0:32], [120:216], [0:768]} | slice | bytes 9437184 | tf_op jit(solution)/shard_map/slice | solution.py:309
  117.3 3.2 fusion.36
  124.9 20.4 %shard_map.255 = (bf16[1248,3072]{1,0:T(8,128)(2,1)S(1)}, bf16[1248,3072]{1,0:T(8,128)(2,1)}) custom-call(bf16[1248,768]{1,0:T(8,128)(2,1)S(1)} %add_convert_fusion.1.rows_ref, bf16[768,3072]{1,0:T(8,128)(2,1)S(1)} %pad_maximum_fusion.weight_ref, f32[1,3072]{1,0:T(1,128)S(1)} %reshape.392.shift_ref), custom_call_target="tpu_custom_call" | custom-call | flops 5888802816 | bytes 23003136 | tf_op jit(solution)/shard_map/pallas_call | solution.py:144
  145.3 8.6 %fusion.2 = bf16[1248,768]{1,0:T(8,128)(2,1)S(1)} fusion(f32[1248,768]{1,0:T(8,128)S(1)} %get-tuple-element.100, bf16[1248,3072]{1,0:T(8,128)(2,1)S(1)} %get-tuple-element.16, bf16[3072,768]{1,0:T(8,128)(2,1)} %bitcast.237, f32[768]{0:T(1024)S(1)} %reshape.393), kind=kOutput, calls=%fused_computation.12 | convolution fusion | flops 5891678208 | bytes 18140160 | tf_op jit(solution)/shard_map/dot_general | solution.py:22
  156.2 8.1 %convolution_convert_fusion = bf16[3072,768]{1,0:T(8,128)(2,1)} fusion(bf16[1248,3072]{1,0:T(8,128)(2,1)S(1)} %get-tuple-element.16, bf16[1248,768]{1,0:T(8,128)(2,1)S(1)} %bitcast.216), kind=kOutput, calls=%fused_computation.6 | convolution fusion | flops 5891162112 | bytes 14303232 | tf_op jit(solution)/shard_map/dot_general | solution.py:22
  164.4 12.0 %convert_reduce_fusion = (f32[3072]{0:T(1024)S(1)}, bf16[1248,3072]{1,0:T(8,128)(2,1)}) fusion(bf16[1248,3072]{1,0:T(8,128)(2,1)} %get-tuple-element.17, bf16[1248,768]{1,0:T(8,128)(2,1)S(1)} %bitcast.217, bf16[3072,768]{1,0:T(8,128)(2,1)} %bitcast.238), kind=kOutput, calls=%fused_computation | convolution fusion | flops 5907969024 | bytes 21983232 | tf_op jit(solution)/shard_map/dot_general | solution.py:22
  176.4 12.2 %multiply_reduce_fusion = (f32[768]{0:T(1024)S(1)}, f32[1248]{0:T(1024)S(1)}, f32[1248]{0:T(1024)S(1)}, f32[768]{0:T(1024)S(1)}, f32[1248,768]{1,0:T(8,128)}) fusion(f32[1248,768]{1,0:T(8,128)S(1)} %get-tuple-element.100, f32[1248]{0:T(1024)S(1)} %add_rsqrt_fusion, f32[1248]{0:T(1024)S(1)} %broadcast_multiply_fusion.4, f32[768]{0:T(1024)S(1)} %reshape.390, ...), kind=kOutput, calls=%fused_computation.16 | convolution fusion | flops 5916299264 | bytes 20083200 | tf_op jit(solution)/shard_map/dot_general | solution.py:22
  188.6 9.9 %convolution_convert_fusion.1 = bf16[768,3072]{1,0:T(8,128)(2,1)S(1)} fusion(bf16[1248,768]{1,0:T(8,128)(2,1)S(1)} %add_convert_fusion.1.rows_ref, bf16[1248,3072]{1,0:T(8,128)(2,1)} %get-tuple-element.104), kind=kOutput, calls=%fused_computation.7 | convolution fusion | flops 5891162112 | bytes 14303232 | tf_op jit(solution)/shard_map/dot_general | solution.py:22
  198.6 3.2 convert_reduce_fusion.3
  201.8 3.8 %convolution_convert_fusion.3 = bf16[768,768]{1,0:T(8,128)(2,1)S(1)} fusion(bf16[1248,768]{1,0:T(8,128)(2,1)S(1)} %bitcast.212, f32[1248,768]{1,0:T(8,128)} %get-tuple-element.29), kind=kOutput, calls=%fused_computation.49 | convolution fusion | flops 1473748992 | bytes 6930432 | tf_op jit(solution)/shard_map/dot_general | solution.py:22
  216.5 4.5 %convolution_convert_fusion.2 = bf16[1248,768]{1,0:T(8,128)(2,1)S(1)} fusion(bf16[768,768]{1,0:T(8,128)(2,1)} %bitcast.250, f32[1248,768]{1,0:T(8,128)} %get-tuple-element.29), kind=kOutput, calls=%fused_computation.35 | convolution fusion | flops 1474117632 | bytes 6930432 | tf_op jit(solution)/shard_map/dot_general | solution.py:22
  221.1 27.9 %shard_map.256 = bf16[6,208,2304]{2,1,0:T(8,128)(2,1)S(1)} custom-call(bf16[6,208,2304]{2,1,0:T(8,128)(2,1)S(1)} %bitcast.209, bf16[6,208,768]{2,1,0:T(8,128)(2,1)S(1)} %bitcast.210), custom_call_target="tpu_custom_call" | custom-call | tf_op jit(solution)/shard_map/pallas_call | solution.py:105
  249.0 7.2 %fusion.35 = (f32[768]{0:T(1024)S(1)}, f32[768]{0:T(1024)S(1)}, f32[1248]{0:T(1024)S(1)}, f32[1248]{0:T(1024)S(1)}, f32[1248,768]{1,0:T(8,128)}) fusion(f32[1248]{0:T(1024)S(1)} %rsqrt.23, f32[1248]{0:T(1024)S(1)} %div.31, bf16[6,197,768]{2,1,0:T(8,128)(2,1)S(1)} %copy-done.3, f32[1248,768]{1,0:T(8,128)S(1)} %copy-done.12, f32[768]{0:T(1024)S(1)} %reshape.387, ...), kind=kOutput, calls=%fused_computation.179 | convolution fusion | flops 4426182656 | bytes 18802176 | tf_op jit(solution)/shard_map/dot_general | solution.py:22
  256.3 3.5 convert_reduce_fusion.1
  260.9 8.0 %bitcast_convert_fusion = bf16[768,2304]{1,0:T(8,128)(2,1)S(1)} fusion(bf16[6,208,2304]{2,1,0:T(8,128)(2,1)} %copy-done, f32[768]{0:T(1024)S(1)} %reshape.388, f32[768]{0:T(1024)S(1)} %reshape.387, f32[6,208]{1,0:T(8,128)S(1)} %copy-done.23, f32[6,208]{1,0:T(8,128)S(1)} %copy-done.21, bf16[6,197,768]{2,1,0:T(8,128)(2,1)S(1)} %copy-done.3), kind=kOutput, calls=%fused_computation.5 | convolution fusion | flops 4424122368 | bytes 11121408 | tf_op jit(solution)/shard_map/dot_general | solution.py:22
  279.2 3.3 multiply_add_fusion
  292.4 11.3 %collective-permute-done.9 = bf16[2,2,2,72,384]{4,3,0,1,2:T(8,128)(2,1)S(1)} collective-permute-done((bf16[2,2,2,72,384]{4,3,0,1,2:T(8,128)(2,1)S(1)}, bf16[2,2,2,72,384]{4,3,0,1,2:T(8,128)(2,1)S(1)}, u32[]{:S(2)}, u32[]{:S(2)}) %collective-permute-start.9) | collective-permute-done | bytes 442400 | tf_op jit(solution)/shard_map/ppermute | solution.py:184
  305.2 6.7 %collective-permute-done.11 = bf16[2,2,2,72,384]{4,3,0,1,2:T(8,128)(2,1)S(1)} collective-permute-done((bf16[2,2,2,72,384]{4,3,0,1,2:T(8,128)(2,1)S(1)}, bf16[2,2,2,72,384]{4,3,0,1,2:T(8,128)(2,1)S(1)}, u32[]{:S(2)}, u32[]{:S(2)}) %collective-permute-start.11) | collective-permute-done | bytes 442400 | tf_op jit(solution)/shard_map/ppermute | solution.py:184
  314.5 3.6 collective-permute-done.12
  318.8 6.2 %collective-permute-done.13 = bf16[2,72,768]{2,1,0:T(8,128)(2,1)S(1)} collective-permute-done((bf16[2,72,768]{2,1,0:T(8,128)(2,1)S(1)}, bf16[2,72,768]{2,1,0:T(8,128)(2,1)S(1)}, u32[]{:S(2)}, u32[]{:S(2)}) %collective-permute-start.13) | collective-permute-done | bytes 221216 | tf_op jit(solution)/shard_map/ppermute | solution.py:184
  325.8 8.8 %collective-permute-done.14 = bf16[72,768]{1,0:T(8,128)(2,1)S(1)} collective-permute-done((bf16[72,768]{1,0:T(8,128)(2,1)S(1)}, bf16[72,768]{1,0:T(8,128)(2,1)S(1)}, u32[]{:S(2)}, u32[]{:S(2)}) %collective-permute-start.14) | collective-permute-done | bytes 110624 | tf_op jit(solution)/shard_map/ppermute | solution.py:184
  335.3 28.4 %reduce-scatter.2.cloned.1.call-done = bf16[1,216,768]{2,1,0:T(8,128)(2,1)} async-done(((bf16[32,216,768]{2,1,0:T(8,128)(2,1)}), bf16[1,216,768]{2,1,0:T(8,128)(2,1)}) %reduce-scatter.2.cloned.1.call-update) | async-done | bytes 331792 | tf_op jit(solution)/shard_map/reduce_scatter | solution.py:346
  (223 shorter events, 86.6 us)
Async XLA Ops:
  7.2 37.6 %copy-start.2 = (bf16[6,197,768]{2,1,0:T(8,128)(2,1)S(1)}, bf16[6,197,768]{2,1,0:T(8,128)(2,1)}, u32[]{:S(2)}) copy-start(bf16[6,197,768]{2,1,0:T(8,128)(2,1)} %param.15) | copy-start | bytes 5446660
  7.2 105.2 %all-gather.3.cloned.1.call-start = ((), (), s32[]{:S(2)}) async-start(), calls=%async_computation.2 | async-start | bytes 10948608 | tf_op jit(solution)/shard_map/all_gather | solution.py:302
  12.9 350.8 %reduce-scatter.2.cloned.1.call-start = ((), (), s32[]{:S(2)}) async-start(), calls=%async_computation.1 | async-start | bytes 10948608 | tf_op jit(solution)/shard_map/reduce_scatter | solution.py:346
  19.3 12.7 %collective-permute-start = (bf16[80,768]{1,0:T(8,128)(2,1)S(1)}, bf16[80,768]{1,0:T(8,128)(2,1)S(1)}, u32[]{:S(2)}, u32[]{:S(2)}) collective-permute-start(bf16[80,768]{1,0:T(8,128)(2,1)S(1)} %pad_maximum_fusion.11), channel_id=1, source_target_pairs={{0,16},{4,20},{8,24},{12,28},{16,0},{20,4},{24,8},{28,12},{1,17},{... | collective-permute-start | bytes 368648 | tf_op jit(solution)/shard_map/ppermute | solution.py:184
  32.0 10.7 %collective-permute-start.1 = (bf16[2,80,768]{2,1,0:T(8,128)(2,1)S(1)}, bf16[2,80,768]{2,1,0:T(8,128)(2,1)S(1)}, u32[]{:S(2)}, u32[]{:S(2)}) collective-permute-start(bf16[2,80,768]{2,1,0:T(8,128)(2,1)S(1)} %pad_maximum_fusion.9), channel_id=1, source_target_pairs={{0,8},{4,12},{8,0},{12,4},{16,24},{20,28},{24,16},{28,20},{1,9},{5... | collective-permute-start | bytes 737288 | tf_op jit(solution)/shard_map/ppermute | solution.py:184
  37.0 23.6 %copy-start.20 = (f32[6,208]{1,0:T(8,128)}, f32[6,208]{1,0:T(8,128)S(1)}, u32[]{:S(2)}) copy-start(f32[6,208]{1,0:T(8,128)S(1)} %broadcast_multiply_fusion.5) | copy-start | bytes 14980
  42.8 12.9 %collective-permute-start.5 = (bf16[2,2,80,384]{3,2,1,0:T(8,128)(2,1)S(1)}, bf16[2,2,80,384]{3,2,1,0:T(8,128)(2,1)S(1)}, u32[]{:S(2)}, u32[]{:S(2)}) collective-permute-start(bf16[2,2,80,384]{3,2,1,0:T(8,128)(2,1)S(1)} %get-tuple-element.62), channel_id=1, source_target_pairs={{0,2},{1,3},{2,0},{3,1},{4,6},{5,7},{6,4},{7,5},{8,10},{9,11},{10,... | collective-permute-start | bytes 737288 | tf_op jit(solution)/shard_map/ppermute | solution.py:184
  45.5 15.8 %copy-start.22 = (f32[6,208]{1,0:T(8,128)}, f32[6,208]{1,0:T(8,128)S(1)}, u32[]{:S(2)}) copy-start(f32[6,208]{1,0:T(8,128)S(1)} %add_rsqrt_fusion.1) | copy-start | bytes 14980
  45.5 15.9 %collective-permute-start.2 = (bf16[2,2,80,384]{3,2,1,0:T(8,128)(2,1)S(1)}, bf16[2,2,80,384]{3,2,1,0:T(8,128)(2,1)S(1)}, u32[]{:S(2)}, u32[]{:S(2)}) collective-permute-start(bf16[2,2,80,384]{3,2,1,0:T(8,128)(2,1)S(1)} %get-tuple-element.63), channel_id=1, source_target_pairs={{0,4},{4,0},{8,12},{12,8},{16,20},{20,16},{24,28},{28,24},{1,5},{5... | collective-permute-start | bytes 737288 | tf_op jit(solution)/shard_map/ppermute | solution.py:184
  56.6 14.9 %collective-permute-start.6 = (bf16[2,2,2,80,384]{4,3,1,0,2:T(8,128)(2,1)}, bf16[2,2,2,80,384]{4,3,1,0,2:T(8,128)(2,1)S(1)}, u32[]{:S(2)}, u32[]{:S(2)}) collective-permute-start(bf16[2,2,2,80,384]{4,3,1,0,2:T(8,128)(2,1)} %pad_maximum_fusion.7), channel_id=1, source_target_pairs={{0,4},{4,0},{8,12},{12,8},{16,20},{20,16},{24,28},{28,24},{1,5},{5... | collective-permute-start | bytes 1474568 | tf_op jit(solution)/shard_map/ppermute | solution.py:184
  61.6 12.6 %collective-permute-start.3 = (bf16[2,2,2,80,384]{4,3,2,1,0:T(8,128)(2,1)S(1)}, bf16[2,2,2,80,384]{4,3,2,1,0:T(8,128)(2,1)S(1)}, u32[]{:S(2)}, u32[]{:S(2)}) collective-permute-start(bf16[2,2,2,80,384]{4,3,2,1,0:T(8,128)(2,1)S(1)} %pad_maximum_fusion.6), channel_id=1, source_target_pairs={{0,2},{1,3},{2,0},{3,1},{4,6},{5,7},{6,4},{7,5},{8,10},{9,11},{10,... | collective-permute-start | bytes 1474568 | tf_op jit(solution)/shard_map/ppermute | solution.py:184
  71.8 5.3 %collective-permute-start.7 = (bf16[2,2,2,2,80,384]{5,4,1,0,3,2:T(8,128)(2,1)S(1)}, bf16[2,2,2,2,80,384]{5,4,1,0,3,2:T(8,128)(2,1)S(1)}, u32[]{:S(2)}, u32[]{:S(2)}) collective-permute-start(bf16[2,2,2,2,80,384]{5,4,1,0,3,2:T(8,128)(2,1)S(1)} %pad_maximum_fusion.5), channel_id=1, source_target_pairs={{0,1},{1,0},{2,3},{3,2},{4,5},{5,4},{6,7},{7,6},{8,9},{9,8},{10,11... | collective-permute-start | bytes 2949128 | tf_op jit(solution)/shard_map/ppermute | solution.py:184
  74.4 4.7 %collective-permute-start.4 = (bf16[2,2,2,2,80,384]{5,4,3,2,1,0:T(8,128)(2,1)S(1)}, bf16[2,2,2,2,80,384]{5,4,3,2,1,0:T(8,128)(2,1)S(1)}, u32[]{:S(2)}, u32[]{:S(2)}) collective-permute-start(bf16[2,2,2,2,80,384]{5,4,3,2,1,0:T(8,128)(2,1)S(1)} %pad_maximum_fusion.4), channel_id=1, source_target_pairs={{0,1},{1,0},{2,3},{3,2},{4,5},{5,4},{6,7},{7,6},{8,9},{9,8},{10,11... | collective-permute-start | bytes 2949128 | tf_op jit(solution)/shard_map/ppermute | solution.py:184
  164.4 12.0 %copy-start.7 = (bf16[32,24,768]{2,1,0:T(8,128)(2,1)S(1)}, bf16[32,24,768]{2,1,0:T(8,128)(2,1)}, u32[]{:S(2)}) copy-start(bf16[32,24,768]{2,1,0:T(8,128)(2,1)} %copy-done.6) | copy-start | bytes 3538948
  164.4 12.1 %copy-start.9 = (bf16[32,24,768]{2,1,0:T(8,128)(2,1)S(1)}, bf16[32,24,768]{2,1,0:T(8,128)(2,1)}, u32[]{:S(2)}) copy-start(bf16[32,24,768]{2,1,0:T(8,128)(2,1)} %copy-done.8) | copy-start | bytes 3538948
  188.6 9.9 %copy-start.10 = (f32[1248,768]{1,0:T(8,128)S(1)}, f32[1248,768]{1,0:T(8,128)}, u32[]{:S(2)}) copy-start(f32[1248,768]{1,0:T(8,128)} %get-tuple-element.101) | copy-start | bytes 11501572
  221.0 27.9 %copy-start.3 = (bf16[6,197,768]{2,1,0:T(8,128)(2,1)S(1)}, bf16[6,197,768]{2,1,0:T(8,128)(2,1)}, u32[]{:S(2)}) copy-start(bf16[6,197,768]{2,1,0:T(8,128)(2,1)} %param.15) | copy-start | bytes 5446660
  221.0 27.9 %copy-start.12 = (f32[1248,768]{1,0:T(8,128)S(1)}, f32[1248,768]{1,0:T(8,128)}, u32[]{:S(2)}) copy-start(f32[1248,768]{1,0:T(8,128)} %fusion.3) | copy-start | bytes 11501572
  221.0 27.9 %copy-start.19 = (bf16[768,2304]{1,0:T(8,128)(2,1)S(1)}, bf16[768,2304]{1,0:T(8,128)(2,1)}, u32[]{:S(2)}) copy-start(bf16[768,2304]{1,0:T(8,128)(2,1)} %copy-done.18) | copy-start | bytes 10616836
  260.6 8.8 %collective-permute-start.15 = (f32[2,2,2,2,1,768]{5,4,3,2,1,0:T(1,128)S(1)}, f32[2,2,2,2,1,768]{5,4,3,2,1,0:T(1,128)S(1)}, u32[]{:S(2)}, u32[]{:S(2)}) collective-permute-start(f32[2,2,2,2,1,768]{5,4,3,2,1,0:T(1,128)S(1)} %dynamic-slice_bitcast_fusion.5), channel_id=1, source_target_pairs={{0,1},{1,0},{2,3},{3,2},{4,5},{5,4},{6,7},{7,6},{8,9},{9,8},{10,11... | collective-permute-start | bytes 147464 | tf_op jit(solution)/shard_map/ppermute | solution.py:184
  269.5 9.6 %copy-start.14 = (f32[1248,768]{1,0:T(8,128)S(1)}, f32[1248,768]{1,0:T(8,128)}, u32[]{:S(2)}) copy-start(f32[1248,768]{1,0:T(8,128)} %get-tuple-element.102) | copy-start | bytes 11501572
  269.6 4.4 %collective-permute-start.16 = (f32[2,2,2,1,768]{4,3,2,1,0:T(1,128)S(1)}, f32[2,2,2,1,768]{4,3,2,1,0:T(1,128)S(1)}, u32[]{:S(2)}, u32[]{:S(2)}) collective-permute-start(f32[2,2,2,1,768]{4,3,2,1,0:T(1,128)S(1)} %dynamic-slice_bitcast_fusion.6), channel_id=1, source_target_pairs={{0,2},{1,3},{2,0},{3,1},{4,6},{5,7},{6,4},{7,5},{8,10},{9,11},{10,... | collective-permute-start | bytes 73736 | tf_op jit(solution)/shard_map/ppermute | solution.py:184
  271.5 14.3 %collective-permute-start.8 = (bf16[2,2,2,2,72,768]{5,4,0,1,3,2:T(8,128)(2,1)S(1)}, bf16[2,2,2,2,72,768]{5,4,0,1,3,2:T(8,128)(2,1)S(1)}, u32[]{:S(2)}, u32[]{:S(2)}) collective-permute-start(bf16[2,2,2,2,72,768]{5,4,0,1,3,2:T(8,128)(2,1)S(1)} %bitcast.248), channel_id=1, source_target_pairs={{0,1},{1,0},{2,3},{3,2},{4,5},{5,4},{6,7},{7,6},{8,9},{9,8},{10,11... | collective-permute-start | bytes 5308424 | tf_op jit(solution)/shard_map/ppermute | solution.py:184
  274.0 3.8 %collective-permute-start.17 = (f32[2,2,1,768]{3,2,1,0:T(1,128)S(1)}, f32[2,2,1,768]{3,2,1,0:T(1,128)S(1)}, u32[]{:S(2)}, u32[]{:S(2)}) collective-permute-start(f32[2,2,1,768]{3,2,1,0:T(1,128)S(1)} %dynamic-slice_bitcast_fusion.7), channel_id=1, source_target_pairs={{0,4},{4,0},{8,12},{12,8},{16,20},{20,16},{24,28},{28,24},{1,5},{5... | collective-permute-start | bytes 36872 | tf_op jit(solution)/shard_map/ppermute | solution.py:184
  277.8 6.7 %collective-permute-start.18 = (f32[2,1,768]{2,1,0:T(1,128)S(1)}, f32[2,1,768]{2,1,0:T(1,128)S(1)}, u32[]{:S(2)}, u32[]{:S(2)}) collective-permute-start(f32[2,1,768]{2,1,0:T(1,128)S(1)} %fusion.27), channel_id=1, source_target_pairs={{0,8},{4,12},{8,0},{12,4},{16,24},{20,28},{24,16},{28,20},{1,9},{5... | collective-permute-start | bytes 18440 | tf_op jit(solution)/shard_map/ppermute | solution.py:184
  284.5 5.7 %collective-permute-start.19 = (f32[1,768]{1,0:T(1,128)S(1)}, f32[1,768]{1,0:T(1,128)S(1)}, u32[]{:S(2)}, u32[]{:S(2)}) collective-permute-start(f32[1,768]{1,0:T(1,128)S(1)} %fusion.30), channel_id=1, source_target_pairs={{0,16},{4,20},{8,24},{12,28},{16,0},{20,4},{24,8},{28,12},{1,17},{... | collective-permute-start | bytes 9224 | tf_op jit(solution)/shard_map/ppermute | solution.py:184
  286.6 17.2 %collective-permute-start.9 = (bf16[2,2,2,72,384]{4,3,0,1,2:T(8,128)(2,1)S(1)}, bf16[2,2,2,72,384]{4,3,0,1,2:T(8,128)(2,1)S(1)}, u32[]{:S(2)}, u32[]{:S(2)}) collective-permute-start(bf16[2,2,2,72,384]{4,3,0,1,2:T(8,128)(2,1)S(1)} %dynamic-slice_bitcast_fusion.1), channel_id=1, source_target_pairs={{0,2},{1,3},{2,0},{3,1},{4,6},{5,7},{6,4},{7,5},{8,10},{9,11},{10,... | collective-permute-start | bytes 1327112 | tf_op jit(solution)/shard_map/ppermute | solution.py:184
  290.3 21.6 %collective-permute-start.11 = (bf16[2,2,2,72,384]{4,3,0,1,2:T(8,128)(2,1)S(1)}, bf16[2,2,2,72,384]{4,3,0,1,2:T(8,128)(2,1)S(1)}, u32[]{:S(2)}, u32[]{:S(2)}) collective-permute-start(bf16[2,2,2,72,384]{4,3,0,1,2:T(8,128)(2,1)S(1)} %dynamic-slice_bitcast_fusion), channel_id=1, source_target_pairs={{0,4},{4,0},{8,12},{12,8},{16,20},{20,16},{24,28},{28,24},{1,5},{5... | collective-permute-start | bytes 1327112 | tf_op jit(solution)/shard_map/ppermute | solution.py:184
  304.0 10.4 %collective-permute-start.10 = (bf16[2,2,72,384]{3,2,0,1:T(8,128)(2,1)S(1)}, bf16[2,2,72,384]{3,2,0,1:T(8,128)(2,1)S(1)}, u32[]{:S(2)}, u32[]{:S(2)}) collective-permute-start(bf16[2,2,72,384]{3,2,0,1:T(8,128)(2,1)S(1)} %dynamic-slice_bitcast_fusion.3), channel_id=1, source_target_pairs={{0,4},{4,0},{8,12},{12,8},{16,20},{20,16},{24,28},{28,24},{1,5},{5... | collective-permute-start | bytes 663560 | tf_op jit(solution)/shard_map/ppermute | solution.py:184
  312.1 6.0 %collective-permute-start.12 = (bf16[2,2,72,384]{3,2,0,1:T(8,128)(2,1)S(1)}, bf16[2,2,72,384]{3,2,0,1:T(8,128)(2,1)S(1)}, u32[]{:S(2)}, u32[]{:S(2)}) collective-permute-start(bf16[2,2,72,384]{3,2,0,1:T(8,128)(2,1)S(1)} %dynamic-slice_bitcast_fusion.2), channel_id=1, source_target_pairs={{0,2},{1,3},{2,0},{3,1},{4,6},{5,7},{6,4},{7,5},{8,10},{9,11},{10,... | collective-permute-start | bytes 663560 | tf_op jit(solution)/shard_map/ppermute | solution.py:184
  318.2 6.9 %collective-permute-start.13 = (bf16[2,72,768]{2,1,0:T(8,128)(2,1)S(1)}, bf16[2,72,768]{2,1,0:T(8,128)(2,1)S(1)}, u32[]{:S(2)}, u32[]{:S(2)}) collective-permute-start(bf16[2,72,768]{2,1,0:T(8,128)(2,1)S(1)} %fusion.20), channel_id=1, source_target_pairs={{0,8},{4,12},{8,0},{12,4},{16,24},{20,28},{24,16},{28,20},{1,9},{5... | collective-permute-start | bytes 663560 | tf_op jit(solution)/shard_map/ppermute | solution.py:184
  325.1 9.5 %collective-permute-start.14 = (bf16[72,768]{1,0:T(8,128)(2,1)S(1)}, bf16[72,768]{1,0:T(8,128)(2,1)S(1)}, u32[]{:S(2)}, u32[]{:S(2)}) collective-permute-start(bf16[72,768]{1,0:T(8,128)(2,1)S(1)} %dynamic-slice_bitcast_fusion.4), channel_id=1, source_target_pairs={{0,16},{4,20},{8,24},{12,28},{16,0},{20,4},{24,8},{28,12},{1,17},{... | collective-permute-start | bytes 331784 | tf_op jit(solution)/shard_map/ppermute | solution.py:184
  (18 other events, 82.2 us)
Sparse Core Ops, SparseCore 0:
  13.0 99.3 all-gather.2
  214.4 149.2 reduce-scatter.1

commit v3 on v2

--- a/solution.py
+++ b/solution.py
@@ -46,7 +46,8 @@
         out_ref[0, :, at : at + 128] = jnp.where(lane < 64, halves[0], halves[1]).astype(jnp.bfloat16)
 
 
-def attend_back(seq_len, factor, proj_ref, back_ref, out_ref):
+def attend_back(seq_len, factor, proj_ref, back_ref, *refs):
+    out_ref = refs[-1]
     rows, model_width = back_ref.shape[1:]
     lane = lax.broadcasted_iota(jnp.int32, (1, 128), 1)
     key_at = lax.broadcasted_iota(jnp.int32, (rows, 1), 0)
@@ -100,16 +101,27 @@
     )(projected)
 
 
-def attention_back(projected, back_head, seq_len, factor):
+def attention_back(projected, back_head, seq_len, factor, group):
     images, rows, wide = projected.shape
-    return pl.pallas_call(
-        functools.partial(attend_back, seq_len, factor),
-        grid=(images,),
-        in_specs=[whole((rows, wide)), whole((rows, wide // 3))],
-        out_specs=whole((rows, wide)),
-        out_shape=jax.ShapeDtypeStruct((images, rows, wide), jnp.bfloat16),
-        compiler_params=pltpu.CompilerParams(vmem_limit_bytes=40 << 20),
-    )(projected, back_head)
+    done = None
+    for start in range(0, images, group):
+        def block(shape, start=start):
+            return pl.BlockSpec((1,) + shape, lambda i: (i + start, 0, 0))
+
+        kept = () if done is None else (done,)
+        done = pl.pallas_call(
+            functools.partial(attend_back, seq_len, factor),
+            grid=(min(group, images - start),),
+            in_specs=[block((rows, wide)), block((rows, wide // 3))] + [pl.BlockSpec(memory_space=pl.ANY)] * len(kept),
+            out_specs=block((rows, wide)),
+            out_shape=jax.ShapeDtypeStruct((images, rows, wide), jnp.bfloat16),
+            input_output_aliases={2: 0} if kept else {},
+            compiler_params=pltpu.CompilerParams(vmem_limit_bytes=40 << 20),
+            cost_estimate=pl.CostEstimate(
+                flops=group * HEADS * 10 * rows * rows * 256, bytes_accessed=14 * group * rows * wide, transcendentals=0
+            ),
+        )(projected, back_head, *kept)
+    return done
 
 
 TERMS = (0.254829592, -0.284496736, 1.421413741, -1.453152027, 1.061405429)
@@ -138,7 +150,7 @@
 
 def expanded(rows, weight, shift, step, width=512):
     count, depth = rows.shape
-    full = weight.shape[1]
+    full = shift.shape[1]
     out = jax.ShapeDtypeStruct((count, full), LOW)
     spec = pl.BlockSpec((count, width), lambda j: (0, j))
     return pl.pallas_call(
@@ -218,23 +230,31 @@
     return block, left
 
 
-def gathered(block, sizes):
+def gathered(block, half, sizes):
     order = places(sizes)
     far, one_way, other_way, core = routes(sizes)
     block, done = gather_by(block, far, [], order, sizes)
-    half = block.shape[-1] // 2
     parts = []
     for part, way in ((block[..., :half], one_way), (block[..., half:], other_way)):
         part, _ = gather_by(part, way + core, done, order, sizes)
-        parts.append(part.reshape((-1,) + part.shape[-2:]))
+        parts.append(part.reshape(-1, part.shape[-1]))
     return parts
 
 
-def scattered(blocks, sizes):
+def scattered(arrays, sizes):
     order = places(sizes)
     far, one_way, other_way, core = routes(sizes)
-    blocks = blocks.reshape((2,) * len(order) + blocks.shape[1:])
-    blocks, left = scatter_by(blocks, core, order, sizes)
+    bit = is_set(*core[0]).astype(jnp.int32)
+
+    def half_of(at):
+        cut = [a.reshape((-1, 2, a.shape[0] // (1 << len(order)), a.shape[1])) for a in arrays]
+        cut = [lax.dynamic_index_in_dim(a, at, 1, keepdims=False) for a in cut]
+        return jnp.concatenate(cut, axis=-1)
+
+    got = flipped(half_of(1 - bit), *core[0], sizes)
+    blocks = (half_of(bit).astype(WIDE) + got.astype(WIDE)).astype(LOW)
+    left = order[:-1]
+    blocks = blocks.reshape((2,) * len(left) + blocks.shape[1:])
     half = blocks.shape[-1] // 2
     one, rest = scatter_by(blocks[..., :half], one_way[::-1], left, sizes)
     two, rest = scatter_by(blocks[..., half:], other_way[::-1], left, sizes)
@@ -275,46 +295,38 @@
     small = (norm1_scale, norm1_offset, qv_bias, out_bias, norm2_scale, norm2_offset, up_bias, down_bias)
     small_sizes = [v.shape[0] for v in small]
 
-    def columns(matrix):
-        return [matrix[:, at : at + width] for at in range(0, matrix.shape[1], width)]
-
-    def small_rows(parts):
-        flat = jnp.concatenate(parts, axis=-1)
-        return jnp.pad(flat, [(0, 0)] * (flat.ndim - 1) + [(0, 8 * width - flat.shape[-1])]).reshape(
-            flat.shape[:-1] + (8, width)
-        )
-
-    def small_split(block):
-        flat, at, parts = block.reshape(block.shape[0], -1), 0, []
+    side = -(-sum(small_sizes) // 128)
+
+    def small_split(flat):
+        at, parts = 0, []
         for size in small_sizes:
             parts.append(flat[:, at : at + size])
             at += size
         return parts
 
-    first = jnp.concatenate([*columns(w_qkv), small_rows(small)], axis=0)
-    first_left, first_right = gathered(first, sizes)
-    qkv_parts = []
-    for i in range(3):
-        for part in (first_left, first_right):
-            qkv_parts.append(part[:, i * share : (i + 1) * share].reshape(width, width // 2))
-    full_qkv = jnp.concatenate(qkv_parts, axis=1)
-    rest = jnp.concatenate([w_out, *columns(w_up), w_down], axis=0)
-    whole = lax.all_gather(rest, AXES, axis=0, tiled=False)
-    at = 0
-
-    def take(count, size=share):
-        nonlocal at
-        parts = []
-        for _ in range(count):
-            parts.append(whole[:, at : at + size].reshape(devices * size, width))
+    def small_join(parts):
+        total, at = 0, 0
+        for part in parts:
+            size = part.shape[-1]
+            ends = [(0, 0)] * (part.ndim - 1) + [(at, side * 128 - at - size)]
+            total = total + jnp.pad(part, ends)
             at += size
-        return parts[0] if count == 1 else jnp.concatenate(parts, axis=1)
-
-    full_out = take(1)
-    full_up = take(w_up.shape[1] // width)
-    full_down = take(1, w_down.shape[0])
-    vectors = [v.reshape(-1).astype(WIDE) for v in small_split(first_left[:, 3 * share :])]
+        return total
+
+    first = [w_qkv, jnp.pad(small_join(small).reshape(side, 128), ((0, share - side), (0, 0)))]
+    left, right = gathered(jnp.concatenate(first, axis=1), 3 * width // 2, sizes)
+    full_qkv = jnp.concatenate([left, right[:, : 3 * width // 2]], axis=1)
+    small_whole = right[:, 3 * width // 2 :].reshape(devices, share, 128)[:, :side].reshape(devices, -1)
+    vectors = [v.reshape(-1).astype(WIDE) for v in small_split(small_whole)]
     scale_one, offset_one, qv_full, out_shift, scale_two, offset_two, up_shift, down_shift = vectors
+    hidden_width = w_up.shape[1]
+    ratio = hidden_width // width
+    rest = [w_up, w_out, *[w_down[i * share : (i + 1) * share] for i in range(ratio)]]
+    whole = lax.all_gather(jnp.concatenate(rest, axis=1), AXES, axis=0, tiled=True)
+    full_up = whole[:, :hidden_width]
+    full_out = whole[:, hidden_width : hidden_width + width]
+    full_down = whole[:, hidden_width + width :].reshape(devices, share, ratio, width)
+    full_down = full_down.swapaxes(1, 2).reshape(hidden_width, width)
 
     def padded(array):
         return jnp.pad(array, ((0, 0), (0, rows - seq_len), (0, 0))).reshape(row_count, width)
@@ -329,25 +341,28 @@
     head_out = attention(projected, seq_len, factor).reshape(row_count, width)
     middle = inputs + dot(head_out, full_out) + out_shift
     normed_two = (centred(middle)[0] * scale_two + offset_two).astype(LOW)
-    active, slope = expanded(normed_two, full_up, up_shift[None], rows)
+    active, slope = expanded(normed_two, whole, up_shift[None], rows)
     result = (middle + dot(active, full_down) + down_shift).reshape(images, rows, width)[:, :seq_len]
     out_tokens = jnp.where(live, result, 0.0).astype(LOW)
 
     grad_down = dot(active, seed_low, TN).astype(LOW)
-    back_hidden = (dot(seed_low, full_down, NT) * slope.astype(WIDE)).astype(LOW)
+    seed_again, grad_down = lax.optimization_barrier((seed_low, grad_down))
+    down_sum = lax.psum_scatter(grad_down, AXES, scatter_dimension=0, tiled=True)
+    back_hidden = (dot(seed_again, full_down, NT) * slope.astype(WIDE)).astype(LOW)
     grad_up = dot(normed_two, back_hidden, TN).astype(LOW)
+    back_hidden, grad_up = lax.optimization_barrier((back_hidden, grad_up))
+    up_sum = scattered([grad_up], sizes)
     back_two = dot(back_hidden, full_up, NT)
     middle_part, grad_scale_two, grad_offset_two = norm_back(middle, scale_two, back_two)
     back_middle = seed_low.astype(WIDE) + middle_part
     back_branch = back_middle.astype(LOW)
     grad_out = dot(head_out, back_branch, TN).astype(LOW)
-    blocks = lambda matrix: [m.reshape(devices, -1, width) for m in columns(matrix)]
-    early = jnp.concatenate([*blocks(grad_out), *blocks(grad_up), *blocks(grad_down)], axis=1)
-    early = lax.psum_scatter(early, AXES, scatter_dimension=0, tiled=True)[0]
 
     back_head = dot(back_branch, full_out, NT).astype(LOW).reshape(images, rows, width)
-    back_projected = attention_back(projected, back_head, seq_len, factor).reshape(row_count, 3 * width)
+    back_projected = attention_back(projected, back_head, seq_len, factor, 2).reshape(row_count, 3 * width)
     grad_qkv = dot(normed, back_projected, TN).astype(LOW)
+    back_projected, grad_qkv = lax.optimization_barrier((back_projected, grad_qkv))
+    late = scattered([grad_qkv, grad_out], sizes)
     back_one = dot(back_projected, full_qkv, NT)
     input_part, grad_scale_one, grad_offset_one = norm_back(inputs, scale_one, back_one)
     grad_inputs = (back_middle + input_part).reshape(images, rows, width)[:, :seq_len]
@@ -362,22 +377,15 @@
         column_total(back_hidden),
         column_total(seed_low),
     )
-    small_block = small_rows([v.reshape(devices, -1) for v in small_grads])[:, :1]
-    small_sum = scattered_small(small_block, sizes)
-    late = scattered(jnp.concatenate(blocks(grad_qkv), axis=1), sizes)
-
-    def join(block, count):
-        return jnp.concatenate([block[i * share : (i + 1) * share] for i in range(count)], axis=1).astype(WIDE)
-
-    ups = w_up.shape[1] // width
+    small_sum = scattered_small(small_join([v.reshape(devices, -1) for v in small_grads]), sizes)
     small_out = [v[0] for v in small_split(small_sum[None])]
     return (
         out_tokens,
         grad_inputs,
-        join(late, 3),
-        join(early, 1),
-        join(early[share:], ups),
-        early[share * (1 + ups) :].astype(WIDE),
+        late[:, : 3 * width],
+        late[:, 3 * width :],
+        up_sum,
+        down_sum.astype(WIDE),
         *small_out,
     )
 

time: 381 us -> 393 us (1.031)
  waiting for transfers between devices: 116 us -> 125 us
  matrix products: 81.4 us -> 74.7 us
    ppermute x20 -> x27, waiting for transfers between devices: 78.5 us -> 107 us  [flipped(): return lax.ppermute(block, name, [(i, i ^ bit) for i in range(sizes[name])])]
    reduce_scatter x1, waiting for transfers between devices: 28.4 us -> 7.07 us  [per_device(): lax.psum_scatter(grad_down, AXES, scatter_dimension=0, tiled=True)]
    reshape x1 -> x3, local copies, waits for them, and re-layouts: 0.04 us -> 13.2 us  [the longest x2 13.1 us: per_device(): whole[:, hidden_width + width:].reshape(devices, share, ratio, width)]
    concatenate x5 -> x1, local copies, waits for them, and re-layouts: 9.06 us -> 0.77 us  [per_device(): jnp.concatenate(rest, axis=1)]
    convert_element_type x7, local copies, waits for them, and re-layouts: 0.57 us -> 8.58 us  [per_device(): vectors = [v.reshape(-1).astype(WIDE) for v in small_split(small_whole)]]
    slice x10 -> x6, local copies, waits for them, and re-layouts: 13.7 us -> 6.39 us  [the longest x1 4.89 us: per_device(): whole[:, hidden_width + width:].reshape(devices, share, ratio, width)]
    unnamed x74 -> x94, local copies, waits for them, and re-layouts: 17.4 us -> 10.6 us
    dot_general x11, matrix products: 81.4 us -> 74.7 us  [dot(): return lax.dot_general(a, b, dims, preferred_element_type=WIDE)]
  transfers between devices with their start and end apart: 22 -> 29, of which waited for: 16 -> 21; matrix products, arithmetic and copies ran while one was open for 17% -> 15% of each run, Pallas kernels for 10% -> 2%
where the time goes in v3:
time: 393 us; the launch traced here: 387 us
  waiting for transfers between devices  125 us (32%)
  matrix products  74.7 us (19%)
  Pallas kernels  57.1 us (15%)
  local copies, waits for them, and re-layouts  51.8 us (13%)
  other arithmetic  35.5 us (9%)
  starting transfers between devices  26.9 us (7%)
  between operations  16.1 us (4%)
    ppermute x27, waiting for transfers between devices, flipped(): return lax.ppermute(block, name, [(i, i ^ bit) for i in range(sizes[name])])  107 us
    dot_general x11, matrix products, dot(): return lax.dot_general(a, b, dims, preferred_element_type=WIDE)  74.7 us
    pallas_call x3, Pallas kernels, attention_back(): pl.pallas_call(functools.partial(attend_back, seq_len, factor), grid=(min...  27.9 us
    ppermute x27, starting transfers between devices, flipped(): return lax.ppermute(block, name, [(i, i ^ bit) for i in range(sizes[name])])  26.9 us
    pallas_call x1, Pallas kernels, expanded(): pl.pallas_call(functools.partial(expand, step), grid=(full // width,), in...  21.4 us
    reshape x2, local copies, waits for them, and re-layouts, per_device(): whole[:, hidden_width + width:].reshape(devices, share, ratio, width)  13.1 us
    all_gather x1, waiting for transfers between devices, per_device(): lax.all_gather(jnp.concatenate(rest, axis=1), AXES, axis=0, tiled=True)  10.8 us
    unnamed x94, local copies, waits for them, and re-layouts  10.6 us
  transfers between devices with their start and end apart: 29, of which 21 were waited for; matrix products, arithmetic and copies ran while one was open for 15% of the time, Pallas kernels for 2%

profile of v3, /device:TPU:0, one launch (start us, length us, event | category | flops | bytes accessed | tf_op | source)
XLA Modules:
  0.0 387.1 jit_solution(592303794741540140)
XLA Ops:
  14.7 4.1 %collective-permute-start = (bf16[24,2432]{1,0:T(8,128)(2,1)S(1)}, bf16[24,2432]{1,0:T(8,128)(2,1)S(1)}, u32[]{:S(2)}, u32[]{:S(2)}) collective-permute-start(bf16[24,2432]{1,0:T(8,128)(2,1)S(1)} %fusion.38), channel_id=1, source_target_pairs={{0,16},{4,20},{8,24},{12,28},{16,0},{20,4},{24,8},{28,12},{1,17},{... | collective-permute-start | bytes 350216 | tf_op jit(solution)/shard_map/ppermute | solution.py:196
  30.1 6.0 %collective-permute-done.1 = bf16[2,24,2432]{2,1,0:T(8,128)(2,1)S(1)} collective-permute-done((bf16[2,24,2432]{2,1,0:T(8,128)(2,1)S(1)}, bf16[2,24,2432]{2,1,0:T(8,128)(2,1)S(1)}, u32[]{:S(2)}, u32[]{:S(2)}) %collective-permute-start.1) | collective-permute-done | bytes 233504 | tf_op jit(solution)/shard_map/ppermute | solution.py:196
  39.1 3.3 collective-permute-done.5
  46.8 11.9 %collective-permute-done.6 = bf16[2,2,2,24,1152]{4,3,1,0,2:T(8,128)(2,1)S(1)} collective-permute-done((bf16[2,2,2,24,1152]{4,3,1,0,2:T(8,128)(2,1)S(1)}, bf16[2,2,2,24,1152]{4,3,1,0,2:T(8,128)(2,1)S(1)}, u32[]{:S(2)}, u32[]{:S(2)}) %collective-permute-start.6) | collective-permute-done | bytes 442400 | tf_op jit(solution)/shard_map/ppermute | solution.py:196
  59.6 6.8 %collective-permute-done.3 = bf16[2,2,2,24,1280]{4,3,2,1,0:T(8,128)(2,1)} collective-permute-done((bf16[2,2,2,24,1280]{4,3,2,1,0:T(8,128)(2,1)}, bf16[2,2,2,24,1280]{4,3,2,1,0:T(8,128)(2,1)}, u32[]{:S(2)}, u32[]{:S(2)}) %collective-permute-start.3) | collective-permute-done | bytes 491552 | tf_op jit(solution)/shard_map/ppermute | solution.py:196
  86.4 7.9 %fusion = bf16[1248,2304]{1,0:T(8,128)(2,1)S(1)} fusion(f32[2304]{0:T(1024)S(1)} %pad_maximum_fusion.12, bf16[768,1152]{1,0:T(8,128)(2,1)S(1)} %slice.188, bf16[768,1152]{1,0:T(8,128)(2,1)S(1)} %bitcast.241, f32[1248,768]{1,0:T(8,128)} %fusion.6, f32[768]{0:T(1024)} %reshape.338, f32[768]{0:T(1024)} %reshape.337), kind=kOutput, calls=%fused_computation.4 | convolution fusion | flops 4432306176 | bytes 13138944 | tf_op jit(solution)/shard_map/dot_general | solution.py:22
  94.3 7.8 %shard_map.254 = bf16[6,208,768]{2,1,0:T(8,128)(2,1)S(1)} custom-call(bf16[6,208,2304]{2,1,0:T(8,128)(2,1)S(1)} %bitcast.214), custom_call_target="tpu_custom_call" | custom-call | tf_op jit(solution)/shard_map/pallas_call | solution.py:94
  104.5 10.8 %all-gather.2.cloned.1.call-done.weight_ref = bf16[768,6912]{1,0:T(8,128)(2,1)} async-done(((bf16[24,6912]{1,0:T(8,128)(2,1)}), bf16[768,6912]{1,0:T(8,128)(2,1)}) %all-gather.2.cloned.1.call-update) | async-done | bytes 10616848 | tf_op jit(solution)/shard_map/all_gather | solution.py:325
  115.3 4.9 %slice.197 = bf16[768,3072]{1,0:T(8,128)(2,1)} slice(bf16[768,6912]{1,0:T(8,128)(2,1)} %all-gather.2.cloned.1.call-done.weight_ref), slice={[0:768], [3840:6912]} | slice | bytes 9437184 | tf_op jit(solution)/shard_map/slice | solution.py:328
  120.2 9.7 %reshape.316 = bf16[32,24,4,768]{3,2,1,0:T(4,128)(2,1)} reshape(bf16[768,3072]{1,0:T(8,128)(2,1)} %slice.197) | data formatting | bytes 9437184 | tf_op jit(solution)/shard_map/reshape | solution.py:328
  129.9 3.4 copy.36
  133.4 4.0 %fusion.57 = (f32[1248]{0:T(1024)S(1)}, f32[1248,768]{1,0:T(8,128)S(1)}) fusion(f32[768]{0:T(1024)S(1)} %copy-done.35, f32[1248,768]{1,0:T(8,128)S(1)} %bitcast.238, bf16[1248,768]{1,0:T(8,128)(2,1)S(1)} %bitcast.223, bf16[768,6912]{1,0:T(8,128)(2,1)} %all-gather.2.cloned.1.call-done.weight_ref), kind=kOutput, calls=%fused_computation.216 | convolution fusion | flops 1475074816 | bytes 10772352 | tf_op jit(solution)/shard_map/dot_general | solution.py:22
  138.9 21.4 %shard_map.255 = (bf16[1248,3072]{1,0:T(8,128)(2,1)S(1)}, bf16[1248,3072]{1,0:T(8,128)(2,1)}) custom-call(bf16[1248,768]{1,0:T(8,128)(2,1)S(1)} %add_convert_fusion.2.rows_ref, bf16[768,6912]{1,0:T(8,128)(2,1)} %all-gather.2.cloned.1.call-done.weight_ref, f32[1,3072]{1,0:T(1,128)S(1)} %reshape.342.shift_ref), custom_call_target="tpu_custom_call" | custom-call | flops 5888802816 | bytes 23003136 | tf_op jit(solution)/shard_map/pallas_call | solution.py:156
  160.3 6.2 %fusion.5 = bf16[1248,768]{1,0:T(8,128)(2,1)S(1)} fusion(f32[1248,768]{1,0:T(8,128)S(1)} %get-tuple-element.99, bf16[1248,3072]{1,0:T(8,128)(2,1)S(1)} %get-tuple-element.22, bf16[3072,768]{1,0:T(8,128)(2,1)S(1)} %bitcast.236, f32[768]{0:T(1024)S(1)} %copy-done.34), kind=kOutput, calls=%fused_computation.16 | convolution fusion | flops 5891678208 | bytes 18140160 | tf_op jit(solution)/shard_map/dot_general | solution.py:22
  170.3 8.3 %convolution_convert_fusion = bf16[3072,768]{1,0:T(8,128)(2,1)} fusion(bf16[1248,3072]{1,0:T(8,128)(2,1)S(1)} %get-tuple-element.22, bf16[1248,768]{1,0:T(8,128)(2,1)S(1)} %bitcast.230), kind=kOutput, calls=%fused_computation.6 | convolution fusion | flops 5891162112 | bytes 14303232 | tf_op jit(solution)/shard_map/dot_general | solution.py:22
  178.6 9.8 %multiply_convert_fusion = bf16[1248,3072]{1,0:T(8,128)(2,1)S(1)} fusion(bf16[1248,3072]{1,0:T(8,128)(2,1)} %get-tuple-element.24, bf16[1248,768]{1,0:T(8,128)(2,1)} %bitcast.231, bf16[3072,768]{1,0:T(8,128)(2,1)} %bitcast.237), kind=kOutput, calls=%fused_computation.1 | convolution fusion | flops 5900304384 | bytes 21970944 | tf_op jit(solution)/shard_map/dot_general | solution.py:22
  188.3 8.2 %convolution_convert_fusion.1 = bf16[768,3072]{1,0:T(8,128)(2,1)} fusion(bf16[1248,768]{1,0:T(8,128)(2,1)S(1)} %add_convert_fusion.2.rows_ref, bf16[1248,3072]{1,0:T(8,128)(2,1)S(1)} %multiply_convert_fusion), kind=kOutput, calls=%fused_computation.7 | convolution fusion | flops 5891162112 | bytes 14303232 | tf_op jit(solution)/shard_map/dot_general | solution.py:22
  198.6 10.0 %multiply_reduce_fusion = (f32[768]{0:T(1024)S(1)}, f32[1248]{0:T(1024)S(1)}, f32[1248]{0:T(1024)S(1)}, f32[768]{0:T(1024)S(1)}, f32[1248,768]{1,0:T(8,128)S(1)}) fusion(f32[1248,768]{1,0:T(8,128)S(1)} %copy-done.6, f32[1248]{0:T(1024)S(1)} %add_rsqrt_fusion, f32[1248]{0:T(1024)S(1)} %broadcast_multiply_fusion.4, f32[768]{0:T(1024)S(1)} %reshape.340, ...), kind=kOutput, calls=%fused_computation.20 | convolution fusion | flops 5897424896 | bytes 20083200 | tf_op jit(solution)/shard_map/dot_general | solution.py:22
  210.3 4.0 %convolution_convert_fusion.2 = bf16[1248,768]{1,0:T(8,128)(2,1)S(1)} fusion(bf16[768,6912]{1,0:T(8,128)(2,1)} %all-gather.2.cloned.1.call-done.weight_ref, f32[1248,768]{1,0:T(8,128)S(1)} %get-tuple-element.43), kind=kOutput, calls=%fused_computation.37 | convolution fusion | flops 1474117632 | bytes 6930432 | tf_op jit(solution)/shard_map/dot_general | solution.py:22
  214.4 9.4 %shard_map.256.refs_0_ = bf16[6,208,2304]{2,1,0:T(8,128)(2,1)S(1)} custom-call(bf16[6,208,2304]{2,1,0:T(8,128)(2,1)S(1)} %bitcast.217, bf16[6,208,768]{2,1,0:T(8,128)(2,1)S(1)} %bitcast.220), custom_call_target="tpu_custom_call" | custom-call | flops 2658140160 | bytes 13418496 | tf_op jit(solution)/shard_map/pallas_call | solution.py:112
  223.9 9.2 %shard_map.257.refs_0_ = bf16[6,208,2304]{2,1,0:T(8,128)(2,1)S(1)} custom-call(bf16[6,208,2304]{2,1,0:T(8,128)(2,1)S(1)} %bitcast.218, bf16[6,208,768]{2,1,0:T(8,128)(2,1)S(1)} %bitcast.221, bf16[6,208,2304]{2,1,0:T(8,128)(2,1)S(1)} %shard_map.256.refs_0_), custom_call_target="tpu_custom_call", output_to_operand_aliasing={{}: (2, {})} | custom-call | flops 2658140160 | bytes 13418496 | tf_op jit(solution)/shard_map/pallas_call | solution.py:112
  233.2 9.2 %shard_map.258 = bf16[6,208,2304]{2,1,0:T(8,128)(2,1)S(1)} custom-call(bf16[6,208,2304]{2,1,0:T(8,128)(2,1)S(1)} %bitcast.219, bf16[6,208,768]{2,1,0:T(8,128)(2,1)S(1)} %bitcast.222, bf16[6,208,2304]{2,1,0:T(8,128)(2,1)S(1)} %shard_map.257.refs_0_), custom_call_target="tpu_custom_call", output_to_operand_aliasing={{}: (2, {})} | custom-call | flops 2658140160 | bytes 13418496 | tf_op jit(solution)/shard_map/pallas_call | solution.py:112
  242.5 7.1 %bitcast_convert_fusion = bf16[768,2304]{1,0:T(8,128)(2,1)} fusion(bf16[6,208,2304]{2,1,0:T(8,128)(2,1)S(1)} %shard_map.258, f32[768]{0:T(1024)S(1)} %copy-done.33, f32[768]{0:T(1024)S(1)} %copy-done.31, f32[6,208]{1,0:T(8,128)S(1)} %copy-done.30, f32[6,208]{1,0:T(8,128)S(1)} %copy-done.24, bf16[6,197,768]{2,1,0:T(8,128)(2,1)S(1)} %copy-done.4), kind=kOutput, calls=%fused_computation.5 | convolution fusion | flops 4424122368 | bytes 11121408 | tf_op jit(solution)/shard_map/dot_general | solution.py:22
  249.7 7.5 %multiply_reduce_fusion.1 = (f32[768]{0:T(1024)S(1)}, f32[768]{0:T(1024)S(1)}, f32[1248]{0:T(1024)S(1)}, f32[1248]{0:T(1024)S(1)}, f32[1248,768]{1,0:T(8,128)}) fusion(f32[1248]{0:T(1024)S(1)} %copy-done.28, f32[1248]{0:T(1024)S(1)} %copy-done.26, bf16[6,197,768]{2,1,0:T(8,128)(2,1)S(1)} %copy-done.4, f32[1248,768]{1,0:T(8,128)S(1)} %copy-done.12, ...), kind=kOutput, calls=%fused_computation.22 | convolution fusion | flops 4433260544 | bytes 18802176 | tf_op jit(solution)/shard_map/dot_general | solution.py:22
  262.8 4.4 %multiply_add_fusion = f32[1248,768]{1,0:T(8,128)S(1)} fusion(f32[1248,768]{1,0:T(8,128)} %copy-done.7, f32[1248,768]{1,0:T(8,128)} %get-tuple-element.101, f32[1248]{0:T(1024)S(1)} %broadcast_multiply_fusion, f32[1248]{0:T(1024)S(1)} %broadcast_multiply_fusion.1, f32[768]{0:T(1024)S(1)} %copy-done.31, f32[1248]{0:T(1024)S(1)} %copy-done.28, ...), kind=kLoop, calls=%fused_computation.23 | loop fusion | flops 8626176 | bytes 13340160 | tf_op jit(solution)/shard_map/add | solution.py:368
  293.4 10.8 %collective-permute-done.18 = bf16[2,2,2,24,1536]{4,3,2,1,0:T(8,128)(2,1)S(1)} collective-permute-done((bf16[2,2,2,24,1536]{4,3,2,1,0:T(8,128)(2,1)S(1)}, bf16[2,2,2,24,1536]{4,3,2,1,0:T(8,128)(2,1)S(1)}, u32[]{:S(2)}, u32[]{:S(2)}) %collective-permute-start.18) | collective-permute-done | bytes 589856 | tf_op jit(solution)/shard_map/ppermute | solution.py:196
  306.6 15.2 %collective-permute-done.11 = bf16[2,2,2,24,1536]{4,3,2,1,0:T(8,128)(2,1)S(1)} collective-permute-done((bf16[2,2,2,24,1536]{4,3,2,1,0:T(8,128)(2,1)S(1)}, bf16[2,2,2,24,1536]{4,3,2,1,0:T(8,128)(2,1)S(1)}, u32[]{:S(2)}, u32[]{:S(2)}) %collective-permute-start.11) | collective-permute-done | bytes 589856 | tf_op jit(solution)/shard_map/ppermute | solution.py:196
  324.9 13.4 %collective-permute-done.12 = bf16[2,2,24,1536]{3,2,1,0:T(8,128)(2,1)S(1)} collective-permute-done((bf16[2,2,24,1536]{3,2,1,0:T(8,128)(2,1)S(1)}, bf16[2,2,24,1536]{3,2,1,0:T(8,128)(2,1)S(1)}, u32[]{:S(2)}, u32[]{:S(2)}) %collective-permute-start.12) | collective-permute-done | bytes 294944 | tf_op jit(solution)/shard_map/ppermute | solution.py:196
  340.9 13.6 %collective-permute-done.13 = bf16[2,24,3072]{2,1,0:T(8,128)(2,1)S(1)} collective-permute-done((bf16[2,24,3072]{2,1,0:T(8,128)(2,1)S(1)}, bf16[2,24,3072]{2,1,0:T(8,128)(2,1)S(1)}, u32[]{:S(2)}, u32[]{:S(2)}) %collective-permute-start.13) | collective-permute-done | bytes 294944 | tf_op jit(solution)/shard_map/ppermute | solution.py:196
  354.7 7.6 %collective-permute-done.20 = bf16[2,24,3072]{2,1,0:T(8,128)(2,1)S(1)} collective-permute-done((bf16[2,24,3072]{2,1,0:T(8,128)(2,1)S(1)}, bf16[2,24,3072]{2,1,0:T(8,128)(2,1)S(1)}, u32[]{:S(2)}, u32[]{:S(2)}) %collective-permute-start.20) | collective-permute-done | bytes 294944 | tf_op jit(solution)/shard_map/ppermute | solution.py:196
  366.3 4.3 %collective-permute-done.21 = bf16[24,3072]{1,0:T(8,128)(2,1)S(1)} collective-permute-done((bf16[24,3072]{1,0:T(8,128)(2,1)S(1)}, bf16[24,3072]{1,0:T(8,128)(2,1)S(1)}, u32[]{:S(2)}, u32[]{:S(2)}) %collective-permute-start.21) | collective-permute-done | bytes 147488 | tf_op jit(solution)/shard_map/ppermute | solution.py:196
  371.3 7.1 %reduce-scatter.2.cloned.1.call-done = bf16[96,768]{1,0:T(8,128)(2,1)} async-done(((bf16[3072,768]{1,0:T(8,128)(2,1)}), bf16[96,768]{1,0:T(8,128)(2,1)}) %reduce-scatter.2.cloned.1.call-update) | async-done | bytes 147472 | tf_op jit(solution)/shard_map/reduce_scatter | solution.py:350
  (267 shorter events, 103.6 us)
Async XLA Ops:
  7.2 108.1 %all-gather.2.cloned.1.call-start = ((), (), s32[]{:S(2)}) async-start(), calls=%async_computation.1 | async-start | bytes 10948608 | tf_op jit(solution)/shard_map/all_gather | solution.py:325
  12.9 365.5 %reduce-scatter.2.cloned.1.call-start = ((), (), s32[]{:S(2)}) async-start(), calls=%async_computation.2 | async-start | bytes 4866048 | tf_op jit(solution)/shard_map/reduce_scatter | solution.py:350
  14.7 9.8 %collective-permute-start = (bf16[24,2432]{1,0:T(8,128)(2,1)S(1)}, bf16[24,2432]{1,0:T(8,128)(2,1)S(1)}, u32[]{:S(2)}, u32[]{:S(2)}) collective-permute-start(bf16[24,2432]{1,0:T(8,128)(2,1)S(1)} %fusion.38), channel_id=1, source_target_pairs={{0,16},{4,20},{8,24},{12,28},{16,0},{20,4},{24,8},{28,12},{1,17},{... | collective-permute-start | bytes 350216 | tf_op jit(solution)/shard_map/ppermute | solution.py:196
  24.6 11.5 %collective-permute-start.1 = (bf16[2,24,2432]{2,1,0:T(8,128)(2,1)S(1)}, bf16[2,24,2432]{2,1,0:T(8,128)(2,1)S(1)}, u32[]{:S(2)}, u32[]{:S(2)}) collective-permute-start(bf16[2,24,2432]{2,1,0:T(8,128)(2,1)S(1)} %pad_maximum_fusion.10), channel_id=1, source_target_pairs={{0,8},{4,12},{8,0},{12,4},{16,24},{20,28},{24,16},{28,20},{1,9},{5... | collective-permute-start | bytes 700424 | tf_op jit(solution)/shard_map/ppermute | solution.py:196
  36.2 6.2 %collective-permute-start.5 = (bf16[2,2,24,1152]{3,2,1,0:T(8,128)(2,1)S(1)}, bf16[2,2,24,1152]{3,2,1,0:T(8,128)(2,1)S(1)}, u32[]{:S(2)}, u32[]{:S(2)}) collective-permute-start(bf16[2,2,24,1152]{3,2,1,0:T(8,128)(2,1)S(1)} %pad_maximum_fusion.11), channel_id=1, source_target_pairs={{0,4},{4,0},{8,12},{12,8},{16,20},{20,16},{24,28},{28,24},{1,5},{5... | collective-permute-start | bytes 663560 | tf_op jit(solution)/shard_map/ppermute | solution.py:196
  37.5 7.7 %collective-permute-start.2 = (bf16[2,2,24,1280]{3,2,1,0:T(8,128)(2,1)S(1)}, bf16[2,2,24,1280]{3,2,1,0:T(8,128)(2,1)S(1)}, u32[]{:S(2)}, u32[]{:S(2)}) collective-permute-start(bf16[2,2,24,1280]{3,2,1,0:T(8,128)(2,1)S(1)} %fusion.36), channel_id=1, source_target_pairs={{0,2},{1,3},{2,0},{3,1},{4,6},{5,7},{6,4},{7,5},{8,10},{9,11},{10,... | collective-permute-start | bytes 737288 | tf_op jit(solution)/shard_map/ppermute | solution.py:196
  42.5 16.2 %collective-permute-start.6 = (bf16[2,2,2,24,1152]{4,3,1,0,2:T(8,128)(2,1)S(1)}, bf16[2,2,2,24,1152]{4,3,1,0,2:T(8,128)(2,1)S(1)}, u32[]{:S(2)}, u32[]{:S(2)}) collective-permute-start(bf16[2,2,2,24,1152]{4,3,1,0,2:T(8,128)(2,1)S(1)} %pad_maximum_fusion.9), channel_id=1, source_target_pairs={{0,2},{1,3},{2,0},{3,1},{4,6},{5,7},{6,4},{7,5},{8,10},{9,11},{10,... | collective-permute-start | bytes 1327112 | tf_op jit(solution)/shard_map/ppermute | solution.py:196
  46.0 20.4 %collective-permute-start.3 = (bf16[2,2,2,24,1280]{4,3,2,1,0:T(8,128)(2,1)}, bf16[2,2,2,24,1280]{4,3,2,1,0:T(8,128)(2,1)}, u32[]{:S(2)}, u32[]{:S(2)}) collective-permute-start(bf16[2,2,2,24,1280]{4,3,2,1,0:T(8,128)(2,1)} %pad_maximum_fusion.8), channel_id=1, source_target_pairs={{0,4},{4,0},{8,12},{12,8},{16,20},{20,16},{24,28},{28,24},{1,5},{5... | collective-permute-start | bytes 1474568 | tf_op jit(solution)/shard_map/ppermute | solution.py:196
  58.9 9.3 %collective-permute-start.7 = (bf16[2,2,2,2,24,1152]{5,4,1,0,2,3:T(8,128)(2,1)S(1)}, bf16[2,2,2,2,24,1152]{5,4,1,0,2,3:T(8,128)(2,1)S(1)}, u32[]{:S(2)}, u32[]{:S(2)}) collective-permute-start(bf16[2,2,2,2,24,1152]{5,4,1,0,2,3:T(8,128)(2,1)S(1)} %pad_maximum_fusion.7), channel_id=1, source_target_pairs={{0,1},{1,0},{2,3},{3,2},{4,5},{5,4},{6,7},{7,6},{8,9},{9,8},{10,11... | collective-permute-start | bytes 2654216 | tf_op jit(solution)/shard_map/ppermute | solution.py:196
  67.6 2.6 collective-permute-start.4
  70.7 23.6 %copy-start.18 = (bf16[768,1152]{1,0:T(8,128)(2,1)}, bf16[768,1152]{1,0:T(8,128)(2,1)S(1)}, u32[]{:S(2)}) copy-start(bf16[768,1152]{1,0:T(8,128)(2,1)S(1)} %slice.188) | copy-start | bytes 5308420
  104.5 28.8 %copy-start.1 = (bf16[6,208,768]{2,1,0:T(8,128)(2,1)}, bf16[6,208,768]{2,1,0:T(8,128)(2,1)S(1)}, u32[]{:S(2)}) copy-start(bf16[6,208,768]{2,1,0:T(8,128)(2,1)S(1)} %shard_map.254) | copy-start | bytes 5750788
  133.3 26.9 %copy-start.11 = (bf16[32,24,4,768]{3,1,2,0:T(8,128)(2,1)}, bf16[32,24,4,768]{3,1,2,0:T(8,128)(2,1)S(1)}, u32[]{:S(2)}) copy-start(bf16[32,24,4,768]{3,1,2,0:T(8,128)(2,1)S(1)} %copy.36) | copy-start | bytes 14155780
  261.7 23.3 %collective-permute-start.15 = (bf16[16,24,3072]{2,1,0:T(8,128)(2,1)}, bf16[16,24,3072]{2,1,0:T(8,128)(2,1)}, u32[]{:S(2)}, u32[]{:S(2)}) collective-permute-start(bf16[16,24,3072]{2,1,0:T(8,128)(2,1)} %dynamic-slice_bitcast_fusion), channel_id=1, source_target_pairs={{0,1},{1,0},{2,3},{3,2},{4,5},{5,4},{6,7},{7,6},{8,9},{9,8},{10,11... | collective-permute-start | bytes 7077896 | tf_op jit(solution)/shard_map/ppermute | solution.py:196
  262.5 4.8 %collective-permute-start.22 = (f32[2,2,2,2,384]{4,3,2,1,0:T(2,128)S(1)}, f32[2,2,2,2,384]{4,3,2,1,0:T(2,128)S(1)}, u32[]{:S(2)}, u32[]{:S(2)}) collective-permute-start(f32[2,2,2,2,384]{4,3,2,1,0:T(2,128)S(1)} %bitcast.251), channel_id=1, source_target_pairs={{0,1},{1,0},{2,3},{3,2},{4,5},{5,4},{6,7},{7,6},{8,9},{9,8},{10,11... | collective-permute-start | bytes 73736 | tf_op jit(solution)/shard_map/ppermute | solution.py:196
  267.4 3.8 collective-permute-start.23
  271.2 3.7 collective-permute-start.24
  274.9 3.7 collective-permute-start.25
  278.6 4.5 %collective-permute-start.26 = (f32[384]{0:T(512)S(1)}, f32[384]{0:T(512)S(1)}, u32[]{:S(2)}, u32[]{:S(2)}) collective-permute-start(f32[384]{0:T(512)S(1)} %get-tuple-element.40), channel_id=1, source_target_pairs={{0,16},{4,20},{8,24},{12,28},{16,0},{20,4},{24,8},{28,12},{1,17},{... | collective-permute-start | bytes 4616 | tf_op jit(solution)/shard_map/ppermute | solution.py:196
  282.7 7.2 %collective-permute-start.8 = (bf16[16,24,3072]{2,1,0:T(8,128)(2,1)S(1)}, bf16[16,24,3072]{2,1,0:T(8,128)(2,1)S(1)}, u32[]{:S(2)}, u32[]{:S(2)}) collective-permute-start(bf16[16,24,3072]{2,1,0:T(8,128)(2,1)S(1)} %pad_maximum_fusion.1), channel_id=1, source_target_pairs={{0,1},{1,0},{2,3},{3,2},{4,5},{5,4},{6,7},{7,6},{8,9},{9,8},{10,11... | collective-permute-start | bytes 7077896 | tf_op jit(solution)/shard_map/ppermute | solution.py:196
  288.0 16.2 %collective-permute-start.18 = (bf16[2,2,2,24,1536]{4,3,2,1,0:T(8,128)(2,1)S(1)}, bf16[2,2,2,24,1536]{4,3,2,1,0:T(8,128)(2,1)S(1)}, u32[]{:S(2)}, u32[]{:S(2)}) collective-permute-start(bf16[2,2,2,24,1536]{4,3,2,1,0:T(8,128)(2,1)S(1)} %dynamic-slice_bitcast_fusion.3), channel_id=1, source_target_pairs={{0,4},{4,0},{8,12},{12,8},{16,20},{20,16},{24,28},{28,24},{1,5},{5... | collective-permute-start | bytes 1769480 | tf_op jit(solution)/shard_map/ppermute | solution.py:196
  289.4 16.3 %collective-permute-start.16 = (bf16[2,2,2,24,1536]{4,3,1,0,2:T(8,128)(2,1)S(1)}, bf16[2,2,2,24,1536]{4,3,1,0,2:T(8,128)(2,1)S(1)}, u32[]{:S(2)}, u32[]{:S(2)}) collective-permute-start(bf16[2,2,2,24,1536]{4,3,1,0,2:T(8,128)(2,1)S(1)} %bitcast.244), channel_id=1, source_target_pairs={{0,2},{1,3},{2,0},{3,1},{4,6},{5,7},{6,4},{7,5},{8,10},{9,11},{10,... | collective-permute-start | bytes 1769480 | tf_op jit(solution)/shard_map/ppermute | solution.py:196
  291.2 30.7 %collective-permute-start.11 = (bf16[2,2,2,24,1536]{4,3,2,1,0:T(8,128)(2,1)S(1)}, bf16[2,2,2,24,1536]{4,3,2,1,0:T(8,128)(2,1)S(1)}, u32[]{:S(2)}, u32[]{:S(2)}) collective-permute-start(bf16[2,2,2,24,1536]{4,3,2,1,0:T(8,128)(2,1)S(1)} %dynamic-slice_bitcast_fusion.4), channel_id=1, source_target_pairs={{0,4},{4,0},{8,12},{12,8},{16,20},{20,16},{24,28},{28,24},{1,5},{5... | collective-permute-start | bytes 1769480 | tf_op jit(solution)/shard_map/ppermute | solution.py:196
  292.7 32.0 %collective-permute-start.9 = (bf16[2,2,2,24,1536]{4,3,1,0,2:T(8,128)(2,1)S(1)}, bf16[2,2,2,24,1536]{4,3,1,0,2:T(8,128)(2,1)S(1)}, u32[]{:S(2)}, u32[]{:S(2)}) collective-permute-start(bf16[2,2,2,24,1536]{4,3,1,0,2:T(8,128)(2,1)S(1)} %bitcast.245), channel_id=1, source_target_pairs={{0,2},{1,3},{2,0},{3,1},{4,6},{5,7},{6,4},{7,5},{8,10},{9,11},{10,... | collective-permute-start | bytes 1769480 | tf_op jit(solution)/shard_map/ppermute | solution.py:196
  304.4 34.7 %collective-permute-start.19 = (bf16[2,2,24,1536]{3,2,1,0:T(8,128)(2,1)S(1)}, bf16[2,2,24,1536]{3,2,1,0:T(8,128)(2,1)S(1)}, u32[]{:S(2)}, u32[]{:S(2)}) collective-permute-start(bf16[2,2,24,1536]{3,2,1,0:T(8,128)(2,1)S(1)} %dynamic-slice_bitcast_fusion.7), channel_id=1, source_target_pairs={{0,2},{1,3},{2,0},{3,1},{4,6},{5,7},{6,4},{7,5},{8,10},{9,11},{10,... | collective-permute-start | bytes 884744 | tf_op jit(solution)/shard_map/ppermute | solution.py:196
  306.0 33.3 %collective-permute-start.17 = (bf16[2,2,24,1536]{3,2,1,0:T(8,128)(2,1)S(1)}, bf16[2,2,24,1536]{3,2,1,0:T(8,128)(2,1)S(1)}, u32[]{:S(2)}, u32[]{:S(2)}) collective-permute-start(bf16[2,2,24,1536]{3,2,1,0:T(8,128)(2,1)S(1)} %dynamic-slice_bitcast_fusion.8), channel_id=1, source_target_pairs={{0,4},{4,0},{8,12},{12,8},{16,20},{20,16},{24,28},{28,24},{1,5},{5... | collective-permute-start | bytes 884744 | tf_op jit(solution)/shard_map/ppermute | solution.py:196
  322.0 16.3 %collective-permute-start.12 = (bf16[2,2,24,1536]{3,2,1,0:T(8,128)(2,1)S(1)}, bf16[2,2,24,1536]{3,2,1,0:T(8,128)(2,1)S(1)}, u32[]{:S(2)}, u32[]{:S(2)}) collective-permute-start(bf16[2,2,24,1536]{3,2,1,0:T(8,128)(2,1)S(1)} %dynamic-slice_bitcast_fusion.9), channel_id=1, source_target_pairs={{0,2},{1,3},{2,0},{3,1},{4,6},{5,7},{6,4},{7,5},{8,10},{9,11},{10,... | collective-permute-start | bytes 884744 | tf_op jit(solution)/shard_map/ppermute | solution.py:196
  324.8 13.5 %collective-permute-start.10 = (bf16[2,2,24,1536]{3,2,1,0:T(8,128)(2,1)S(1)}, bf16[2,2,24,1536]{3,2,1,0:T(8,128)(2,1)S(1)}, u32[]{:S(2)}, u32[]{:S(2)}) collective-permute-start(bf16[2,2,24,1536]{3,2,1,0:T(8,128)(2,1)S(1)} %dynamic-slice_bitcast_fusion.10), channel_id=1, source_target_pairs={{0,4},{4,0},{8,12},{12,8},{16,20},{20,16},{24,28},{28,24},{1,5},{5... | collective-permute-start | bytes 884744 | tf_op jit(solution)/shard_map/ppermute | solution.py:196
  338.5 16.0 %collective-permute-start.13 = (bf16[2,24,3072]{2,1,0:T(8,128)(2,1)S(1)}, bf16[2,24,3072]{2,1,0:T(8,128)(2,1)S(1)}, u32[]{:S(2)}, u32[]{:S(2)}) collective-permute-start(bf16[2,24,3072]{2,1,0:T(8,128)(2,1)S(1)} %fusion.33), channel_id=1, source_target_pairs={{0,8},{4,12},{8,0},{12,4},{16,24},{20,28},{24,16},{28,20},{1,9},{5... | collective-permute-start | bytes 884744 | tf_op jit(solution)/shard_map/ppermute | solution.py:196
  339.4 22.9 %collective-permute-start.20 = (bf16[2,24,3072]{2,1,0:T(8,128)(2,1)S(1)}, bf16[2,24,3072]{2,1,0:T(8,128)(2,1)S(1)}, u32[]{:S(2)}, u32[]{:S(2)}) collective-permute-start(bf16[2,24,3072]{2,1,0:T(8,128)(2,1)S(1)} %fusion.29), channel_id=1, source_target_pairs={{0,8},{4,12},{8,0},{12,4},{16,24},{20,28},{24,16},{28,20},{1,9},{5... | collective-permute-start | bytes 884744 | tf_op jit(solution)/shard_map/ppermute | solution.py:196
  354.6 10.2 %collective-permute-start.14 = (bf16[24,3072]{1,0:T(8,128)(2,1)S(1)}, bf16[24,3072]{1,0:T(8,128)(2,1)S(1)}, u32[]{:S(2)}, u32[]{:S(2)}) collective-permute-start(bf16[24,3072]{1,0:T(8,128)(2,1)S(1)} %dynamic-slice_bitcast_fusion.12), channel_id=1, source_target_pairs={{0,16},{4,20},{8,24},{12,28},{16,0},{20,4},{24,8},{28,12},{1,17},{... | collective-permute-start | bytes 442376 | tf_op jit(solution)/shard_map/ppermute | solution.py:196
  362.4 8.2 %collective-permute-start.21 = (bf16[24,3072]{1,0:T(8,128)(2,1)S(1)}, bf16[24,3072]{1,0:T(8,128)(2,1)S(1)}, u32[]{:S(2)}, u32[]{:S(2)}) collective-permute-start(bf16[24,3072]{1,0:T(8,128)(2,1)S(1)} %dynamic-slice_bitcast_fusion.11), channel_id=1, source_target_pairs={{0,16},{4,20},{8,24},{12,28},{16,0},{20,4},{24,8},{28,12},{1,17},{... | collective-permute-start | bytes 442376 | tf_op jit(solution)/shard_map/ppermute | solution.py:196
  (38 other events, 280.0 us)
Sparse Core Ops, SparseCore 0:
  13.0 102.2 all-gather.1
  258.2 120.1 reduce-scatter.1

commit v4 on v3

--- a/solution.py
+++ b/solution.py
@@ -101,13 +101,15 @@
     )(projected)
 
 
-def attention_back(projected, back_head, seq_len, factor, group):
+def attention_back(projected, back_head, seq_len, factor, group, ties):
     images, rows, wide = projected.shape
     done = None
     for start in range(0, images, group):
         def block(shape, start=start):
             return pl.BlockSpec((1,) + shape, lambda i: (i + start, 0, 0))
 
+        if ties.get(start):
+            back_head = ties[start](back_head)
         kept = () if done is None else (done,)
         done = pl.pallas_call(
             functools.partial(attend_back, seq_len, factor),
@@ -219,17 +221,6 @@
     return block, done
 
 
-def scatter_by(block, steps, left, sizes, kind=LOW):
-    for place in steps:
-        at = left.index(place)
-        bit = is_set(*place).astype(jnp.int32)
-        got = flipped(lax.dynamic_index_in_dim(block, 1 - bit, at, keepdims=False), *place, sizes)
-        mine = lax.dynamic_index_in_dim(block, bit, at, keepdims=False)
-        block = (mine.astype(WIDE) + got.astype(WIDE)).astype(kind)
-        left = [p for p in left if p != place]
-    return block, left
-
-
 def gathered(block, half, sizes):
     order = places(sizes)
     far, one_way, other_way, core = routes(sizes)
@@ -241,31 +232,104 @@
     return parts
 
 
-def scattered(arrays, sizes):
-    order = places(sizes)
-    far, one_way, other_way, core = routes(sizes)
-    bit = is_set(*core[0]).astype(jnp.int32)
-
-    def half_of(at):
-        cut = [a.reshape((-1, 2, a.shape[0] // (1 << len(order)), a.shape[1])) for a in arrays]
-        cut = [lax.dynamic_index_in_dim(a, at, 1, keepdims=False) for a in cut]
-        return jnp.concatenate(cut, axis=-1)
-
-    got = flipped(half_of(1 - bit), *core[0], sizes)
-    blocks = (half_of(bit).astype(WIDE) + got.astype(WIDE)).astype(LOW)
-    left = order[:-1]
-    blocks = blocks.reshape((2,) * len(left) + blocks.shape[1:])
-    half = blocks.shape[-1] // 2
-    one, rest = scatter_by(blocks[..., :half], one_way[::-1], left, sizes)
-    two, rest = scatter_by(blocks[..., half:], other_way[::-1], left, sizes)
-    blocks, rest = scatter_by(jnp.concatenate([one, two], axis=-1), far[:0:-1], rest, sizes)
-    return scatter_by(blocks, far[:1], rest, sizes, WIDE)[0]
-
-
-def scattered_small(blocks, sizes):
-    order = places(sizes)
-    blocks = blocks.reshape((2,) * len(order) + blocks.shape[1:])
-    return scatter_by(blocks, order[::-1], order, sizes, WIDE)[0]
+def halved(block, place, left, sizes, kind=LOW):
+    at = left.index(place)
+    bit = is_set(*place).astype(jnp.int32)
+    got = flipped(lax.dynamic_index_in_dim(block, 1 - bit, at, keepdims=False), *place, sizes)
+    mine = lax.dynamic_index_in_dim(block, bit, at, keepdims=False)
+    return (mine.astype(WIDE) + got.astype(WIDE)).astype(kind)
+
+
+class Scatter:
+    def __init__(self, arrays, way, sizes):
+        far, one_way, other_way, core = routes(sizes)
+        self.sizes = sizes
+        self.left = places(sizes)
+        self.plan = core + (one_way, other_way)[way][::-1] + far[::-1]
+        self.block = None
+        place = self.plan[0]
+        bit = is_set(*place).astype(jnp.int32)
+        cut = [a.reshape((-1, 2, a.shape[0] >> len(self.left), a.shape[1])) for a in arrays]
+
+        def half_of(at):
+            return jnp.concatenate([lax.dynamic_index_in_dim(a, at, 1, keepdims=False) for a in cut], axis=-1)
+
+        self.theirs = half_of(1 - bit)
+        self.mine = half_of(bit)
+
+    def step(self):
+        if not self.plan:
+            return
+        place, self.plan = self.plan[0], self.plan[1:]
+        if self.block is None:
+            got = flipped(self.theirs, *place, self.sizes)
+            block = (self.mine.astype(WIDE) + got.astype(WIDE)).astype(LOW)
+            self.block = block.reshape((2,) * (len(self.left) - 1) + block.shape[1:])
+        else:
+            self.block = halved(self.block, place, self.left, self.sizes, LOW if self.plan else WIDE)
+        self.left = [q for q in self.left if q != place]
+
+    def step_and_tie(self, value):
+        self.step()
+        value, self.block = lax.optimization_barrier((value, self.block))
+        return value
+
+    def cut_and_tie(self, value):
+        value, self.theirs = lax.optimization_barrier((value, self.theirs))
+        return value
+
+    def result(self):
+        while self.plan:
+            self.step()
+        return self.block
+
+
+def lay_out(sizes_of, block_ref, out_ref):
+    devices = block_ref.shape[0]
+    shares = block_ref[...].astype(WIDE)
+    at, to = 0, 0
+    for size in sizes_of:
+        full = devices * size
+        row = lax.broadcasted_iota(jnp.int32, (block_ref.shape[1], full), 0)
+        column = lax.broadcasted_iota(jnp.int32, (block_ref.shape[1], full), 1)
+        pick = jnp.where(row == at + lax.rem(column, size), 1.0, 0.0).astype(LOW)
+        spread = dot(shares.astype(LOW), pick)
+        device = lax.broadcasted_iota(jnp.int32, (devices, full), 0)
+        own = lax.div(lax.broadcasted_iota(jnp.int32, (devices, full), 1), size)
+        out_ref[:, to : to + full] = jnp.sum(jnp.where(device == own, spread, 0.0), axis=0, keepdims=True)
+        at += size
+        to += full
+
+
+def laid_out(block, sizes_of):
+    full = block.shape[0] * sum(sizes_of)
+    flat = pl.pallas_call(
+        functools.partial(lay_out, sizes_of),
+        out_shape=jax.ShapeDtypeStruct((1, full), WIDE),
+        compiler_params=pltpu.CompilerParams(vmem_limit_bytes=40 << 20),
+    )(block)
+    parts, at = [], 0
+    for size in sizes_of:
+        parts.append(flat[:, at : at + block.shape[0] * size])
+        at += block.shape[0] * size
+    return parts
+
+
+def put_beside(up_ref, down_ref, out_ref):
+    share, hidden_width = up_ref.shape
+    width = down_ref.shape[1]
+    out_ref[:, :hidden_width] = up_ref[...]
+    down = down_ref[...].astype(WIDE)
+    for i in range(down.shape[0] // share):
+        to = hidden_width + i * width
+        out_ref[:, to : to + width] = down[i * share : (i + 1) * share].astype(LOW)
+
+
+def beside(up, down):
+    return pl.pallas_call(
+        put_beside,
+        out_shape=jax.ShapeDtypeStruct((up.shape[0], up.shape[1] + down.size // up.shape[0]), LOW),
+    )(up, down)
 
 
 def per_device(
@@ -313,20 +377,20 @@
             at += size
         return total
 
-    first = [w_qkv, jnp.pad(small_join(small).reshape(side, 128), ((0, share - side), (0, 0)))]
-    left, right = gathered(jnp.concatenate(first, axis=1), 3 * width // 2, sizes)
-    full_qkv = jnp.concatenate([left, right[:, : 3 * width // 2]], axis=1)
-    small_whole = right[:, 3 * width // 2 :].reshape(devices, share, 128)[:, :side].reshape(devices, -1)
-    vectors = [v.reshape(-1).astype(WIDE) for v in small_split(small_whole)]
-    scale_one, offset_one, qv_full, out_shift, scale_two, offset_two, up_shift, down_shift = vectors
     hidden_width = w_up.shape[1]
     ratio = hidden_width // width
-    rest = [w_up, w_out, *[w_down[i * share : (i + 1) * share] for i in range(ratio)]]
-    whole = lax.all_gather(jnp.concatenate(rest, axis=1), AXES, axis=0, tiled=True)
+    whole = lax.all_gather(beside(w_up, w_down), AXES, axis=0, tiled=True)
+    small_block = jnp.pad(small_join(small).reshape(side, 128), ((0, share - side), (0, 0)))
+    first = jnp.concatenate([w_qkv, w_out, small_block], axis=1)
+    left, right = gathered(first, 2 * width, sizes)
+    full_qkv = jnp.concatenate([left, right[:, :width]], axis=1)
+    full_out = right[:, width : 2 * width]
+    small_whole = right[:, 2 * width :].reshape(devices, share, 128)[:, :side].reshape(devices, -1)
+    vectors = laid_out(small_whole, small_sizes)
+    scale_one, offset_one, qv_full, out_shift, scale_two, offset_two, up_shift, down_shift = vectors
     full_up = whole[:, :hidden_width]
-    full_out = whole[:, hidden_width : hidden_width + width]
-    full_down = whole[:, hidden_width + width :].reshape(devices, share, ratio, width)
-    full_down = full_down.swapaxes(1, 2).reshape(hidden_width, width)
+    full_down = [whole[:, to : to + width].reshape(devices, share, width) for to in range(hidden_width, 2 * hidden_width, width)]
+    full_down = jnp.stack(full_down, axis=1).reshape(hidden_width, width)
 
     def padded(array):
         return jnp.pad(array, ((0, 0), (0, rows - seq_len), (0, 0))).reshape(row_count, width)
@@ -336,12 +400,12 @@
     seed_low = padded(jnp.where(live, cotangent, jnp.zeros((), LOW)))
 
     normed = (centred(inputs)[0] * scale_one + offset_one).astype(LOW)
-    bias_full = jnp.concatenate([qv_full[:width], jnp.zeros((width,), WIDE), qv_full[width:]])
+    bias_full = jnp.concatenate([qv_full[:, :width], jnp.zeros((1, width), WIDE), qv_full[:, width:]], axis=1)
     projected = (dot(normed, full_qkv) + bias_full).astype(LOW).reshape(images, rows, 3 * width)
     head_out = attention(projected, seq_len, factor).reshape(row_count, width)
     middle = inputs + dot(head_out, full_out) + out_shift
     normed_two = (centred(middle)[0] * scale_two + offset_two).astype(LOW)
-    active, slope = expanded(normed_two, whole, up_shift[None], rows)
+    active, slope = expanded(normed_two, whole, up_shift, rows)
     result = (middle + dot(active, full_down) + down_shift).reshape(images, rows, width)[:, :seq_len]
     out_tokens = jnp.where(live, result, 0.0).astype(LOW)
 
@@ -351,19 +415,24 @@
     back_hidden = (dot(seed_again, full_down, NT) * slope.astype(WIDE)).astype(LOW)
     grad_up = dot(normed_two, back_hidden, TN).astype(LOW)
     back_hidden, grad_up = lax.optimization_barrier((back_hidden, grad_up))
-    up_sum = scattered([grad_up], sizes)
-    back_two = dot(back_hidden, full_up, NT)
+    up_sums = [Scatter([grad_up[:, : hidden_width // 2]], 0, sizes), Scatter([grad_up[:, hidden_width // 2 :]], 1, sizes)]
+
+    def step(value):
+        for part in up_sums:
+            value = part.step_and_tie(value)
+        return value
+
+    back_two = step(dot(back_hidden, full_up, NT))
     middle_part, grad_scale_two, grad_offset_two = norm_back(middle, scale_two, back_two)
     back_middle = seed_low.astype(WIDE) + middle_part
     back_branch = back_middle.astype(LOW)
     grad_out = dot(head_out, back_branch, TN).astype(LOW)
-
     back_head = dot(back_branch, full_out, NT).astype(LOW).reshape(images, rows, width)
-    back_projected = attention_back(projected, back_head, seq_len, factor, 2).reshape(row_count, 3 * width)
-    grad_qkv = dot(normed, back_projected, TN).astype(LOW)
+    back_projected = attention_back(projected, back_head, seq_len, factor, 2, {2: step, 4: step})
+    back_projected = back_projected.reshape(row_count, 3 * width)
+    grad_qkv = step(dot(normed, back_projected, TN).astype(LOW))
     back_projected, grad_qkv = lax.optimization_barrier((back_projected, grad_qkv))
-    late = scattered([grad_qkv, grad_out], sizes)
-    back_one = dot(back_projected, full_qkv, NT)
+    back_one = step(dot(back_projected, full_qkv, NT))
     input_part, grad_scale_one, grad_offset_one = norm_back(inputs, scale_one, back_one)
     grad_inputs = (back_middle + input_part).reshape(images, rows, width)[:, :seq_len]
     sums = column_total(back_projected)
@@ -377,14 +446,18 @@
         column_total(back_hidden),
         column_total(seed_low),
     )
-    small_sum = scattered_small(small_join([v.reshape(devices, -1) for v in small_grads]), sizes)
-    small_out = [v[0] for v in small_split(small_sum[None])]
+    small_block = small_join([v.reshape(devices, -1) for v in small_grads]).astype(LOW).reshape(devices, side, 128)
+    small_block = jnp.pad(small_block, ((0, 0), (0, share - side), (0, 0))).reshape(width, 128)
+    small_block, down_sum = lax.optimization_barrier((small_block, down_sum))
+    late_one = Scatter([grad_qkv[:, : 2 * width]], 0, sizes).result()
+    late_two = Scatter([grad_qkv[:, 2 * width :], grad_out, small_block], 1, sizes).result()
+    small_out = [v[0] for v in small_split(late_two[:side, 2 * width :].reshape(1, -1))]
     return (
         out_tokens,
         grad_inputs,
-        late[:, : 3 * width],
-        late[:, 3 * width :],
-        up_sum,
+        jnp.concatenate([late_one, late_two[:, :width]], axis=1),
+        late_two[:, width : 2 * width],
+        jnp.concatenate([part.result() for part in up_sums], axis=1),
         down_sum.astype(WIDE),
         *small_out,
     )

time: 393 us -> 359 us (0.913)
  waiting for transfers between devices: 125 us -> 85.5 us
  local copies, waits for them, and re-layouts: 51.8 us -> 33.6 us
  other arithmetic: 35.5 us -> 52.5 us
  starting transfers between devices: 26.9 us -> 36.3 us
  matrix products: 74.7 us -> 66.7 us
  Pallas kernels: 57.1 us -> 61.5 us
    ppermute x27 -> x28, waiting for transfers between devices: 107 us -> 81.6 us  [flipped(): return lax.ppermute(block, name, [(i, i ^ bit) for i in range(sizes[name])])]
    reshape x3 -> x1, local copies, waits for them, and re-layouts: 13.2 us -> 0.01 us  [per_device(): small_join([v.reshape(devices, -1) for v in small_grads]).astype(LOW)]
    ppermute x27 -> x28, starting transfers between devices: 26.9 us -> 36.2 us  [flipped(): return lax.ppermute(block, name, [(i, i ^ bit) for i in range(sizes[name])])]
    reduce_sum x0 -> x2, other arithmetic: none -> 8.88 us  [norm_back(): return (back, jnp.sum(grad * unit, axis=0), jnp.sum(grad, axis=0))]
    convert_element_type x7 -> x0, local copies, waits for them, and re-layouts: 8.58 us -> none  [per_device(): vectors = [v.reshape(-1).astype(WIDE) for v in small_split(small_whole)]]
    dot_general x11, matrix products: 74.7 us -> 66.7 us  [dot(): return lax.dot_general(a, b, dims, preferred_element_type=WIDE)]
    reduce_scatter x1, waiting for transfers between devices: 7.07 us -> 0.01 us  [per_device(): lax.psum_scatter(grad_down, AXES, scatter_dimension=0, tiled=True)]
    all_gather x1, waiting for transfers between devices: 10.8 us -> 3.88 us  [per_device(): whole = lax.all_gather(beside(w_up, w_down), AXES, axis=0, tiled=True)]
  transfers between devices with their start and end apart: 29 -> 30, of which waited for: 21 -> 14; matrix products, arithmetic and copies ran while one was open for 15% -> 32% of each run, Pallas kernels for 2% -> 11%
where the time goes in v4:
time: 359 us; the launch traced here: 352 us
  waiting for transfers between devices  85.5 us (24%)
  matrix products  66.7 us (19%)
  Pallas kernels  61.5 us (17%)
  other arithmetic  52.5 us (15%)
  starting transfers between devices  36.3 us (10%)
  local copies, waits for them, and re-layouts  33.6 us (9%)
  between operations  16.4 us (5%)
    ppermute x28, waiting for transfers between devices, flipped(): return lax.ppermute(block, name, [(i, i ^ bit) for i in range(sizes[name])])  81.6 us
    dot_general x11, matrix products, dot(): return lax.dot_general(a, b, dims, preferred_element_type=WIDE)  66.7 us
    ppermute x28, starting transfers between devices, flipped(): return lax.ppermute(block, name, [(i, i ^ bit) for i in range(sizes[name])])  36.2 us
    pallas_call x3, Pallas kernels, attention_back(): pl.pallas_call(functools.partial(attend_back, seq_len, factor), grid=(min...  28 us
    pallas_call x1, Pallas kernels, expanded(): pl.pallas_call(functools.partial(expand, step), grid=(full // width,), in...  22 us
    unnamed x133, local copies, waits for them, and re-layouts  12.7 us
    reduce_sum x2, other arithmetic, norm_back(): return (back, jnp.sum(grad * unit, axis=0), jnp.sum(grad, axis=0))  8.88 us
    pallas_call x1, Pallas kernels, attention(): pl.pallas_call(functools.partial(attend, seq_len, factor), grid=(images,)...  7.76 us
  transfers between devices with their start and end apart: 30, of which 14 were waited for; matrix products, arithmetic and copies ran while one was open for 32% of the time, Pallas kernels for 11%

profile of v4, /device:TPU:0, one launch (start us, length us, event | category | flops | bytes accessed | tf_op | source)
XLA Modules:
  0.0 352.5 jit_solution(17519488487551028598)
XLA Ops:
  11.0 4.1 %collective-permute-start = (bf16[24,3200]{1,0:T(8,128)(2,1)S(1)}, bf16[24,3200]{1,0:T(8,128)(2,1)S(1)}, u32[]{:S(2)}, u32[]{:S(2)}) collective-permute-start(bf16[24,3200]{1,0:T(8,128)(2,1)S(1)} %fusion.34), channel_id=1, source_target_pairs={{0,16},{4,20},{8,24},{12,28},{16,0},{20,4},{24,8},{28,12},{1,17},{... | collective-permute-start | bytes 460808 | tf_op jit(solution)/shard_map/ppermute | solution.py:198
  16.9 5.4 %collective-permute-done = bf16[24,3200]{1,0:T(8,128)(2,1)S(1)} collective-permute-done((bf16[24,3200]{1,0:T(8,128)(2,1)S(1)}, bf16[24,3200]{1,0:T(8,128)(2,1)S(1)}, u32[]{:S(2)}, u32[]{:S(2)}) %collective-permute-start) | collective-permute-done | bytes 153632 | tf_op jit(solution)/shard_map/ppermute | solution.py:198
  23.9 12.3 %collective-permute-done.1 = bf16[2,24,3200]{2,1,0:T(8,128)(2,1)S(1)} collective-permute-done((bf16[2,24,3200]{2,1,0:T(8,128)(2,1)S(1)}, bf16[2,24,3200]{2,1,0:T(8,128)(2,1)S(1)}, u32[]{:S(2)}, u32[]{:S(2)}) %collective-permute-start.1) | collective-permute-done | bytes 307232 | tf_op jit(solution)/shard_map/ppermute | solution.py:198
  39.7 5.2 %collective-permute-done.5 = bf16[2,2,24,1536]{3,2,1,0:T(8,128)(2,1)S(1)} collective-permute-done((bf16[2,2,24,1536]{3,2,1,0:T(8,128)(2,1)S(1)}, bf16[2,2,24,1536]{3,2,1,0:T(8,128)(2,1)S(1)}, u32[]{:S(2)}, u32[]{:S(2)}) %collective-permute-start.5) | collective-permute-done | bytes 294944 | tf_op jit(solution)/shard_map/ppermute | solution.py:198
  46.3 4.7 %collective-permute-done.2 = bf16[2,2,24,1664]{3,2,1,0:T(8,128)(2,1)S(1)} collective-permute-done((bf16[2,2,24,1664]{3,2,1,0:T(8,128)(2,1)S(1)}, bf16[2,2,24,1664]{3,2,1,0:T(8,128)(2,1)S(1)}, u32[]{:S(2)}, u32[]{:S(2)}) %collective-permute-start.2) | collective-permute-done | bytes 319520 | tf_op jit(solution)/shard_map/ppermute | solution.py:198
  51.3 12.3 %collective-permute-done.6 = bf16[2,2,2,24,1536]{4,3,1,0,2:T(8,128)(2,1)S(1)} collective-permute-done((bf16[2,2,2,24,1536]{4,3,1,0,2:T(8,128)(2,1)S(1)}, bf16[2,2,2,24,1536]{4,3,1,0,2:T(8,128)(2,1)S(1)}, u32[]{:S(2)}, u32[]{:S(2)}) %collective-permute-start.6) | collective-permute-done | bytes 589856 | tf_op jit(solution)/shard_map/ppermute | solution.py:198
  64.9 3.2 collective-permute-done.3
  82.2 5.1 %fusion = bf16[1248,2304]{1,0:T(8,128)(2,1)S(1)} fusion(f32[2304]{0:T(1024)S(1)} %fusion.44, bf16[768,768]{1,0:T(8,128)(2,1)S(1)} %slice.179, bf16[768,1536]{1,0:T(8,128)(2,1)S(1)} %bitcast.287, f32[1248,768]{1,0:T(8,128)S(1)} %copy-done.15, f32[768]{0:T(1024)S(1)} %get-tuple-element.88, f32[768]{0:T(1024)S(1)} %get-tuple-element.89), kind=kOutput, calls=%fused_computation.4 | convolution fusion | flops 4432306176 | bytes 13138944 | tf_op jit(solution)/shard_map/dot_general | solution.py:22
  87.4 7.8 %shard_map.255 = bf16[6,208,768]{2,1,0:T(8,128)(2,1)S(1)} custom-call(bf16[6,208,2304]{2,1,0:T(8,128)(2,1)S(1)} %bitcast.247), custom_call_target="tpu_custom_call" | custom-call | tf_op jit(solution)/shard_map/pallas_call | solution.py:94
  99.6 3.9 %all-gather.2.cloned.1.call-done.weight_ref = bf16[768,6144]{1,0:T(8,128)(2,1)} async-done(((bf16[24,6144]{1,0:T(8,128)(2,1)}), bf16[768,6144]{1,0:T(8,128)(2,1)}) %all-gather.2.cloned.1.call-update) | async-done | bytes 9437200 | tf_op jit(solution)/shard_map/all_gather | solution.py:382
  106.8 22.0 %shard_map.257 = (bf16[1248,3072]{1,0:T(8,128)(2,1)S(1)}, bf16[1248,3072]{1,0:T(8,128)(2,1)}) custom-call(bf16[1248,768]{1,0:T(8,128)(2,1)S(1)} %add_convert_fusion.1.rows_ref, bf16[768,6144]{1,0:T(8,128)(2,1)} %all-gather.2.cloned.1.call-done.weight_ref, f32[1,3072]{1,0:T(1,128)S(1)} %slice.186.shift_ref), custom_call_target="tpu_custom_call" | custom-call | flops 5888802816 | bytes 23003136 | tf_op jit(solution)/shard_map/pallas_call | solution.py:158
  128.9 6.2 %fusion.4 = bf16[1248,768]{1,0:T(8,128)(2,1)S(1)} fusion(f32[1248,768]{1,0:T(8,128)S(1)} %copy-done.9, bf16[1248,3072]{1,0:T(8,128)(2,1)S(1)} %get-tuple-element.44, bf16[3072,768]{1,0:T(8,128)(2,1)S(1)} %bitcast.276, f32[768]{0:T(1024)S(1)} %get-tuple-element.84), kind=kOutput, calls=%fused_computation.14 | convolution fusion | flops 5891678208 | bytes 18140160 | tf_op jit(solution)/shard_map/dot_general | solution.py:22
  142.4 11.4 %convolution_convert_fusion = bf16[3072,768]{1,0:T(8,128)(2,1)} fusion(bf16[1248,3072]{1,0:T(8,128)(2,1)} %copy-done.4, bf16[1248,768]{1,0:T(8,128)(2,1)S(1)} %bitcast.264), kind=kOutput, calls=%fused_computation.6 | convolution fusion | flops 5891162112 | bytes 14303232 | tf_op jit(solution)/shard_map/dot_general | solution.py:22
  153.8 9.8 %multiply_convert_fusion = bf16[1248,3072]{1,0:T(8,128)(2,1)S(1)} fusion(bf16[1248,3072]{1,0:T(8,128)(2,1)} %get-tuple-element.46, bf16[1248,768]{1,0:T(8,128)(2,1)} %bitcast.265, bf16[3072,768]{1,0:T(8,128)(2,1)} %bitcast.277), kind=kOutput, calls=%fused_computation.1 | convolution fusion | flops 5900304384 | bytes 21970944 | tf_op jit(solution)/shard_map/dot_general | solution.py:22
  163.6 6.9 %convolution_convert_fusion.1 = bf16[768,3072]{1,0:T(8,128)(2,1)S(1)} fusion(bf16[1248,768]{1,0:T(8,128)(2,1)S(1)} %add_convert_fusion.1.rows_ref, bf16[1248,3072]{1,0:T(8,128)(2,1)S(1)} %multiply_convert_fusion), kind=kOutput, calls=%fused_computation.7 | convolution fusion | flops 5891162112 | bytes 14303232 | tf_op jit(solution)/shard_map/dot_general | solution.py:22
  174.1 8.1 %fusion.1 = f32[1248,768]{1,0:T(8,128)} fusion(bf16[1248,3072]{1,0:T(8,128)(2,1)S(1)} %multiply_convert_fusion, bf16[768,6144]{1,0:T(8,128)(2,1)S(1)} %bitcast.286), kind=kOutput, calls=%fused_computation.8 | convolution fusion | flops 5888802816 | bytes 16220160 | tf_op jit(solution)/shard_map/dot_general | solution.py:22
  190.2 3.8 %multiply_reduce_fusion = (f32[768]{0:T(1024)S(1)}, f32[1248]{0:T(1024)S(1)}, f32[1248]{0:T(1024)S(1)}, f32[768]{0:T(1024)S(1)}) fusion(f32[1248,768]{1,0:T(8,128)} %fusion.1, f32[1248,768]{1,0:T(8,128)S(1)} %copy-done.10, f32[1248]{0:T(1024)S(1)} %add_rsqrt_fusion, f32[1248]{0:T(1024)S(1)} %broadcast_multiply_fusion.4, f32[768]{0:T(1024)S(1)} %copy-done.52), kind=kLoop, calls=%fused_computation.18 | loop fusion | flops 8622144 | bytes 7696896 | tf_op jit(solution)/shard_map/reduce_sum | solution.py:186
  196.1 3.9 %convolution_convert_fusion.2 = bf16[1248,768]{1,0:T(8,128)(2,1)S(1)} fusion(bf16[768,1664]{1,0:T(8,128)(2,1)} %bitcast.269, f32[1248,768]{1,0:T(8,128)S(1)} %get-tuple-element.91), kind=kOutput, calls=%fused_computation.35 | convolution fusion | flops 1474117632 | bytes 6930432 | tf_op jit(solution)/shard_map/dot_general | solution.py:22
  208.0 9.2 %shard_map.258.refs_0_ = bf16[6,208,2304]{2,1,0:T(8,128)(2,1)S(1)} custom-call(bf16[6,208,2304]{2,1,0:T(8,128)(2,1)S(1)} %bitcast.248, bf16[6,208,768]{2,1,0:T(8,128)(2,1)S(1)} %bitcast.251), custom_call_target="tpu_custom_call" | custom-call | flops 2658140160 | bytes 13418496 | tf_op jit(solution)/shard_map/pallas_call | solution.py:114
  219.0 6.9 %collective-permute-done.10 = bf16[2,2,2,24,1536]{4,3,2,1,0:T(8,128)(2,1)} collective-permute-done((bf16[2,2,2,24,1536]{4,3,2,1,0:T(8,128)(2,1)S(1)}, bf16[2,2,2,24,1536]{4,3,2,1,0:T(8,128)(2,1)}, u32[]{:S(2)}, u32[]{:S(2)}) %collective-permute-start.10) | collective-permute-done | bytes 589856 | tf_op jit(solution)/shard_map/ppermute | solution.py:198
  229.4 9.2 %shard_map.259.refs_0_ = bf16[6,208,2304]{2,1,0:T(8,128)(2,1)S(1)} custom-call(bf16[6,208,2304]{2,1,0:T(8,128)(2,1)S(1)} %bitcast.249, bf16[6,208,768]{2,1,0:T(8,128)(2,1)S(1)} %bitcast.252, bf16[6,208,2304]{2,1,0:T(8,128)(2,1)S(1)} %shard_map.258.refs_0_), custom_call_target="tpu_custom_call", output_to_operand_aliasing={{}: (2, {})} | custom-call | flops 2658140160 | bytes 13418496 | tf_op jit(solution)/shard_map/pallas_call | solution.py:114
  241.1 9.6 %shard_map.260 = bf16[6,208,2304]{2,1,0:T(8,128)(2,1)S(1)} custom-call(bf16[6,208,2304]{2,1,0:T(8,128)(2,1)S(1)} %bitcast.250, bf16[6,208,768]{2,1,0:T(8,128)(2,1)S(1)} %bitcast.253, bf16[6,208,2304]{2,1,0:T(8,128)(2,1)S(1)} %shard_map.259.refs_0_), custom_call_target="tpu_custom_call", output_to_operand_aliasing={{}: (2, {})} | custom-call | flops 2658140160 | bytes 13418496 | tf_op jit(solution)/shard_map/pallas_call | solution.py:114
  250.8 5.4 %bitcast_convert_fusion = bf16[768,2304]{1,0:T(8,128)(2,1)S(1)} fusion(bf16[6,208,2304]{2,1,0:T(8,128)(2,1)S(1)} %shard_map.260, f32[768]{0:T(1024)S(1)} %copy-done.61, f32[768]{0:T(1024)S(1)} %copy-done.54, f32[6,208]{1,0:T(8,128)S(1)} %copy-done.59, f32[6,208]{1,0:T(8,128)S(1)} %copy-done.45, bf16[6,197,768]{2,1,0:T(8,128)(2,1)S(1)} %copy-done.6), kind=kOutput, calls=%fused_computation.5 | convolution fusion | flops 4424122368 | bytes 11121408 | tf_op jit(solution)/shard_map/dot_general | solution.py:22
  262.5 6.5 %fusion.10 = f32[1248,768]{1,0:T(8,128)} fusion(bf16[1248,2304]{1,0:T(8,128)(2,1)S(1)} %bitcast.246, bf16[768,768]{1,0:T(8,128)(2,1)S(1)} %copy-done.34, bf16[768,1536]{1,0:T(8,128)(2,1)S(1)} %bitcast.288), kind=kOutput, calls=%fused_computation.47 | convolution fusion | flops 4423680000 | bytes 13123584 | tf_op jit(solution)/shard_map/dot_general | solution.py:22
  273.2 4.9 %collective-permute-done.17 = bf16[24,1536]{1,0:T(8,128)(2,1)S(1)} collective-permute-done((bf16[24,1536]{1,0:T(8,128)(2,1)S(1)}, bf16[24,1536]{1,0:T(8,128)(2,1)S(1)}, u32[]{:S(2)}, u32[]{:S(2)}) %collective-permute-start.17) | collective-permute-done | bytes 73760 | tf_op jit(solution)/shard_map/ppermute | solution.py:198
  279.1 5.0 %multiply_reduce_fusion.1 = (f32[768]{0:T(1024)S(1)}, f32[768]{0:T(1024)S(1)}, f32[1248]{0:T(1024)}, f32[1248]{0:T(1024)}) fusion(f32[1248,768]{1,0:T(8,128)} %fusion.10, f32[1248]{0:T(1024)S(1)} %copy-done.42, f32[1248]{0:T(1024)S(1)} %copy-done.40, bf16[6,197,768]{2,1,0:T(8,128)(2,1)S(1)} %copy-done.7, f32[1248,768]{1,0:T(8,128)} %fusion.5, ...), kind=kLoop, calls=%fused_computation.20 | loop fusion | flops 9580608 | bytes 9512448 | tf_op jit(solution)/shard_map/reduce_sum | solution.py:186
  291.0 4.0 %multiply_add_fusion = f32[1248,768]{1,0:T(8,128)S(1)} fusion(f32[1248,768]{1,0:T(8,128)} %copy-done.12, f32[1248,768]{1,0:T(8,128)} %fusion.10, f32[1248]{0:T(1024)S(1)} %get-tuple-element.140, f32[1248]{0:T(1024)S(1)} %get-tuple-element.141, f32[768]{0:T(1024)S(1)} %copy-done.55, f32[1248]{0:T(1024)S(1)} %copy-done.43, f32[1248]{0:T(1024)S(1)} %copy-done.40, ...), kind=kLoop, calls=%fused_computation.21 | loop fusion | flops 8626176 | bytes 13340160 | tf_op jit(solution)/shard_map/add | solution.py:437
  305.0 7.3 %collective-permute-done.20 = bf16[2,2,24,1536]{3,2,1,0:T(8,128)(2,1)S(1)} collective-permute-done((bf16[2,2,24,1536]{3,2,1,0:T(8,128)(2,1)S(1)}, bf16[2,2,24,1536]{3,2,1,0:T(8,128)(2,1)S(1)}, u32[]{:S(2)}, u32[]{:S(2)}) %collective-permute-start.20) | collective-permute-done | bytes 294944 | tf_op jit(solution)/shard_map/ppermute | solution.py:198
  314.0 8.3 %collective-permute-done.24 = bf16[2,2,2,24,1664]{4,3,0,1,2:T(8,128)(2,1)S(1)} collective-permute-done((bf16[2,2,2,24,1664]{4,3,0,1,2:T(8,128)(2,1)S(1)}, bf16[2,2,2,24,1664]{4,3,0,1,2:T(8,128)(2,1)S(1)}, u32[]{:S(2)}, u32[]{:S(2)}) %collective-permute-start.24) | collective-permute-done | bytes 639008 | tf_op jit(solution)/shard_map/ppermute | solution.py:198
  323.2 6.3 %collective-permute-done.25 = bf16[2,2,24,1664]{3,2,0,1:T(8,128)(2,1)S(1)} collective-permute-done((bf16[2,2,24,1664]{3,2,0,1:T(8,128)(2,1)S(1)}, bf16[2,2,24,1664]{3,2,0,1:T(8,128)(2,1)S(1)}, u32[]{:S(2)}, u32[]{:S(2)}) %collective-permute-start.25) | collective-permute-done | bytes 319520 | tf_op jit(solution)/shard_map/ppermute | solution.py:198
  331.3 4.4 %collective-permute-start.22 = (bf16[24,1536]{1,0:T(8,128)(2,1)S(1)}, bf16[24,1536]{1,0:T(8,128)(2,1)S(1)}, u32[]{:S(2)}, u32[]{:S(2)}) collective-permute-start(bf16[24,1536]{1,0:T(8,128)(2,1)S(1)} %dynamic-slice_bitcast_fusion.20), channel_id=1, source_target_pairs={{0,16},{4,20},{8,24},{12,28},{16,0},{20,4},{24,8},{28,12},{1,17},{... | collective-permute-start | bytes 221192 | tf_op jit(solution)/shard_map/ppermute | solution.py:198
  335.8 4.2 %collective-permute-start.27 = (bf16[24,1664]{1,0:T(8,128)(2,1)S(1)}, bf16[24,1664]{1,0:T(8,128)(2,1)S(1)}, u32[]{:S(2)}, u32[]{:S(2)}) collective-permute-start(bf16[24,1664]{1,0:T(8,128)(2,1)S(1)} %dynamic-slice_bitcast_fusion.19), channel_id=1, source_target_pairs={{0,16},{4,20},{8,24},{12,28},{16,0},{20,4},{24,8},{28,12},{1,17},{... | collective-permute-start | bytes 239624 | tf_op jit(solution)/shard_map/ppermute | solution.py:198
  (305 shorter events, 108.9 us)
Async XLA Ops:
  7.2 96.3 %all-gather.2.cloned.1.call-start = ((), (), s32[]{:S(2)}) async-start(), calls=%async_computation.1 | async-start | bytes 9732096 | tf_op jit(solution)/shard_map/all_gather | solution.py:382
  9.1 280.4 %reduce-scatter.2.cloned.1.call-start = ((), (), s32[]{:S(2)}) async-start(), calls=%async_computation.2 | async-start | bytes 4866048 | tf_op jit(solution)/shard_map/reduce_scatter | solution.py:414
  11.0 11.4 %collective-permute-start = (bf16[24,3200]{1,0:T(8,128)(2,1)S(1)}, bf16[24,3200]{1,0:T(8,128)(2,1)S(1)}, u32[]{:S(2)}, u32[]{:S(2)}) collective-permute-start(bf16[24,3200]{1,0:T(8,128)(2,1)S(1)} %fusion.34), channel_id=1, source_target_pairs={{0,16},{4,20},{8,24},{12,28},{16,0},{20,4},{24,8},{28,12},{1,17},{... | collective-permute-start | bytes 460808 | tf_op jit(solution)/shard_map/ppermute | solution.py:198
  22.5 13.8 %collective-permute-start.1 = (bf16[2,24,3200]{2,1,0:T(8,128)(2,1)S(1)}, bf16[2,24,3200]{2,1,0:T(8,128)(2,1)S(1)}, u32[]{:S(2)}, u32[]{:S(2)}) collective-permute-start(bf16[2,24,3200]{2,1,0:T(8,128)(2,1)S(1)} %pad_maximum_fusion.11), channel_id=1, source_target_pairs={{0,8},{4,12},{8,0},{12,4},{16,24},{20,28},{24,16},{28,20},{1,9},{5... | collective-permute-start | bytes 921608 | tf_op jit(solution)/shard_map/ppermute | solution.py:198
  36.3 8.6 %collective-permute-start.5 = (bf16[2,2,24,1536]{3,2,1,0:T(8,128)(2,1)S(1)}, bf16[2,2,24,1536]{3,2,1,0:T(8,128)(2,1)S(1)}, u32[]{:S(2)}, u32[]{:S(2)}) collective-permute-start(bf16[2,2,24,1536]{3,2,1,0:T(8,128)(2,1)S(1)} %pad_maximum_fusion.12), channel_id=1, source_target_pairs={{0,4},{4,0},{8,12},{12,8},{16,20},{20,16},{24,28},{28,24},{1,5},{5... | collective-permute-start | bytes 884744 | tf_op jit(solution)/shard_map/ppermute | solution.py:198
  38.0 31.4 %copy-start.39 = (f32[1248]{0:T(1024)}, f32[1248]{0:T(1024)S(1)}, u32[]{:S(2)}) copy-start(f32[1248]{0:T(1024)S(1)} %div.31) | copy-start | bytes 14980
  38.1 31.3 %copy-start.41 = (f32[1248]{0:T(1024)}, f32[1248]{0:T(1024)S(1)}, u32[]{:S(2)}) copy-start(f32[1248]{0:T(1024)S(1)} %rsqrt.23) | copy-start | bytes 14980
  38.1 12.9 %collective-permute-start.2 = (bf16[2,2,24,1664]{3,2,1,0:T(8,128)(2,1)S(1)}, bf16[2,2,24,1664]{3,2,1,0:T(8,128)(2,1)S(1)}, u32[]{:S(2)}, u32[]{:S(2)}) collective-permute-start(bf16[2,2,24,1664]{3,2,1,0:T(8,128)(2,1)S(1)} %fusion.28), channel_id=1, source_target_pairs={{0,2},{1,3},{2,0},{3,1},{4,6},{5,7},{6,4},{7,5},{8,10},{9,11},{10,... | collective-permute-start | bytes 958472 | tf_op jit(solution)/shard_map/ppermute | solution.py:198
  45.1 18.4 %collective-permute-start.6 = (bf16[2,2,2,24,1536]{4,3,1,0,2:T(8,128)(2,1)S(1)}, bf16[2,2,2,24,1536]{4,3,1,0,2:T(8,128)(2,1)S(1)}, u32[]{:S(2)}, u32[]{:S(2)}) collective-permute-start(bf16[2,2,2,24,1536]{4,3,1,0,2:T(8,128)(2,1)S(1)} %pad_maximum_fusion.10), channel_id=1, source_target_pairs={{0,2},{1,3},{2,0},{3,1},{4,6},{5,7},{6,4},{7,5},{8,10},{9,11},{10,... | collective-permute-start | bytes 1769480 | tf_op jit(solution)/shard_map/ppermute | solution.py:198
  51.2 16.9 %collective-permute-start.3 = (bf16[2,2,2,24,1664]{4,3,2,1,0:T(8,128)(2,1)S(1)}, bf16[2,2,2,24,1664]{4,3,2,1,0:T(8,128)(2,1)S(1)}, u32[]{:S(2)}, u32[]{:S(2)}) collective-permute-start(bf16[2,2,2,24,1664]{4,3,2,1,0:T(8,128)(2,1)S(1)} %pad_maximum_fusion.9), channel_id=1, source_target_pairs={{0,4},{4,0},{8,12},{12,8},{16,20},{20,16},{24,28},{28,24},{1,5},{5... | collective-permute-start | bytes 1916936 | tf_op jit(solution)/shard_map/ppermute | solution.py:198
  64.9 8.6 %collective-permute-start.7 = (bf16[2,2,2,2,24,1536]{5,4,1,0,2,3:T(8,128)(2,1)}, bf16[2,2,2,2,24,1536]{5,4,1,0,2,3:T(8,128)(2,1)}, u32[]{:S(2)}, u32[]{:S(2)}) collective-permute-start(bf16[2,2,2,2,24,1536]{5,4,1,0,2,3:T(8,128)(2,1)} %pad_maximum_fusion.8), channel_id=1, source_target_pairs={{0,1},{1,0},{2,3},{3,2},{4,5},{5,4},{6,7},{7,6},{8,9},{9,8},{10,11... | collective-permute-start | bytes 3538952 | tf_op jit(solution)/shard_map/ppermute | solution.py:198
  69.4 6.9 %collective-permute-start.4 = (bf16[2,2,2,2,24,1664]{5,4,3,2,1,0:T(8,128)(2,1)}, bf16[2,2,2,2,24,1664]{5,4,3,2,1,0:T(8,128)(2,1)}, u32[]{:S(2)}, u32[]{:S(2)}) collective-permute-start(bf16[2,2,2,2,24,1664]{5,4,3,2,1,0:T(8,128)(2,1)} %pad_maximum_fusion.6), channel_id=1, source_target_pairs={{0,1},{1,0},{2,3},{3,2},{4,5},{5,4},{6,7},{7,6},{8,9},{9,8},{10,11... | collective-permute-start | bytes 3833864 | tf_op jit(solution)/shard_map/ppermute | solution.py:198
  173.5 15.1 %collective-permute-start.9 = (bf16[16,24,1536]{2,1,0:T(8,128)(2,1)S(1)}, bf16[16,24,1536]{2,1,0:T(8,128)(2,1)}, u32[]{:S(2)}, u32[]{:S(2)}) collective-permute-start(bf16[16,24,1536]{2,1,0:T(8,128)(2,1)S(1)} %dynamic-slice_bitcast_fusion.1), channel_id=1, source_target_pairs={{0,1},{1,0},{2,3},{3,2},{4,5},{5,4},{6,7},{7,6},{8,9},{9,8},{10,11... | collective-permute-start | bytes 3538952 | tf_op jit(solution)/shard_map/ppermute | solution.py:198
  173.8 11.6 %collective-permute-start.8 = (bf16[16,24,1536]{2,1,0:T(8,128)(2,1)}, bf16[16,24,1536]{2,1,0:T(8,128)(2,1)}, u32[]{:S(2)}, u32[]{:S(2)}) collective-permute-start(bf16[16,24,1536]{2,1,0:T(8,128)(2,1)} %dynamic-slice_bitcast_fusion.2), channel_id=1, source_target_pairs={{0,1},{1,0},{2,3},{3,2},{4,5},{5,4},{6,7},{7,6},{8,9},{9,8},{10,11... | collective-permute-start | bytes 3538952 | tf_op jit(solution)/shard_map/ppermute | solution.py:198
  203.4 22.5 %collective-permute-start.10 = (bf16[2,2,2,24,1536]{4,3,2,1,0:T(8,128)(2,1)S(1)}, bf16[2,2,2,24,1536]{4,3,2,1,0:T(8,128)(2,1)}, u32[]{:S(2)}, u32[]{:S(2)}) collective-permute-start(bf16[2,2,2,24,1536]{4,3,2,1,0:T(8,128)(2,1)S(1)} %dynamic-slice_bitcast_fusion.8), channel_id=1, source_target_pairs={{0,2},{1,3},{2,0},{3,1},{4,6},{5,7},{6,4},{7,5},{8,10},{9,11},{10,... | collective-permute-start | bytes 1769480 | tf_op jit(solution)/shard_map/ppermute | solution.py:198
  204.8 23.8 %collective-permute-start.11 = (bf16[2,2,2,24,1536]{4,3,0,1,2:T(8,128)(2,1)S(1)}, bf16[2,2,2,24,1536]{4,3,0,1,2:T(8,128)(2,1)S(1)}, u32[]{:S(2)}, u32[]{:S(2)}) collective-permute-start(bf16[2,2,2,24,1536]{4,3,0,1,2:T(8,128)(2,1)S(1)} %copy_bitcast_fusion.2), channel_id=1, source_target_pairs={{0,4},{4,0},{8,12},{12,8},{16,20},{20,16},{24,28},{28,24},{1,5},{5... | collective-permute-start | bytes 1769480 | tf_op jit(solution)/shard_map/ppermute | solution.py:198
  227.1 11.6 %collective-permute-start.12 = (bf16[2,2,24,1536]{3,2,1,0:T(8,128)(2,1)S(1)}, bf16[2,2,24,1536]{3,2,1,0:T(8,128)(2,1)S(1)}, u32[]{:S(2)}, u32[]{:S(2)}) collective-permute-start(bf16[2,2,24,1536]{3,2,1,0:T(8,128)(2,1)S(1)} %dynamic-slice_bitcast_fusion.12), channel_id=1, source_target_pairs={{0,4},{4,0},{8,12},{12,8},{16,20},{20,16},{24,28},{28,24},{1,5},{5... | collective-permute-start | bytes 884744 | tf_op jit(solution)/shard_map/ppermute | solution.py:198
  228.8 11.5 %collective-permute-start.13 = (bf16[2,2,24,1536]{3,2,0,1:T(8,128)(2,1)S(1)}, bf16[2,2,24,1536]{3,2,0,1:T(8,128)(2,1)S(1)}, u32[]{:S(2)}, u32[]{:S(2)}) collective-permute-start(bf16[2,2,24,1536]{3,2,0,1:T(8,128)(2,1)S(1)} %dynamic-slice_bitcast_fusion.11), channel_id=1, source_target_pairs={{0,2},{1,3},{2,0},{3,1},{4,6},{5,7},{6,4},{7,5},{8,10},{9,11},{10,... | collective-permute-start | bytes 884744 | tf_op jit(solution)/shard_map/ppermute | solution.py:198
  238.8 17.4 %collective-permute-start.14 = (bf16[2,24,1536]{2,1,0:T(8,128)(2,1)S(1)}, bf16[2,24,1536]{2,1,0:T(8,128)(2,1)S(1)}, u32[]{:S(2)}, u32[]{:S(2)}) collective-permute-start(bf16[2,24,1536]{2,1,0:T(8,128)(2,1)S(1)} %dynamic-slice_bitcast_fusion.16), channel_id=1, source_target_pairs={{0,8},{4,12},{8,0},{12,4},{16,24},{20,28},{24,16},{28,20},{1,9},{5... | collective-permute-start | bytes 442376 | tf_op jit(solution)/shard_map/ppermute | solution.py:198
  240.5 15.7 %collective-permute-start.15 = (bf16[2,24,1536]{2,1,0:T(8,128)(2,1)S(1)}, bf16[2,24,1536]{2,1,0:T(8,128)(2,1)S(1)}, u32[]{:S(2)}, u32[]{:S(2)}) collective-permute-start(bf16[2,24,1536]{2,1,0:T(8,128)(2,1)S(1)} %dynamic-slice_bitcast_fusion.15), channel_id=1, source_target_pairs={{0,8},{4,12},{8,0},{12,4},{16,24},{20,28},{24,16},{28,20},{1,9},{5... | collective-permute-start | bytes 442376 | tf_op jit(solution)/shard_map/ppermute | solution.py:198
  257.9 15.3 %collective-permute-start.16 = (bf16[24,1536]{1,0:T(8,128)(2,1)S(1)}, bf16[24,1536]{1,0:T(8,128)(2,1)S(1)}, u32[]{:S(2)}, u32[]{:S(2)}) collective-permute-start(bf16[24,1536]{1,0:T(8,128)(2,1)S(1)} %dynamic-slice_bitcast_fusion.22), channel_id=1, source_target_pairs={{0,16},{4,20},{8,24},{12,28},{16,0},{20,4},{24,8},{28,12},{1,17},{... | collective-permute-start | bytes 221192 | tf_op jit(solution)/shard_map/ppermute | solution.py:198
  260.5 24.8 %collective-permute-start.18 = (bf16[16,24,1536]{2,1,0:T(8,128)(2,1)S(1)}, bf16[16,24,1536]{2,1,0:T(8,128)(2,1)}, u32[]{:S(2)}, u32[]{:S(2)}) collective-permute-start(bf16[16,24,1536]{2,1,0:T(8,128)(2,1)S(1)} %dynamic-slice_bitcast_fusion), channel_id=1, source_target_pairs={{0,1},{1,0},{2,3},{3,2},{4,5},{5,4},{6,7},{7,6},{8,9},{9,8},{10,11... | collective-permute-start | bytes 3538952 | tf_op jit(solution)/shard_map/ppermute | solution.py:198
  271.8 6.3 %collective-permute-start.17 = (bf16[24,1536]{1,0:T(8,128)(2,1)S(1)}, bf16[24,1536]{1,0:T(8,128)(2,1)S(1)}, u32[]{:S(2)}, u32[]{:S(2)}) collective-permute-start(bf16[24,1536]{1,0:T(8,128)(2,1)S(1)} %dynamic-slice_bitcast_fusion.21), channel_id=1, source_target_pairs={{0,16},{4,20},{8,24},{12,28},{16,0},{20,4},{24,8},{28,12},{1,17},{... | collective-permute-start | bytes 221192 | tf_op jit(solution)/shard_map/ppermute | solution.py:198
  288.1 12.9 %collective-permute-start.19 = (bf16[2,2,2,24,1536]{4,3,2,1,0:T(8,128)(2,1)}, bf16[2,2,2,24,1536]{4,3,2,1,0:T(8,128)(2,1)}, u32[]{:S(2)}, u32[]{:S(2)}) collective-permute-start(bf16[2,2,2,24,1536]{4,3,2,1,0:T(8,128)(2,1)} %dynamic-slice_bitcast_fusion.7), channel_id=1, source_target_pairs={{0,2},{1,3},{2,0},{3,1},{4,6},{5,7},{6,4},{7,5},{8,10},{9,11},{10,... | collective-permute-start | bytes 1769480 | tf_op jit(solution)/shard_map/ppermute | solution.py:198
  290.9 12.0 %collective-permute-start.23 = (bf16[16,24,1664]{2,1,0:T(8,128)(2,1)S(1)}, bf16[16,24,1664]{2,1,0:T(8,128)(2,1)S(1)}, u32[]{:S(2)}, u32[]{:S(2)}) collective-permute-start(bf16[16,24,1664]{2,1,0:T(8,128)(2,1)S(1)} %pad_maximum_fusion.7), channel_id=1, source_target_pairs={{0,1},{1,0},{2,3},{3,2},{4,5},{5,4},{6,7},{7,6},{8,9},{9,8},{10,11... | collective-permute-start | bytes 3833864 | tf_op jit(solution)/shard_map/ppermute | solution.py:198
  302.3 10.0 %collective-permute-start.20 = (bf16[2,2,24,1536]{3,2,1,0:T(8,128)(2,1)S(1)}, bf16[2,2,24,1536]{3,2,1,0:T(8,128)(2,1)S(1)}, u32[]{:S(2)}, u32[]{:S(2)}) collective-permute-start(bf16[2,2,24,1536]{3,2,1,0:T(8,128)(2,1)S(1)} %dynamic-slice_bitcast_fusion.10), channel_id=1, source_target_pairs={{0,4},{4,0},{8,12},{12,8},{16,20},{20,16},{24,28},{28,24},{1,5},{5... | collective-permute-start | bytes 884744 | tf_op jit(solution)/shard_map/ppermute | solution.py:198
  303.4 18.8 %collective-permute-start.24 = (bf16[2,2,2,24,1664]{4,3,0,1,2:T(8,128)(2,1)S(1)}, bf16[2,2,2,24,1664]{4,3,0,1,2:T(8,128)(2,1)S(1)}, u32[]{:S(2)}, u32[]{:S(2)}) collective-permute-start(bf16[2,2,2,24,1664]{4,3,0,1,2:T(8,128)(2,1)S(1)} %bitcast.292), channel_id=1, source_target_pairs={{0,4},{4,0},{8,12},{12,8},{16,20},{20,16},{24,28},{28,24},{1,5},{5... | collective-permute-start | bytes 1916936 | tf_op jit(solution)/shard_map/ppermute | solution.py:198
  312.4 10.7 %collective-permute-start.21 = (bf16[2,24,1536]{2,1,0:T(8,128)(2,1)S(1)}, bf16[2,24,1536]{2,1,0:T(8,128)(2,1)S(1)}, u32[]{:S(2)}, u32[]{:S(2)}) collective-permute-start(bf16[2,24,1536]{2,1,0:T(8,128)(2,1)S(1)} %dynamic-slice_bitcast_fusion.14), channel_id=1, source_target_pairs={{0,8},{4,12},{8,0},{12,4},{16,24},{20,28},{24,16},{28,20},{1,9},{5... | collective-permute-start | bytes 442376 | tf_op jit(solution)/shard_map/ppermute | solution.py:198
  322.5 7.1 %collective-permute-start.25 = (bf16[2,2,24,1664]{3,2,0,1:T(8,128)(2,1)S(1)}, bf16[2,2,24,1664]{3,2,0,1:T(8,128)(2,1)S(1)}, u32[]{:S(2)}, u32[]{:S(2)}) collective-permute-start(bf16[2,2,24,1664]{3,2,0,1:T(8,128)(2,1)S(1)} %dynamic-slice_bitcast_fusion.9), channel_id=1, source_target_pairs={{0,2},{1,3},{2,0},{3,1},{4,6},{5,7},{6,4},{7,5},{8,10},{9,11},{10,... | collective-permute-start | bytes 958472 | tf_op jit(solution)/shard_map/ppermute | solution.py:198
  329.6 6.0 %collective-permute-start.26 = (bf16[2,24,1664]{2,1,0:T(8,128)(2,1)S(1)}, bf16[2,24,1664]{2,1,0:T(8,128)(2,1)S(1)}, u32[]{:S(2)}, u32[]{:S(2)}) collective-permute-start(bf16[2,24,1664]{2,1,0:T(8,128)(2,1)S(1)} %dynamic-slice_bitcast_fusion.13), channel_id=1, source_target_pairs={{0,8},{4,12},{8,0},{12,4},{16,24},{20,28},{24,16},{28,20},{1,9},{5... | collective-permute-start | bytes 479240 | tf_op jit(solution)/shard_map/ppermute | solution.py:198
  331.3 8.6 %collective-permute-start.22 = (bf16[24,1536]{1,0:T(8,128)(2,1)S(1)}, bf16[24,1536]{1,0:T(8,128)(2,1)S(1)}, u32[]{:S(2)}, u32[]{:S(2)}) collective-permute-start(bf16[24,1536]{1,0:T(8,128)(2,1)S(1)} %dynamic-slice_bitcast_fusion.20), channel_id=1, source_target_pairs={{0,16},{4,20},{8,24},{12,28},{16,0},{20,4},{24,8},{28,12},{1,17},{... | collective-permute-start | bytes 221192 | tf_op jit(solution)/shard_map/ppermute | solution.py:198
  335.8 6.6 %collective-permute-start.27 = (bf16[24,1664]{1,0:T(8,128)(2,1)S(1)}, bf16[24,1664]{1,0:T(8,128)(2,1)S(1)}, u32[]{:S(2)}, u32[]{:S(2)}) collective-permute-start(bf16[24,1664]{1,0:T(8,128)(2,1)S(1)} %dynamic-slice_bitcast_fusion.19), channel_id=1, source_target_pairs={{0,16},{4,20},{8,24},{12,28},{16,0},{20,4},{24,8},{28,12},{1,17},{... | collective-permute-start | bytes 239624 | tf_op jit(solution)/shard_map/ppermute | solution.py:198
  (64 other events, 476.2 us)
Sparse Core Ops, SparseCore 0:
  11.5 91.9 all-gather.1
  153.9 115.8 reduce-scatter.1
